TPU v7x, 128 devices: a whole 4x4x4 slice. The times are simulated.
128 devices in a mesh: slab: 32 (over x, z, core), pencil: 4 (over y).
Axes of the slice: x: 4, y: 4, z: 4, core: 2. Of those that a mesh axis runs over, the one named last changes fastest.
Arguments:
- basis: bfloat16 [88, 256, 128, 128], P(None, 'slab', 'pencil'), may hold values from -6 to 6
- image: bfloat16 [88, 256, 128, 128], P(None, 'slab', 'pencil'), may hold values from -6.3 to 6.3
- material: int32 [256, 128, 128], P('slab', 'pencil'), may hold values from 0 to 3
- picked: int32 [32], replicated, may hold values from 0 to 87, as said below
Outputs:
- recycle_out: float32 [32, 256, 128, 128], P(None, 'slab', 'pencil')
- images_out: float32 [32, 256, 128, 128], P(None, 'slab', 'pencil')
Inputs may be any that keep to these rules, and one draw needn't show every extreme that they name: `picked`: 32 distinct column numbers.
All inputs are finite; a program needn't handle non-finite values.
Results may differ from a plain program's by a relative error of at most 0.0061.
Values may be sent and summed in bfloat16 or wider, within the bound.
No kernel may reach another device: no remote copies, remote signals or barrier semaphores. Data moves between devices by JAX's collectives and lax.ppermute only.
A program may use at most 128 MiB of HBM per device.

v0:
```python
import jax
import jax.numpy as jnp
from jax import lax
from jax.experimental import pallas as pl
from jax.experimental.pallas import tpu as pltpu
from jax.sharding import PartitionSpec as P

F32 = jnp.float32
BF16 = jnp.bfloat16
CELLS = 4194304.0
PITCH = 44
NT = (((1,), (1,)), ((), ()))
TN = (((0,), (0,)), ((), ()))
MIB = 2**20


def gram_kernel(picked, image, basis, sums, turned, image_slab, basis_slab, rows, sems):
    columns, depth, height, width = image.shape
    count = picked.shape[0]
    total = columns + count
    slots = image_slab.shape[0]

    def copies(z, slot):
        return (
            pltpu.make_async_copy(image.at[:, z], image_slab.at[slot], sems.at[slot, 0]),
            pltpu.make_async_copy(basis.at[:, z], basis_slab.at[slot], sems.at[slot, 1]),
        )

    for z in range(slots - 1):
        for copy in copies(z, z):
            copy.start()
    sums[...] = jnp.zeros_like(sums)

    def step(z, _):
        slot = lax.rem(z, slots)

        @pl.when(z + slots - 1 < depth)
        def _():
            for copy in copies(z + slots - 1, lax.rem(z + slots - 1, slots)):
                copy.start()

        for copy in copies(z, slot):
            copy.wait()
        for c in range(columns):
            rows[c * PITCH : c * PITCH + height] = image_slab[slot, c].astype(F32)
        for c in range(count):
            at = (columns + c) * PITCH
            rows[at : at + height] = basis_slab[slot, picked[c]].astype(F32)
        for y in range(0, height, 16):
            turned[z, y : y + 16] = jnp.swapaxes(basis_slab[slot, :, y : y + 16, :], 0, 1)
        both = jnp.concatenate(
            [rows[pl.ds(y, total, stride=PITCH), :].astype(BF16) for y in range(height)], 1
        )
        part = lax.dot_general(both, both[:columns], NT, preferred_element_type=F32)
        sums[:, :columns] += part
        return 0

    lax.fori_loop(0, depth, step, 0)


def coefficient(material):
    squared = jnp.where(
        material == 0, 0.3, jnp.where(material == 1, 0.9, jnp.where(material == 2, 1.6, 2.5))
    ).astype(F32)
    return 6.0 - squared


def beside_in_row(row, first, last):
    width = row.shape[1]
    up = jnp.where(first, 0.0, pltpu.roll(row, 1, 1))
    down = jnp.where(last, 0.0, pltpu.roll(row, width - 1, 1))
    return up + down


def normal_kernel(
    sums, turned, material, z_low, z_high, y_low, y_high, packed, field, gram, sems
):
    depth, height, columns, width = turned.shape
    count = sums.shape[0] - columns
    copies = [
        pltpu.make_async_copy(turned.at[z], field.at[z + 1, 1 : height + 1], sems.at[z])
        for z in range(depth)
    ]
    for copy in copies:
        copy.start()
    for y in range(0, height, 16):
        field[0, y + 1 : y + 17] = jnp.swapaxes(z_low[:, y : y + 16, :], 0, 1)
        field[depth + 1, y + 1 : y + 17] = jnp.swapaxes(z_high[:, y : y + 16, :], 0, 1)
    low = jnp.swapaxes(y_low[...], 0, 1)
    high = jnp.swapaxes(y_high[...], 0, 1)
    for z in range(depth):
        field[z + 1, 0] = low[z]
        field[z + 1, height + 1] = high[z]
    gram[...] = jnp.zeros_like(gram)
    for copy in copies:
        copy.wait()
    lane = lax.broadcasted_iota(jnp.int32, (columns, width), 1)
    first, last = lane == 0, lane == width - 1

    def step(z, _):
        scale = coefficient(material[z])
        highs, lows = [], []
        for y in range(height):
            row = field[z + 1, y + 1].astype(F32)
            beside = field[z, y + 1].astype(F32) + field[z + 2, y + 1].astype(F32)
            beside = beside + (field[z + 1, y].astype(F32) + field[z + 1, y + 2].astype(F32))
            beside = beside + beside_in_row(row, first, last)
            image = scale[y : y + 1, :] * row - beside
            rounded = image.astype(BF16)
            highs.append(rounded)
            lows.append((image - rounded.astype(F32)).astype(BF16))
        rounded = jnp.concatenate(highs, 1)
        both = jnp.concatenate([rounded, jnp.concatenate(lows, 1)], 0)
        gram[...] += lax.dot_general(both, rounded, NT, preferred_element_type=F32)
        return 0

    lax.fori_loop(0, depth, step, 0)
    side = jnp.zeros((columns, 128 - columns), F32)
    foot = jnp.zeros((128 - columns, 128), F32)
    cross = jnp.concatenate([gram[columns:], side], 1)
    cross_t = jnp.concatenate([cross, foot], 0).T[:columns]
    normal = jnp.concatenate([gram[:columns], side], 1) + cross + cross_t
    col = lax.broadcasted_iota(jnp.int32, (columns, 128), 1)
    line = lax.broadcasted_iota(jnp.int32, (columns, 128), 0)
    diagonal = jnp.sum(jnp.where(line == col, normal, 0.0), axis=1, keepdims=True)
    grams = sums[:columns]
    picked_t = jnp.concatenate(
        [jnp.concatenate([sums[columns:], jnp.zeros((count, 128 - columns), F32)], 1),
         jnp.zeros((128 - count, 128), F32)], 0
    ).T[:columns]
    placed = pltpu.roll(picked_t, columns, 1)
    grams = jnp.concatenate([grams, side], 1)
    out = jnp.where(line >= col, grams, normal)
    out = jnp.where(col >= columns, placed, out)
    packed[...] = jnp.where(col == columns + count, diagonal, out)


def spread(row, lane):
    return jnp.broadcast_to(row[:, lane : lane + 1], row.shape)


def eliminate(blocks, panel, followers):
    base = 8 * panel
    wide = blocks[panel].shape
    rows = [jnp.broadcast_to(blocks[panel][i : i + 1, :], wide) for i in range(8)]
    heads = [[spread(rows[i], base + j) for j in range(8)] for i in range(8)]
    forward, pivots = [], []
    for k in range(8):
        forward.append(rows[k])
        pivots.append(heads[k][k])
        inverse = 1.0 / heads[k][k]
        rows[k] = rows[k] * inverse
        for j in range(k + 1, 8):
            heads[k][j] = heads[k][j] * inverse
        for i in range(8):
            if i == k:
                continue
            factor = heads[i][k]
            rows[i] = rows[i] - factor * rows[k]
            for j in range(k + 1, 8):
                heads[i][j] = heads[i][j] - factor * heads[k][j]
    for i in followers:
        block = blocks[i]
        for j in range(8):
            block = block - spread(blocks[i], base + j) * rows[j]
        blocks[i] = block
    return rows, forward, pivots


def stacked(rows):
    line = lax.broadcasted_iota(jnp.int32, rows[0].shape, 0)
    out = rows[0]
    for i in range(1, 8):
        out = jnp.where(line == i, rows[i], out)
    return out


def combination(packed, columns, count):
    exact = lax.Precision.HIGHEST
    shape = (128, 128)
    col = lax.broadcasted_iota(jnp.int32, shape, 1)
    line = lax.broadcasted_iota(jnp.int32, shape, 0)
    full = jnp.concatenate([packed, jnp.zeros((128 - columns, 128), F32)], 0)
    flipped = full.T
    grams = jnp.where(line >= col, full, flipped)
    grams = jnp.where(col >= columns, full, grams)
    diagonal = jnp.broadcast_to(full[:, columns + count : columns + count + 1], shape)
    normal = jnp.where(line < col, full, flipped)
    normal = jnp.where(line == col, diagonal, normal)
    normal = jnp.where((col < columns) & (line < columns), normal, 0.0)
    blocks = [grams[8 * i : 8 * i + 8] for i in range(columns // 8)]
    for panel in range(len(blocks)):
        rest = [i for i in range(len(blocks)) if i != panel]
        rows, _, _ = eliminate(blocks, panel, rest)
        blocks[panel] = stacked(rows)
    solved = jnp.concatenate(blocks + [jnp.zeros((128 - columns, 128), F32)], 0)
    solved = pltpu.roll(solved, 128 - columns, 1)
    chosen = jnp.where(col < count, solved, 0.0).astype(BF16).astype(F32)
    chosen_t = chosen.T
    product = jnp.dot(normal, chosen, precision=exact, preferred_element_type=F32)
    normal = jnp.dot(chosen_t, product, precision=exact, preferred_element_type=F32)
    normal = normal[:count] * (1.0 / CELLS)
    joined = jnp.where(col[:count] < count, normal, pltpu.roll(chosen_t[:count], count, 1))
    blocks = [joined[8 * i : 8 * i + 8] for i in range(count // 8)]
    for panel in range(len(blocks)):
        rest = range(panel + 1, len(blocks))
        _, forward, pivots = eliminate(blocks, panel, rest)
        blocks[panel] = stacked([r * lax.rsqrt(d) for r, d in zip(forward, pivots)])
    return pltpu.roll(jnp.concatenate(blocks, 0), 128 - count, 1)[:, :columns]


def update_kernel(
    packed, turned, material, z_low, z_high, y_low, y_high, recycle, images,
    field, planes, first_out, second_out, load_sems, store_sems,
):
    depth, height, columns, width = turned.shape
    count = recycle.shape[0]
    loads = [
        pltpu.make_async_copy(turned.at[z], field.at[z + 1], load_sems.at[z])
        for z in range(depth)
    ]
    for copy in loads:
        copy.start()
    for y in range(0, height, 16):
        field[0, y : y + 16] = jnp.swapaxes(z_low[:, y : y + 16, :], 0, 1)
        field[depth + 1, y : y + 16] = jnp.swapaxes(z_high[:, y : y + 16, :], 0, 1)
    weights = combination(packed[...], columns, count)
    rounded = weights.astype(BF16)
    both = jnp.concatenate([rounded, (weights - rounded.astype(F32)).astype(BF16)], 0)

    def combine(row):
        part = jnp.dot(both, row, preferred_element_type=F32)
        return part[:count] + part[count:]

    low = jnp.swapaxes(y_low[...], 0, 1)
    high = jnp.swapaxes(y_high[...], 0, 1)
    low = combine(jnp.concatenate([low[z] for z in range(depth)], 1))
    high = combine(jnp.concatenate([high[z] for z in range(depth)], 1))
    for z in range(depth):
        planes[z + 1, 0] = low[:, z * width : (z + 1) * width]
        planes[z + 1, height + 1] = high[:, z * width : (z + 1) * width]
    for copy in loads:
        copy.wait()

    def fill(z):
        plane = combine(jnp.concatenate([field[z, y] for y in range(height)], 1))
        for y in range(height):
            planes[z, y + 1] = plane[:, y * width : (y + 1) * width]

    def stores(z, slot):
        return (
            pltpu.make_async_copy(first_out.at[slot], recycle.at[:, z], store_sems.at[slot, 0]),
            pltpu.make_async_copy(second_out.at[slot], images.at[:, z], store_sems.at[slot, 1]),
        )

    fill(0)
    fill(1)
    lane = lax.broadcasted_iota(jnp.int32, (count, width), 1)
    first, last = lane == 0, lane == width - 1

    def step(z, _):
        slot = lax.rem(z, 2)
        fill(z + 2)

        @pl.when(z >= 2)
        def _():
            for copy in stores(z - 2, slot):
                copy.wait()

        scale = coefficient(material[z])
        one = first_out.at[slot].reshape(count * height, width)
        two = second_out.at[slot].reshape(count * height, width)
        for y in range(height):
            row = planes[z + 1, y + 1]
            beside = planes[z, y + 1] + planes[z + 2, y + 1]
            beside = beside + (planes[z + 1, y] + planes[z + 1, y + 2])
            beside = beside + beside_in_row(row, first, last)
            one[pl.ds(y, count, stride=height), :] = row
            two[pl.ds(y, count, stride=height), :] = scale[y : y + 1, :] * row - beside
        for copy in stores(z, slot):
            copy.start()
        return 0

    lax.fori_loop(0, depth, step, 0)
    for z in (depth - 2, depth - 1):
        for copy in stores(z, z % 2):
            copy.wait()


def device_sum(value):
    def shifted(axis, perm):
        return lax.ppermute(value, axis, perm)

    slabs = range(32)
    value = value + shifted("slab", [(i, i ^ 1) for i in slabs])
    for stride in (8, 2, 0):
        if stride:
            def move(i, d):
                place = (i // stride) % 4
                return i + ((place + d) % 4 - place) * stride
            axis, perms = "slab", [[(i, move(i, d)) for i in slabs] for d in (1, 2, 3)]
        else:
            axis = "pencil"
            perms = [[(i, (i + d) % 4) for i in range(4)] for d in (1, 2, 3)]
        left, opposite, right = [shifted(axis, perm) for perm in perms]
        value = (value + opposite) + (left + right)
    return value


def whole(memory=pltpu.VMEM):
    return pl.BlockSpec(memory_space=memory)


def local(basis, image, material, picked):
    columns, depth, height, width = basis.shape
    count = picked.shape[0]
    slabs, pencils = lax.axis_size("slab"), lax.axis_size("pencil")

    def neighbours(low_face, high_face, axis, size):
        up = [(i, i + 1) for i in range(size - 1)]
        down = [(j, i) for i, j in up]
        return lax.ppermute(high_face, axis, up), lax.ppermute(low_face, axis, down)

    z_low, z_high = neighbours(basis[:, 0], basis[:, depth - 1], "slab", slabs)
    y_low, y_high = neighbours(basis[:, :, 0], basis[:, :, height - 1], "pencil", pencils)

    sums, turned = pl.pallas_call(
        gram_kernel,
        in_specs=[whole(pltpu.SMEM), whole(pl.ANY), whole(pl.ANY)],
        out_specs=[whole(), whole()],
        out_shape=[
            jax.ShapeDtypeStruct((columns + count, columns), F32),
            jax.ShapeDtypeStruct((depth, height, columns, width), BF16),
        ],
        scratch_shapes=[
            pltpu.VMEM((3, columns, height, width), BF16),
            pltpu.VMEM((3, columns, height, width), BF16),
            pltpu.VMEM(((columns + count) * PITCH, width), F32),
            pltpu.SemaphoreType.DMA((3, 2)),
        ],
        compiler_params=pltpu.CompilerParams(vmem_limit_bytes=24 * MIB),
        cost_estimate=pl.CostEstimate(flops=2 * 10**9, bytes_accessed=17 * 10**6, transcendentals=0),
        name="gram",
    )(picked, image, basis)
    faces = (z_low, z_high, y_low, y_high)
    packed = pl.pallas_call(
        normal_kernel,
        in_specs=[whole(), whole(pl.ANY), whole(), whole(), whole(), whole(), whole()],
        out_specs=whole(),
        out_shape=jax.ShapeDtypeStruct((columns, 128), F32),
        scratch_shapes=[
            pltpu.VMEM((depth + 2, height + 2, columns, width), BF16),
            pltpu.VMEM((2 * columns, columns), F32),
            pltpu.SemaphoreType.DMA((depth,)),
        ],
        compiler_params=pltpu.CompilerParams(vmem_limit_bytes=24 * MIB),
        name="normal",
    )(sums, turned, material, *faces)
    packed = device_sum(packed)
    grid_shape = (count, depth, height, width)
    return pl.pallas_call(
        update_kernel,
        in_specs=[whole(), whole(pl.ANY), whole(), whole(), whole(), whole(), whole()],
        out_specs=[whole(pl.ANY), whole(pl.ANY)],
        out_shape=[jax.ShapeDtypeStruct(grid_shape, F32)] * 2,
        scratch_shapes=[
            pltpu.VMEM((depth + 2, height, columns, width), BF16),
            pltpu.VMEM((depth + 2, height + 2, count, width), F32),
            pltpu.VMEM((2, count, height, width), F32),
            pltpu.VMEM((2, count, height, width), F32),
            pltpu.SemaphoreType.DMA((depth,)),
            pltpu.SemaphoreType.DMA((2, 2)),
        ],
        compiler_params=pltpu.CompilerParams(vmem_limit_bytes=32 * MIB),
        name="update",
    )(packed, turned, material, *faces)


def solution(mesh):
    field = P(None, "slab", "pencil", None)
    return jax.shard_map(
        local,
        mesh=mesh,
        in_specs=(field, field, P("slab", "pencil", None), P()),
        out_specs=(field, field),
        check_vma=False,
    )
```

profile of v0, /device:TPU:0, one launch (start us, length us, event | category | flops | bytes accessed | tf_op | source)
XLA Modules:
  0.0 92.3 jit_solution(10665996113902870709)
XLA Ops:
  0.6 1.6 %slice_bitcast_fusion = (bf16[88,32,128]{2,1,0:T(8,128)(2,1)S(1)}, bf16[88,32,128]{2,1,0:T(8,128)(2,1)S(1)}) fusion(bf16[88,8,32,128]{3,2,1,0:T(8,128)(2,1)} %basis.1), kind=kLoop, calls=%fused_computation | loop fusion | bytes 2883584 | tf_op jit(solution)/shard_map/squeeze | solution.py:324
  2.2 1.3 %collective-permute-start.1 = (bf16[88,32,128]{2,1,0:T(8,128)(2,1)S(1)}, bf16[88,32,128]{2,1,0:T(8,128)(2,1)S(1)}, u32[]{:S(2)}, u32[]{:S(2)}) collective-permute-start(bf16[88,32,128]{2,1,0:T(8,128)(2,1)S(1)} %get-tuple-element.8), channel_id=1, source_target_pairs={{4,0},{8,4},{12,8},{16,12},{20,16},{24,20},{28,24},{32,28},{36,32}... | collective-permute-start | bytes 2162696 | tf_op jit(solution)/shard_map/ppermute | solution.py:322
  3.5 3.1 %collective-permute-start = (bf16[88,32,128]{2,1,0:T(8,128)(2,1)S(1)}, bf16[88,32,128]{2,1,0:T(8,128)(2,1)S(1)}, u32[]{:S(2)}, u32[]{:S(2)}) collective-permute-start(bf16[88,32,128]{2,1,0:T(8,128)(2,1)S(1)} %get-tuple-element.9), channel_id=1, source_target_pairs={{0,4},{4,8},{8,12},{12,16},{16,20},{20,24},{24,28},{28,32},{32,36}... | collective-permute-start | bytes 2162696 | tf_op jit(solution)/shard_map/ppermute | solution.py:322
  6.6 2.5 %fusion = (bf16[88,8,1,128]{3,2,1,0:T(2,128)(2,1)S(1)}, bf16[88,8,1,128]{3,2,1,0:T(2,128)(2,1)S(1)}) fusion(bf16[88,8,32,128]{3,2,1,0:T(8,128)(2,1)} %basis.1), kind=kLoop, calls=%fused_computation.7 | loop fusion | bytes 720896 | tf_op jit(solution)/shard_map/slice | solution.py:325
  9.1 3.6 %collective-permute-start.2 = (bf16[88,8,128]{2,1,0:T(8,128)(2,1)S(1)}, bf16[88,8,128]{2,1,0:T(8,128)(2,1)S(1)}, u32[]{:S(2)}, u32[]{:S(2)}) collective-permute-start(bf16[88,8,128]{2,1,0:T(8,128)(2,1)S(1)} %bitcast.14), channel_id=1, source_target_pairs={{0,1},{1,2},{2,3},{4,5},{5,6},{6,7},{8,9},{9,10},{10,11},{12,13},{... | collective-permute-start | bytes 540680 | tf_op jit(solution)/shard_map/ppermute | solution.py:322
  12.7 1.3 %collective-permute-start.3 = (bf16[88,8,128]{2,1,0:T(8,128)(2,1)S(1)}, bf16[88,8,128]{2,1,0:T(8,128)(2,1)S(1)}, u32[]{:S(2)}, u32[]{:S(2)}) collective-permute-start(bf16[88,8,128]{2,1,0:T(8,128)(2,1)S(1)} %bitcast.15), channel_id=1, source_target_pairs={{1,0},{2,1},{3,2},{5,4},{6,5},{7,6},{9,8},{10,9},{11,10},{13,12},{... | collective-permute-start | bytes 540680 | tf_op jit(solution)/shard_map/ppermute | solution.py:322
  14.0 0.0 copy-start
  14.0 2.6 %copy-done = bf16[88,8,32,128]{3,2,1,0:T(8,128)(2,1)S(1)} copy-done((bf16[88,8,32,128]{3,2,1,0:T(8,128)(2,1)S(1)}, bf16[88,8,32,128]{3,2,1,0:T(8,128)(2,1)}, u32[]{:S(2)}) %copy-start) | copy-done | bytes 5767192
  16.7 0.0 copy-start.1
  16.7 2.6 %copy-done.1 = bf16[88,8,32,128]{3,2,1,0:T(8,128)(2,1)S(1)} copy-done((bf16[88,8,32,128]{3,2,1,0:T(8,128)(2,1)S(1)}, bf16[88,8,32,128]{3,2,1,0:T(8,128)(2,1)}, u32[]{:S(2)}) %copy-start.1) | copy-done | bytes 5767192
  19.3 0.0 copy-start.3
  19.3 0.7 copy-done.3
  20.0 0.0 copy-start.2
  20.0 7.9 %gram.1 = (f32[120,88]{1,0:T(8,128)S(1)}, bf16[8,32,88,128]{3,2,1,0:T(8,128)(2,1)S(1)}) custom-call(s32[32]{0:T(128)S(1)} %copy-done.3, bf16[88,8,32,128]{3,2,1,0:T(8,128)(2,1)S(1)} %copy-done.1, bf16[88,8,32,128]{3,2,1,0:T(8,128)(2,1)S(1)} %copy-done), custom_call_target="tpu_custom_call" | custom-call | flops 2000000000 | bytes 17000000 | tf_op jit(solution)/shard_map/gram/pallas_call | solution.py:327
  27.9 0.0 collective-permute-done.2.y_low
  27.9 0.0 collective-permute-done.3.y_high
  27.9 0.0 collective-permute-done.1.z_high
  28.0 0.0 collective-permute-done.z_low
  28.0 0.0 copy-done.2
  28.0 12.8 %normal.1 = f32[88,128]{1,0:T(8,128)S(1)} custom-call(f32[120,88]{1,0:T(8,128)S(1)} %get-tuple-element.4.sums, bf16[8,32,88,128]{3,2,1,0:T(8,128)(2,1)S(1)} %get-tuple-element.5.turned, s32[8,32,128]{2,1,0:T(8,128)S(1)} %copy-done.2, bf16[88,32,128]{2,1,0:T(8,128)(2,1)S(1)} %collective-permute-done.z_low, ...), custom_call_target="tpu_custom_call" | custom-call | tf_op jit(solution)/shard_map/normal/pallas_call | solution.py:346
  40.8 1.3 %collective-permute-start.4 = (f32[88,128]{1,0:T(8,128)S(1)}, f32[88,128]{1,0:T(8,128)S(1)}, u32[]{:S(2)}, u32[]{:S(2)}) collective-permute-start(f32[88,128]{1,0:T(8,128)S(1)} %normal.1), channel_id=1, source_target_pairs={{0,4},{4,0},{8,12},{12,8},{16,20},{20,16},{24,28},{28,24},{32,36},... | collective-permute-start | bytes 135176 | tf_op jit(solution)/shard_map/ppermute | solution.py:292
  42.1 0.9 collective-permute-done.4
  43.0 5.2 %collective-permute-start.7 = (f32[88,128]{1,0:T(8,128)S(1)}, f32[88,128]{1,0:T(8,128)S(1)}, u32[]{:S(2)}, u32[]{:S(2)}) collective-permute-start(f32[88,128]{1,0:T(8,128)S(1)} %add.30), channel_id=1, source_target_pairs={{0,96},{4,100},{8,104},{12,108},{16,112},{20,116},{24,120},{28,124... | collective-permute-start | bytes 135176 | tf_op jit(solution)/shard_map/ppermute | solution.py:292
  48.1 0.0 collective-permute-start.6
  48.1 2.0 %collective-permute-start.5 = (f32[88,128]{1,0:T(8,128)S(1)}, f32[88,128]{1,0:T(8,128)S(1)}, u32[]{:S(2)}, u32[]{:S(2)}) collective-permute-start(f32[88,128]{1,0:T(8,128)S(1)} %add.30), channel_id=1, source_target_pairs={{0,64},{4,68},{8,72},{12,76},{16,80},{20,84},{24,88},{28,92},{32,9... | collective-permute-start | bytes 135176 | tf_op jit(solution)/shard_map/ppermute | solution.py:292
  50.1 0.0 collective-permute-done.7
  50.1 3.7 %collective-permute-done.6 = f32[88,128]{1,0:T(8,128)S(1)} collective-permute-done((f32[88,128]{1,0:T(8,128)S(1)}, f32[88,128]{1,0:T(8,128)S(1)}, u32[]{:S(2)}, u32[]{:S(2)}) %collective-permute-start.6) | collective-permute-done | bytes 45088 | tf_op jit(solution)/shard_map/ppermute | solution.py:292
  53.9 0.0 collective-permute-done.5
  53.9 2.6 %collective-permute-start.10 = (f32[88,128]{1,0:T(8,128)S(1)}, f32[88,128]{1,0:T(8,128)S(1)}, u32[]{:S(2)}, u32[]{:S(2)}) collective-permute-start(f32[88,128]{1,0:T(8,128)S(1)} %add_add_fusion.2), channel_id=1, source_target_pairs={{0,24},{4,28},{8,0},{12,4},{16,8},{20,12},{24,16},{28,20},{32,56},... | collective-permute-start | bytes 135176 | tf_op jit(solution)/shard_map/ppermute | solution.py:292
  56.5 0.0 collective-permute-start.9
  56.5 1.5 %collective-permute-start.8 = (f32[88,128]{1,0:T(8,128)S(1)}, f32[88,128]{1,0:T(8,128)S(1)}, u32[]{:S(2)}, u32[]{:S(2)}) collective-permute-start(f32[88,128]{1,0:T(8,128)S(1)} %add_add_fusion.2), channel_id=1, source_target_pairs={{0,16},{4,20},{8,24},{12,28},{16,0},{20,4},{24,8},{28,12},{32,48},... | collective-permute-start | bytes 135176 | tf_op jit(solution)/shard_map/ppermute | solution.py:292
  58.0 0.2 collective-permute-done.10
  58.2 4.0 %collective-permute-done.9 = f32[88,128]{1,0:T(8,128)S(1)} collective-permute-done((f32[88,128]{1,0:T(8,128)S(1)}, f32[88,128]{1,0:T(8,128)S(1)}, u32[]{:S(2)}, u32[]{:S(2)}) %collective-permute-start.9) | collective-permute-done | bytes 45088 | tf_op jit(solution)/shard_map/ppermute | solution.py:292
  62.2 0.0 collective-permute-done.8
  62.2 3.9 %collective-permute-start.13 = (f32[88,128]{1,0:T(8,128)S(1)}, f32[88,128]{1,0:T(8,128)S(1)}, u32[]{:S(2)}, u32[]{:S(2)}) collective-permute-start(f32[88,128]{1,0:T(8,128)S(1)} %add_add_fusion.1), channel_id=1, source_target_pairs={{0,3},{1,0},{2,1},{3,2},{4,7},{5,4},{6,5},{7,6},{8,11},{9,8},{10,9... | collective-permute-start | bytes 135176 | tf_op jit(solution)/shard_map/ppermute | solution.py:292
  66.1 0.0 collective-permute-start.12
  66.1 2.2 %collective-permute-start.11 = (f32[88,128]{1,0:T(8,128)S(1)}, f32[88,128]{1,0:T(8,128)S(1)}, u32[]{:S(2)}, u32[]{:S(2)}) collective-permute-start(f32[88,128]{1,0:T(8,128)S(1)} %add_add_fusion.1), channel_id=1, source_target_pairs={{0,2},{1,3},{2,0},{3,1},{4,6},{5,7},{6,4},{7,5},{8,10},{9,11},{10,... | collective-permute-start | bytes 135176 | tf_op jit(solution)/shard_map/ppermute | solution.py:292
  68.3 0.0 collective-permute-done.13
  68.3 3.5 %collective-permute-done.12 = f32[88,128]{1,0:T(8,128)S(1)} collective-permute-done((f32[88,128]{1,0:T(8,128)S(1)}, f32[88,128]{1,0:T(8,128)S(1)}, u32[]{:S(2)}, u32[]{:S(2)}) %collective-permute-start.12) | collective-permute-done | bytes 45088 | tf_op jit(solution)/shard_map/ppermute | solution.py:292
  71.8 0.0 collective-permute-done.11
  71.8 20.3 %update.1 = (f32[32,8,32,128]{3,2,1,0:T(8,128)}, f32[32,8,32,128]{3,2,1,0:T(8,128)}) custom-call(f32[88,128]{1,0:T(8,128)S(1)} %add_add_fusion.packed, bf16[8,32,88,128]{3,2,1,0:T(8,128)(2,1)S(1)} %get-tuple-element.5.turned, s32[8,32,128]{2,1,0:T(8,128)S(1)} %copy-done.2, bf16[88,32,128]{2,1,0:T(8,128)(2,1)S(1)} %collective-permute-done.z_low, ...), custom_call_target="tpu_custom_call" | custom-call | tf_op jit(solution)/shard_map/update/pallas_call | solution.py:361
  (6 shorter events, 0.1 us)
Async XLA Ops:
  2.2 25.7 %collective-permute-start.1 = (bf16[88,32,128]{2,1,0:T(8,128)(2,1)S(1)}, bf16[88,32,128]{2,1,0:T(8,128)(2,1)S(1)}, u32[]{:S(2)}, u32[]{:S(2)}) collective-permute-start(bf16[88,32,128]{2,1,0:T(8,128)(2,1)S(1)} %get-tuple-element.8), channel_id=1, source_target_pairs={{4,0},{8,4},{12,8},{16,12},{20,16},{24,20},{28,24},{32,28},{36,32}... | collective-permute-start | bytes 2162696 | tf_op jit(solution)/shard_map/ppermute | solution.py:322
  3.5 24.4 %collective-permute-start = (bf16[88,32,128]{2,1,0:T(8,128)(2,1)S(1)}, bf16[88,32,128]{2,1,0:T(8,128)(2,1)S(1)}, u32[]{:S(2)}, u32[]{:S(2)}) collective-permute-start(bf16[88,32,128]{2,1,0:T(8,128)(2,1)S(1)} %get-tuple-element.9), channel_id=1, source_target_pairs={{0,4},{4,8},{8,12},{12,16},{16,20},{20,24},{24,28},{28,32},{32,36}... | collective-permute-start | bytes 2162696 | tf_op jit(solution)/shard_map/ppermute | solution.py:322
  9.1 18.8 %collective-permute-start.2 = (bf16[88,8,128]{2,1,0:T(8,128)(2,1)S(1)}, bf16[88,8,128]{2,1,0:T(8,128)(2,1)S(1)}, u32[]{:S(2)}, u32[]{:S(2)}) collective-permute-start(bf16[88,8,128]{2,1,0:T(8,128)(2,1)S(1)} %bitcast.14), channel_id=1, source_target_pairs={{0,1},{1,2},{2,3},{4,5},{5,6},{6,7},{8,9},{9,10},{10,11},{12,13},{... | collective-permute-start | bytes 540680 | tf_op jit(solution)/shard_map/ppermute | solution.py:322
  12.7 15.2 %collective-permute-start.3 = (bf16[88,8,128]{2,1,0:T(8,128)(2,1)S(1)}, bf16[88,8,128]{2,1,0:T(8,128)(2,1)S(1)}, u32[]{:S(2)}, u32[]{:S(2)}) collective-permute-start(bf16[88,8,128]{2,1,0:T(8,128)(2,1)S(1)} %bitcast.15), channel_id=1, source_target_pairs={{1,0},{2,1},{3,2},{5,4},{6,5},{7,6},{9,8},{10,9},{11,10},{13,12},{... | collective-permute-start | bytes 540680 | tf_op jit(solution)/shard_map/ppermute | solution.py:322
  14.0 2.6 %copy-start = (bf16[88,8,32,128]{3,2,1,0:T(8,128)(2,1)S(1)}, bf16[88,8,32,128]{3,2,1,0:T(8,128)(2,1)}, u32[]{:S(2)}) copy-start(bf16[88,8,32,128]{3,2,1,0:T(8,128)(2,1)} %basis.1) | copy-start | bytes 17301508
  16.7 2.6 %copy-start.1 = (bf16[88,8,32,128]{3,2,1,0:T(8,128)(2,1)S(1)}, bf16[88,8,32,128]{3,2,1,0:T(8,128)(2,1)}, u32[]{:S(2)}) copy-start(bf16[88,8,32,128]{3,2,1,0:T(8,128)(2,1)} %image.1) | copy-start | bytes 17301508
  19.3 0.7 copy-start.3
  20.0 8.0 %copy-start.2 = (s32[8,32,128]{2,1,0:T(8,128)S(1)}, s32[8,32,128]{2,1,0:T(8,128)}, u32[]{:S(2)}) copy-start(s32[8,32,128]{2,1,0:T(8,128)} %material.3) | copy-start | bytes 393220
  40.8 2.2 %collective-permute-start.4 = (f32[88,128]{1,0:T(8,128)S(1)}, f32[88,128]{1,0:T(8,128)S(1)}, u32[]{:S(2)}, u32[]{:S(2)}) collective-permute-start(f32[88,128]{1,0:T(8,128)S(1)} %normal.1), channel_id=1, source_target_pairs={{0,4},{4,0},{8,12},{12,8},{16,20},{20,16},{24,28},{28,24},{32,36},... | collective-permute-start | bytes 135176 | tf_op jit(solution)/shard_map/ppermute | solution.py:292
  43.0 7.2 %collective-permute-start.7 = (f32[88,128]{1,0:T(8,128)S(1)}, f32[88,128]{1,0:T(8,128)S(1)}, u32[]{:S(2)}, u32[]{:S(2)}) collective-permute-start(f32[88,128]{1,0:T(8,128)S(1)} %add.30), channel_id=1, source_target_pairs={{0,96},{4,100},{8,104},{12,108},{16,112},{20,116},{24,120},{28,124... | collective-permute-start | bytes 135176 | tf_op jit(solution)/shard_map/ppermute | solution.py:292
  48.1 5.7 %collective-permute-start.6 = (f32[88,128]{1,0:T(8,128)S(1)}, f32[88,128]{1,0:T(8,128)S(1)}, u32[]{:S(2)}, u32[]{:S(2)}) collective-permute-start(f32[88,128]{1,0:T(8,128)S(1)} %add.30), channel_id=1, source_target_pairs={{0,32},{4,36},{8,40},{12,44},{16,48},{20,52},{24,56},{28,60},{32,6... | collective-permute-start | bytes 135176 | tf_op jit(solution)/shard_map/ppermute | solution.py:292
  48.1 5.7 %collective-permute-start.5 = (f32[88,128]{1,0:T(8,128)S(1)}, f32[88,128]{1,0:T(8,128)S(1)}, u32[]{:S(2)}, u32[]{:S(2)}) collective-permute-start(f32[88,128]{1,0:T(8,128)S(1)} %add.30), channel_id=1, source_target_pairs={{0,64},{4,68},{8,72},{12,76},{16,80},{20,84},{24,88},{28,92},{32,9... | collective-permute-start | bytes 135176 | tf_op jit(solution)/shard_map/ppermute | solution.py:292
  53.9 4.3 %collective-permute-start.10 = (f32[88,128]{1,0:T(8,128)S(1)}, f32[88,128]{1,0:T(8,128)S(1)}, u32[]{:S(2)}, u32[]{:S(2)}) collective-permute-start(f32[88,128]{1,0:T(8,128)S(1)} %add_add_fusion.2), channel_id=1, source_target_pairs={{0,24},{4,28},{8,0},{12,4},{16,8},{20,12},{24,16},{28,20},{32,56},... | collective-permute-start | bytes 135176 | tf_op jit(solution)/shard_map/ppermute | solution.py:292
  56.5 5.7 %collective-permute-start.9 = (f32[88,128]{1,0:T(8,128)S(1)}, f32[88,128]{1,0:T(8,128)S(1)}, u32[]{:S(2)}, u32[]{:S(2)}) collective-permute-start(f32[88,128]{1,0:T(8,128)S(1)} %add_add_fusion.2), channel_id=1, source_target_pairs={{0,8},{4,12},{8,16},{12,20},{16,24},{20,28},{24,0},{28,4},{32,40},... | collective-permute-start | bytes 135176 | tf_op jit(solution)/shard_map/ppermute | solution.py:292
  56.5 5.7 %collective-permute-start.8 = (f32[88,128]{1,0:T(8,128)S(1)}, f32[88,128]{1,0:T(8,128)S(1)}, u32[]{:S(2)}, u32[]{:S(2)}) collective-permute-start(f32[88,128]{1,0:T(8,128)S(1)} %add_add_fusion.2), channel_id=1, source_target_pairs={{0,16},{4,20},{8,24},{12,28},{16,0},{20,4},{24,8},{28,12},{32,48},... | collective-permute-start | bytes 135176 | tf_op jit(solution)/shard_map/ppermute | solution.py:292
  62.2 6.1 %collective-permute-start.13 = (f32[88,128]{1,0:T(8,128)S(1)}, f32[88,128]{1,0:T(8,128)S(1)}, u32[]{:S(2)}, u32[]{:S(2)}) collective-permute-start(f32[88,128]{1,0:T(8,128)S(1)} %add_add_fusion.1), channel_id=1, source_target_pairs={{0,3},{1,0},{2,1},{3,2},{4,7},{5,4},{6,5},{7,6},{8,11},{9,8},{10,9... | collective-permute-start | bytes 135176 | tf_op jit(solution)/shard_map/ppermute | solution.py:292
  66.1 5.7 %collective-permute-start.12 = (f32[88,128]{1,0:T(8,128)S(1)}, f32[88,128]{1,0:T(8,128)S(1)}, u32[]{:S(2)}, u32[]{:S(2)}) collective-permute-start(f32[88,128]{1,0:T(8,128)S(1)} %add_add_fusion.1), channel_id=1, source_target_pairs={{0,1},{1,2},{2,3},{3,0},{4,5},{5,6},{6,7},{7,4},{8,9},{9,10},{10,1... | collective-permute-start | bytes 135176 | tf_op jit(solution)/shard_map/ppermute | solution.py:292
  66.1 5.7 %collective-permute-start.11 = (f32[88,128]{1,0:T(8,128)S(1)}, f32[88,128]{1,0:T(8,128)S(1)}, u32[]{:S(2)}, u32[]{:S(2)}) collective-permute-start(f32[88,128]{1,0:T(8,128)S(1)} %add_add_fusion.1), channel_id=1, source_target_pairs={{0,2},{1,3},{2,0},{3,1},{4,6},{5,7},{6,4},{7,5},{8,10},{9,11},{10,... | collective-permute-start | bytes 135176 | tf_op jit(solution)/shard_map/ppermute | solution.py:292
where the time goes:
time: 92.6 us; the launch traced here: 92.3 us
  Pallas kernels  41.1 us (44%)
  starting transfers between devices  27.9 us (30%)
  waiting for transfers between devices  12.4 us (13%)
  local copies, waits for them, and re-layouts  10 us (11%)
  between operations  0.93 us (1%)
    pallas_call x1, Pallas kernels, local(): pl.pallas_call(update_kernel, in_specs=[whole(), whole(pl.ANY), whole(),...  20.3 us
    ppermute x10, starting transfers between devices, shifted(): return lax.ppermute(value, axis, perm)  18.6 us
    pallas_call x1, Pallas kernels, local(): pl.pallas_call(normal_kernel, in_specs=[whole(), whole(pl.ANY), whole(),...  12.8 us
    ppermute x10, waiting for transfers between devices, shifted(): return lax.ppermute(value, axis, perm)  12.4 us
    pallas_call x1, Pallas kernels, local(): pl.pallas_call(gram_kernel, in_specs=[whole(pltpu.SMEM), whole(pl.ANY), w...  7.95 us
    ppermute x2, starting transfers between devices, neighbours(): lax.ppermute(high_face, axis, up)  6.65 us
    unnamed x10, local copies, waits for them, and re-layouts  5.98 us
    ppermute x2, starting transfers between devices, neighbours(): lax.ppermute(low_face, axis, down)  2.58 us
  transfers between devices with their start and end apart: 14, of which 5 were waited for; matrix products, arithmetic and copies ran while one was open for 3% of the time, Pallas kernels for 9%

commit v1 on v0

--- a/solution.py
+++ b/solution.py
@@ -9,50 +9,82 @@
 BF16 = jnp.bfloat16
 CELLS = 4194304.0
 PITCH = 44
+STEP = 40
 NT = (((1,), (1,)), ((), ()))
 TN = (((0,), (0,)), ((), ()))
 MIB = 2**20
 
 
-def gram_kernel(picked, image, basis, sums, turned, image_slab, basis_slab, rows, sems):
+def turn_kernel(basis, turned, z_first, z_last, y_first, y_last, slab, sems):
+    columns, depth, height, width = basis.shape
+    slots = slab.shape[0]
+
+    def load(z, slot):
+        return pltpu.make_async_copy(basis.at[:, z], slab.at[slot], sems.at[slot])
+
+    for z in range(slots - 1):
+        load(z, z).start()
+
+    def step(z, _):
+        slot = lax.rem(z, slots)
+
+        @pl.when(z + slots - 1 < depth)
+        def _():
+            load(z + slots - 1, lax.rem(z + slots - 1, slots)).start()
+
+        load(z, slot).wait()
+        for y in range(0, height, 16):
+            part = jnp.swapaxes(slab[slot, :, y : y + 16, :], 0, 1)
+            turned[z, y : y + 16] = part
+            if y == 0:
+                y_first[z] = part[0]
+            if y + 16 == height:
+                y_last[z] = part[15]
+        return 0
+
+    lax.fori_loop(0, depth, step, 0)
+    z_first[...] = turned[0]
+    z_last[...] = turned[depth - 1]
+
+
+def gram_kernel(picked, image, basis, sums, image_slab, picked_slab, rows, sems, picked_sems):
     columns, depth, height, width = image.shape
     count = picked.shape[0]
     total = columns + count
     slots = image_slab.shape[0]
 
-    def copies(z, slot):
-        return (
-            pltpu.make_async_copy(image.at[:, z], image_slab.at[slot], sems.at[slot, 0]),
-            pltpu.make_async_copy(basis.at[:, z], basis_slab.at[slot], sems.at[slot, 1]),
-        )
-
-    for z in range(slots - 1):
-        for copy in copies(z, z):
-            copy.start()
+    def load(z, slot):
+        return pltpu.make_async_copy(image.at[:, z], image_slab.at[slot], sems.at[slot])
+
+    def load_picked(c):
+        return pltpu.make_async_copy(basis.at[picked[c]], picked_slab.at[c], picked_sems.at[c])
+
+    load(0, 0).start()
+    for c in range(count):
+        load_picked(c).start()
+    for z in range(1, slots - 1):
+        load(z, z).start()
     sums[...] = jnp.zeros_like(sums)
+    for c in range(count):
+        load_picked(c).wait()
 
     def step(z, _):
         slot = lax.rem(z, slots)
 
         @pl.when(z + slots - 1 < depth)
         def _():
-            for copy in copies(z + slots - 1, lax.rem(z + slots - 1, slots)):
-                copy.start()
-
-        for copy in copies(z, slot):
-            copy.wait()
+            load(z + slots - 1, lax.rem(z + slots - 1, slots)).start()
+
+        for c in range(count):
+            at = (columns + c) * PITCH
+            rows[at : at + height] = picked_slab[c, z].astype(F32)
+        load(z, slot).wait()
         for c in range(columns):
             rows[c * PITCH : c * PITCH + height] = image_slab[slot, c].astype(F32)
-        for c in range(count):
-            at = (columns + c) * PITCH
-            rows[at : at + height] = basis_slab[slot, picked[c]].astype(F32)
-        for y in range(0, height, 16):
-            turned[z, y : y + 16] = jnp.swapaxes(basis_slab[slot, :, y : y + 16, :], 0, 1)
         both = jnp.concatenate(
             [rows[pl.ds(y, total, stride=PITCH), :].astype(BF16) for y in range(height)], 1
         )
-        part = lax.dot_general(both, both[:columns], NT, preferred_element_type=F32)
-        sums[:, :columns] += part
+        sums[...] += lax.dot_general(both, both[:columns], NT, preferred_element_type=F32)
         return 0
 
     lax.fori_loop(0, depth, step, 0)
@@ -73,37 +105,42 @@
 
 
 def normal_kernel(
-    sums, turned, material, z_low, z_high, y_low, y_high, packed, field, gram, sems
+    sums, turned, material, z_low, z_high, y_low, y_high, packed, field, kinds, gram, sems, kind_sem
 ):
     depth, height, columns, width = turned.shape
     count = sums.shape[0] - columns
-    copies = [
-        pltpu.make_async_copy(turned.at[z], field.at[z + 1, 1 : height + 1], sems.at[z])
-        for z in range(depth)
-    ]
-    for copy in copies:
+    kind_load = pltpu.make_async_copy(material, kinds, kind_sem)
+    loads = [pltpu.make_async_copy(z_low, field.at[0], sems.at[0])]
+    for z in range(depth):
+        loads.append(pltpu.make_async_copy(turned.at[z], field.at[z + 1], sems.at[z + 1]))
+    loads.append(pltpu.make_async_copy(z_high, field.at[depth + 1], sems.at[depth + 1]))
+    for copy in [kind_load] + loads:
         copy.start()
-    for y in range(0, height, 16):
-        field[0, y + 1 : y + 17] = jnp.swapaxes(z_low[:, y : y + 16, :], 0, 1)
-        field[depth + 1, y + 1 : y + 17] = jnp.swapaxes(z_high[:, y : y + 16, :], 0, 1)
-    low = jnp.swapaxes(y_low[...], 0, 1)
-    high = jnp.swapaxes(y_high[...], 0, 1)
-    for z in range(depth):
-        field[z + 1, 0] = low[z]
-        field[z + 1, height + 1] = high[z]
     gram[...] = jnp.zeros_like(gram)
-    for copy in copies:
-        copy.wait()
     lane = lax.broadcasted_iota(jnp.int32, (columns, width), 1)
     first, last = lane == 0, lane == width - 1
+    kind_load.wait()
+    loads[0].wait()
+    loads[1].wait()
 
     def step(z, _):
-        scale = coefficient(material[z])
+        @pl.when(z < depth - 1)
+        def _():
+            pltpu.make_async_copy(turned.at[z + 1], field.at[z + 2], sems.at[z + 2]).wait()
+
+        @pl.when(z == depth - 1)
+        def _():
+            loads[depth + 1].wait()
+
+        scale = coefficient(kinds[z])
+        middle = [y_low[z].astype(F32), field[z + 1, 0].astype(F32)]
         highs, lows = [], []
         for y in range(height):
-            row = field[z + 1, y + 1].astype(F32)
-            beside = field[z, y + 1].astype(F32) + field[z + 2, y + 1].astype(F32)
-            beside = beside + (field[z + 1, y].astype(F32) + field[z + 1, y + 2].astype(F32))
+            after = y_high[z] if y == height - 1 else field[z + 1, y + 1]
+            middle.append(after.astype(F32))
+            row = middle[y + 1]
+            beside = field[z, y].astype(F32) + field[z + 2, y].astype(F32)
+            beside = beside + (middle[y] + middle[y + 2])
             beside = beside + beside_in_row(row, first, last)
             image = scale[y : y + 1, :] * row - beside
             rounded = image.astype(BF16)
@@ -211,19 +248,17 @@
 
 def update_kernel(
     packed, turned, material, z_low, z_high, y_low, y_high, recycle, images,
-    field, planes, first_out, second_out, load_sems, store_sems,
+    field, kinds, planes, first_out, second_out, load_sems, kind_sem, store_sems,
 ):
     depth, height, columns, width = turned.shape
     count = recycle.shape[0]
-    loads = [
-        pltpu.make_async_copy(turned.at[z], field.at[z + 1], load_sems.at[z])
-        for z in range(depth)
-    ]
+    loads = [pltpu.make_async_copy(z_low, field.at[0], load_sems.at[0])]
+    for z in range(depth):
+        loads.append(pltpu.make_async_copy(turned.at[z], field.at[z + 1], load_sems.at[z + 1]))
+    loads.append(pltpu.make_async_copy(z_high, field.at[depth + 1], load_sems.at[depth + 1]))
+    loads.append(pltpu.make_async_copy(material, kinds, kind_sem))
     for copy in loads:
         copy.start()
-    for y in range(0, height, 16):
-        field[0, y : y + 16] = jnp.swapaxes(z_low[:, y : y + 16, :], 0, 1)
-        field[depth + 1, y : y + 16] = jnp.swapaxes(z_high[:, y : y + 16, :], 0, 1)
     weights = combination(packed[...], columns, count)
     rounded = weights.astype(BF16)
     both = jnp.concatenate([rounded, (weights - rounded.astype(F32)).astype(BF16)], 0)
@@ -232,10 +267,8 @@
         part = jnp.dot(both, row, preferred_element_type=F32)
         return part[:count] + part[count:]
 
-    low = jnp.swapaxes(y_low[...], 0, 1)
-    high = jnp.swapaxes(y_high[...], 0, 1)
-    low = combine(jnp.concatenate([low[z] for z in range(depth)], 1))
-    high = combine(jnp.concatenate([high[z] for z in range(depth)], 1))
+    low = combine(jnp.concatenate([y_low[z] for z in range(depth)], 1))
+    high = combine(jnp.concatenate([y_high[z] for z in range(depth)], 1))
     for z in range(depth):
         planes[z + 1, 0] = low[:, z * width : (z + 1) * width]
         planes[z + 1, height + 1] = high[:, z * width : (z + 1) * width]
@@ -249,8 +282,8 @@
 
     def stores(z, slot):
         return (
-            pltpu.make_async_copy(first_out.at[slot], recycle.at[:, z], store_sems.at[slot, 0]),
-            pltpu.make_async_copy(second_out.at[slot], images.at[:, z], store_sems.at[slot, 1]),
+            pltpu.make_async_copy(first_out.at[slot, :, :height], recycle.at[:, z], store_sems.at[slot, 0]),
+            pltpu.make_async_copy(second_out.at[slot, :, :height], images.at[:, z], store_sems.at[slot, 1]),
         )
 
     fill(0)
@@ -267,16 +300,16 @@
             for copy in stores(z - 2, slot):
                 copy.wait()
 
-        scale = coefficient(material[z])
-        one = first_out.at[slot].reshape(count * height, width)
-        two = second_out.at[slot].reshape(count * height, width)
+        scale = coefficient(kinds[z])
+        one = first_out.at[slot].reshape(count * STEP, width)
+        two = second_out.at[slot].reshape(count * STEP, width)
         for y in range(height):
             row = planes[z + 1, y + 1]
             beside = planes[z, y + 1] + planes[z + 2, y + 1]
             beside = beside + (planes[z + 1, y] + planes[z + 1, y + 2])
             beside = beside + beside_in_row(row, first, last)
-            one[pl.ds(y, count, stride=height), :] = row
-            two[pl.ds(y, count, stride=height), :] = scale[y : y + 1, :] * row - beside
+            one[pl.ds(y, count, stride=STEP), :] = row
+            two[pl.ds(y, count, stride=STEP), :] = scale[y : y + 1, :] * row - beside
         for copy in stores(z, slot):
             copy.start()
         return 0
@@ -321,37 +354,51 @@
         down = [(j, i) for i, j in up]
         return lax.ppermute(high_face, axis, up), lax.ppermute(low_face, axis, down)
 
-    z_low, z_high = neighbours(basis[:, 0], basis[:, depth - 1], "slab", slabs)
-    y_low, y_high = neighbours(basis[:, :, 0], basis[:, :, height - 1], "pencil", pencils)
-
-    sums, turned = pl.pallas_call(
-        gram_kernel,
-        in_specs=[whole(pltpu.SMEM), whole(pl.ANY), whole(pl.ANY)],
-        out_specs=[whole(), whole()],
-        out_shape=[
-            jax.ShapeDtypeStruct((columns + count, columns), F32),
-            jax.ShapeDtypeStruct((depth, height, columns, width), BF16),
-        ],
+    face = jax.ShapeDtypeStruct((height, columns, width), BF16)
+    edge = jax.ShapeDtypeStruct((depth, columns, width), BF16)
+    turned, z_first, z_last, y_first, y_last = pl.pallas_call(
+        turn_kernel,
+        in_specs=[whole(pltpu.HBM)],
+        out_specs=[whole()] * 5,
+        out_shape=[jax.ShapeDtypeStruct((depth, height, columns, width), BF16), face, face, edge, edge],
         scratch_shapes=[
             pltpu.VMEM((3, columns, height, width), BF16),
+            pltpu.SemaphoreType.DMA((3,)),
+        ],
+        compiler_params=pltpu.CompilerParams(vmem_limit_bytes=46 * MIB),
+        name="turn",
+    )(basis)
+    z_low, z_high = neighbours(z_first, z_last, "slab", slabs)
+    y_low, y_high = neighbours(y_first, y_last, "pencil", pencils)
+    sums = pl.pallas_call(
+        gram_kernel,
+        in_specs=[whole(pltpu.SMEM), whole(pltpu.HBM), whole(pltpu.HBM)],
+        out_specs=whole(),
+        out_shape=jax.ShapeDtypeStruct((columns + count, columns), F32),
+        scratch_shapes=[
             pltpu.VMEM((3, columns, height, width), BF16),
+            pltpu.VMEM((count, depth, height, width), BF16),
             pltpu.VMEM(((columns + count) * PITCH, width), F32),
-            pltpu.SemaphoreType.DMA((3, 2)),
+            pltpu.SemaphoreType.DMA((3,)),
+            pltpu.SemaphoreType.DMA((count,)),
         ],
-        compiler_params=pltpu.CompilerParams(vmem_limit_bytes=24 * MIB),
+        compiler_params=pltpu.CompilerParams(vmem_limit_bytes=51 * MIB),
         cost_estimate=pl.CostEstimate(flops=2 * 10**9, bytes_accessed=17 * 10**6, transcendentals=0),
         name="gram",
     )(picked, image, basis)
     faces = (z_low, z_high, y_low, y_high)
+    specs = [whole(), whole(pl.ANY), whole(pltpu.HBM), whole(pl.ANY), whole(pl.ANY), whole(), whole()]
     packed = pl.pallas_call(
         normal_kernel,
-        in_specs=[whole(), whole(pl.ANY), whole(), whole(), whole(), whole(), whole()],
+        in_specs=specs,
         out_specs=whole(),
         out_shape=jax.ShapeDtypeStruct((columns, 128), F32),
         scratch_shapes=[
-            pltpu.VMEM((depth + 2, height + 2, columns, width), BF16),
+            pltpu.VMEM((depth + 2, height, columns, width), BF16),
+            pltpu.VMEM((depth, height, width), jnp.int32),
             pltpu.VMEM((2 * columns, columns), F32),
-            pltpu.SemaphoreType.DMA((depth,)),
+            pltpu.SemaphoreType.DMA((depth + 2,)),
+            pltpu.SemaphoreType.DMA,
         ],
         compiler_params=pltpu.CompilerParams(vmem_limit_bytes=24 * MIB),
         name="normal",
@@ -360,15 +407,17 @@
     grid_shape = (count, depth, height, width)
     return pl.pallas_call(
         update_kernel,
-        in_specs=[whole(), whole(pl.ANY), whole(), whole(), whole(), whole(), whole()],
-        out_specs=[whole(pl.ANY), whole(pl.ANY)],
+        in_specs=specs,
+        out_specs=[whole(pltpu.HBM), whole(pltpu.HBM)],
         out_shape=[jax.ShapeDtypeStruct(grid_shape, F32)] * 2,
         scratch_shapes=[
             pltpu.VMEM((depth + 2, height, columns, width), BF16),
+            pltpu.VMEM((depth, height, width), jnp.int32),
             pltpu.VMEM((depth + 2, height + 2, count, width), F32),
-            pltpu.VMEM((2, count, height, width), F32),
-            pltpu.VMEM((2, count, height, width), F32),
-            pltpu.SemaphoreType.DMA((depth,)),
+            pltpu.VMEM((2, count, STEP, width), F32),
+            pltpu.VMEM((2, count, STEP, width), F32),
+            pltpu.SemaphoreType.DMA((depth + 2,)),
+            pltpu.SemaphoreType.DMA,
             pltpu.SemaphoreType.DMA((2, 2)),
         ],
         compiler_params=pltpu.CompilerParams(vmem_limit_bytes=32 * MIB),

time: 92.6 us -> 81.1 us (0.88)
  local copies, waits for them, and re-layouts: 10 us -> 0.01 us
  Pallas kernels: 41.1 us -> 39.5 us
    unnamed x10 -> x4, local copies, waits for them, and re-layouts: 5.98 us -> 0.01 us
    slice x1 -> x0, local copies, waits for them, and re-layouts: 2.47 us -> none  [local(): basis[:, :, 0]]
    ppermute x10, starting transfers between devices: 18.6 us -> 20.4 us  [shifted(): return lax.ppermute(value, axis, perm)]
    squeeze x1 -> x0, local copies, waits for them, and re-layouts: 1.6 us -> none  [local(): z_low, z_high = neighbours(basis[:, 0], basis[:, depth - 1], 'slab', slabs)]
    pallas_call x3 -> x4, Pallas kernels: 41.1 us -> 39.5 us  [the longest x1 15.2 us: local(): pl.pallas_call(update_kernel, in_specs=specs, out_specs=[whole(pltpu.HBM)...]
    ppermute x2, starting transfers between devices: 6.65 us -> 5.36 us  [neighbours(): lax.ppermute(high_face, axis, up)]
  transfers between devices with their start and end apart: 14 -> 14, of which waited for: 5 -> 5; matrix products, arithmetic and copies ran while one was open for 3% -> 0% of each run, Pallas kernels for 9% -> 9%
where the time goes in v1:
time: 81.1 us; the launch traced here: 80.5 us
  Pallas kernels  39.5 us (49%)
  starting transfers between devices  28.4 us (35%)
  waiting for transfers between devices  11.8 us (15%)
    ppermute x10, starting transfers between devices, shifted(): return lax.ppermute(value, axis, perm)  20.4 us
    pallas_call x1, Pallas kernels, local(): pl.pallas_call(update_kernel, in_specs=specs, out_specs=[whole(pltpu.HBM)...  15.2 us
    pallas_call x1, Pallas kernels, local(): pl.pallas_call(normal_kernel, in_specs=specs, out_specs=whole(), out_shap...  12.7 us
    ppermute x10, waiting for transfers between devices, shifted(): return lax.ppermute(value, axis, perm)  11.8 us
    pallas_call x1, Pallas kernels, local(): pl.pallas_call(gram_kernel, in_specs=[whole(pltpu.SMEM), whole(pltpu.HBM)...  7.05 us
    ppermute x2, starting transfers between devices, neighbours(): lax.ppermute(high_face, axis, up)  5.36 us
    pallas_call x1, Pallas kernels, local(): pl.pallas_call(turn_kernel, in_specs=[whole(pltpu.HBM)], out_specs=[whole...  4.51 us
    ppermute x2, starting transfers between devices, neighbours(): lax.ppermute(low_face, axis, down)  2.72 us
  transfers between devices with their start and end apart: 14, of which 5 were waited for; matrix products, arithmetic and copies ran while one was open for 0% of the time, Pallas kernels for 9%

profile of v1, /device:TPU:0, one launch (start us, length us, event | category | flops | bytes accessed | tf_op | source)
XLA Modules:
  0.0 80.5 jit_solution(9938573899878956023)
XLA Ops:
  0.6 0.0 copy-start.1
  0.6 4.5 %turn.1 = (bf16[8,32,88,128]{3,2,1,0:T(8,128)(2,1)S(1)}, bf16[32,88,128]{2,1,0:T(8,128)(2,1)S(1)}, bf16[32,88,128]{2,1,0:T(8,128)(2,1)S(1)}, bf16[8,88,128]{2,1,0:T(8,128)(2,1)S(1)}, bf16[8,88,128]{2,1,0:T(8,128)(2,1)S(1)}) custom-call(bf16[88,8,32,128]{3,2,1,0:T(8,128)(2,1)} %basis.3), custom_call_target="tpu_custom_call" | custom-call | tf_op jit(solution)/shard_map/turn/pallas_call | solution.py:359
  5.2 1.3 %collective-permute-start = (bf16[32,88,128]{2,1,0:T(8,128)(2,1)S(1)}, bf16[32,88,128]{2,1,0:T(8,128)(2,1)S(1)}, u32[]{:S(2)}, u32[]{:S(2)}) collective-permute-start(bf16[32,88,128]{2,1,0:T(8,128)(2,1)S(1)} %get-tuple-element.8), channel_id=1, source_target_pairs={{0,4},{4,8},{8,12},{12,16},{16,20},{20,24},{24,28},{28,32},{32,36}... | collective-permute-start | bytes 2162696 | tf_op jit(solution)/shard_map/ppermute | solution.py:355
  6.5 1.3 %collective-permute-start.1 = (bf16[32,88,128]{2,1,0:T(8,128)(2,1)S(1)}, bf16[32,88,128]{2,1,0:T(8,128)(2,1)S(1)}, u32[]{:S(2)}, u32[]{:S(2)}) collective-permute-start(bf16[32,88,128]{2,1,0:T(8,128)(2,1)S(1)} %get-tuple-element.9), channel_id=1, source_target_pairs={{4,0},{8,4},{12,8},{16,12},{20,16},{24,20},{28,24},{32,28},{36,32}... | collective-permute-start | bytes 2162696 | tf_op jit(solution)/shard_map/ppermute | solution.py:355
  7.8 4.0 %collective-permute-start.2 = (bf16[8,88,128]{2,1,0:T(8,128)(2,1)S(1)}, bf16[8,88,128]{2,1,0:T(8,128)(2,1)S(1)}, u32[]{:S(2)}, u32[]{:S(2)}) collective-permute-start(bf16[8,88,128]{2,1,0:T(8,128)(2,1)S(1)} %get-tuple-element.10), channel_id=1, source_target_pairs={{0,1},{1,2},{2,3},{4,5},{5,6},{6,7},{8,9},{9,10},{10,11},{12,13},{... | collective-permute-start | bytes 540680 | tf_op jit(solution)/shard_map/ppermute | solution.py:355
  11.8 0.0 copy-start
  11.8 1.4 %collective-permute-start.3 = (bf16[8,88,128]{2,1,0:T(8,128)(2,1)S(1)}, bf16[8,88,128]{2,1,0:T(8,128)(2,1)S(1)}, u32[]{:S(2)}, u32[]{:S(2)}) collective-permute-start(bf16[8,88,128]{2,1,0:T(8,128)(2,1)S(1)} %get-tuple-element.11), channel_id=1, source_target_pairs={{1,0},{2,1},{3,2},{5,4},{6,5},{7,6},{9,8},{10,9},{11,10},{13,12},{... | collective-permute-start | bytes 540680 | tf_op jit(solution)/shard_map/ppermute | solution.py:355
  13.3 0.0 copy-done.1
  13.3 7.0 %gram.1.sums = f32[120,88]{1,0:T(8,128)S(1)} custom-call(s32[32]{0:T(128)S(1)} %copy-done.1, bf16[88,8,32,128]{3,2,1,0:T(8,128)(2,1)} %image.1, bf16[88,8,32,128]{3,2,1,0:T(8,128)(2,1)} %basis.3), custom_call_target="tpu_custom_call" | custom-call | flops 2000000000 | bytes 17000000 | tf_op jit(solution)/shard_map/gram/pallas_call | solution.py:373
  20.3 0.0 collective-permute-done.2.y_low
  20.4 0.0 collective-permute-done.3.y_high
  20.4 0.0 collective-permute-done.z_low
  20.4 0.0 collective-permute-done.1.z_high
  20.4 0.0 copy-done
  20.4 12.7 %normal.1 = f32[88,128]{1,0:T(8,128)S(1)} custom-call(f32[120,88]{1,0:T(8,128)S(1)} %gram.1.sums, bf16[8,32,88,128]{3,2,1,0:T(8,128)(2,1)S(1)} %get-tuple-element.7.turned, s32[8,32,128]{2,1,0:T(8,128)S(1)} %copy-done, bf16[32,88,128]{2,1,0:T(8,128)(2,1)S(1)} %collective-permute-done.z_low, bf16[32,88,128]{2,1,0:T(8,128)(2,1)S(1)} %collective-permute-done.1.z_high, ...), custom_call_target="tpu_custom_call" | custom-call | tf_op jit(solution)/shard_map/normal/pallas_call | solution.py:391
  33.1 2.6 %collective-permute-start.4 = (f32[88,128]{1,0:T(8,128)S(1)}, f32[88,128]{1,0:T(8,128)S(1)}, u32[]{:S(2)}, u32[]{:S(2)}) collective-permute-start(f32[88,128]{1,0:T(8,128)S(1)} %normal.1), channel_id=1, source_target_pairs={{0,4},{4,0},{8,12},{12,8},{16,20},{20,16},{24,28},{28,24},{32,36},... | collective-permute-start | bytes 135176 | tf_op jit(solution)/shard_map/ppermute | solution.py:325
  35.7 0.9 %collective-permute-done.4 = f32[88,128]{1,0:T(8,128)S(1)} collective-permute-done((f32[88,128]{1,0:T(8,128)S(1)}, f32[88,128]{1,0:T(8,128)S(1)}, u32[]{:S(2)}, u32[]{:S(2)}) %collective-permute-start.4) | collective-permute-done | bytes 45088 | tf_op jit(solution)/shard_map/ppermute | solution.py:325
  36.6 5.3 %collective-permute-start.7 = (f32[88,128]{1,0:T(8,128)S(1)}, f32[88,128]{1,0:T(8,128)S(1)}, u32[]{:S(2)}, u32[]{:S(2)}) collective-permute-start(f32[88,128]{1,0:T(8,128)S(1)} %add.30), channel_id=1, source_target_pairs={{0,96},{4,100},{8,104},{12,108},{16,112},{20,116},{24,120},{28,124... | collective-permute-start | bytes 135176 | tf_op jit(solution)/shard_map/ppermute | solution.py:325
  41.9 0.0 collective-permute-start.6
  41.9 2.3 %collective-permute-start.5 = (f32[88,128]{1,0:T(8,128)S(1)}, f32[88,128]{1,0:T(8,128)S(1)}, u32[]{:S(2)}, u32[]{:S(2)}) collective-permute-start(f32[88,128]{1,0:T(8,128)S(1)} %add.30), channel_id=1, source_target_pairs={{0,64},{4,68},{8,72},{12,76},{16,80},{20,84},{24,88},{28,92},{32,9... | collective-permute-start | bytes 135176 | tf_op jit(solution)/shard_map/ppermute | solution.py:325
  44.1 0.0 collective-permute-done.7
  44.1 3.5 %collective-permute-done.6 = f32[88,128]{1,0:T(8,128)S(1)} collective-permute-done((f32[88,128]{1,0:T(8,128)S(1)}, f32[88,128]{1,0:T(8,128)S(1)}, u32[]{:S(2)}, u32[]{:S(2)}) %collective-permute-start.6) | collective-permute-done | bytes 45088 | tf_op jit(solution)/shard_map/ppermute | solution.py:325
  47.6 0.0 collective-permute-done.5
  47.6 2.0 %collective-permute-start.10 = (f32[88,128]{1,0:T(8,128)S(1)}, f32[88,128]{1,0:T(8,128)S(1)}, u32[]{:S(2)}, u32[]{:S(2)}) collective-permute-start(f32[88,128]{1,0:T(8,128)S(1)} %add_add_fusion.2), channel_id=1, source_target_pairs={{0,24},{4,28},{8,0},{12,4},{16,8},{20,12},{24,16},{28,20},{32,56},... | collective-permute-start | bytes 135176 | tf_op jit(solution)/shard_map/ppermute | solution.py:325
  49.6 0.1 collective-permute-start.9
  49.7 1.8 %collective-permute-start.8 = (f32[88,128]{1,0:T(8,128)S(1)}, f32[88,128]{1,0:T(8,128)S(1)}, u32[]{:S(2)}, u32[]{:S(2)}) collective-permute-start(f32[88,128]{1,0:T(8,128)S(1)} %add_add_fusion.2), channel_id=1, source_target_pairs={{0,16},{4,20},{8,24},{12,28},{16,0},{20,4},{24,8},{28,12},{32,48},... | collective-permute-start | bytes 135176 | tf_op jit(solution)/shard_map/ppermute | solution.py:325
  51.5 0.2 collective-permute-done.10
  51.7 3.6 %collective-permute-done.9 = f32[88,128]{1,0:T(8,128)S(1)} collective-permute-done((f32[88,128]{1,0:T(8,128)S(1)}, f32[88,128]{1,0:T(8,128)S(1)}, u32[]{:S(2)}, u32[]{:S(2)}) %collective-permute-start.9) | collective-permute-done | bytes 45088 | tf_op jit(solution)/shard_map/ppermute | solution.py:325
  55.4 0.0 collective-permute-done.8
  55.4 4.2 %collective-permute-start.13 = (f32[88,128]{1,0:T(8,128)S(1)}, f32[88,128]{1,0:T(8,128)S(1)}, u32[]{:S(2)}, u32[]{:S(2)}) collective-permute-start(f32[88,128]{1,0:T(8,128)S(1)} %add_add_fusion.1), channel_id=1, source_target_pairs={{0,3},{1,0},{2,1},{3,2},{4,7},{5,4},{6,5},{7,6},{8,11},{9,8},{10,9... | collective-permute-start | bytes 135176 | tf_op jit(solution)/shard_map/ppermute | solution.py:325
  59.6 0.0 collective-permute-start.12
  59.6 2.2 %collective-permute-start.11 = (f32[88,128]{1,0:T(8,128)S(1)}, f32[88,128]{1,0:T(8,128)S(1)}, u32[]{:S(2)}, u32[]{:S(2)}) collective-permute-start(f32[88,128]{1,0:T(8,128)S(1)} %add_add_fusion.1), channel_id=1, source_target_pairs={{0,2},{1,3},{2,0},{3,1},{4,6},{5,7},{6,4},{7,5},{8,10},{9,11},{10,... | collective-permute-start | bytes 135176 | tf_op jit(solution)/shard_map/ppermute | solution.py:325
  61.8 0.0 collective-permute-done.13
  61.8 3.5 %collective-permute-done.12 = f32[88,128]{1,0:T(8,128)S(1)} collective-permute-done((f32[88,128]{1,0:T(8,128)S(1)}, f32[88,128]{1,0:T(8,128)S(1)}, u32[]{:S(2)}, u32[]{:S(2)}) %collective-permute-start.12) | collective-permute-done | bytes 45088 | tf_op jit(solution)/shard_map/ppermute | solution.py:325
  65.3 0.0 collective-permute-done.11
  65.3 15.2 %update.1 = (f32[32,8,32,128]{3,2,1,0:T(8,128)}, f32[32,8,32,128]{3,2,1,0:T(8,128)}) custom-call(f32[88,128]{1,0:T(8,128)S(1)} %add_add_fusion.packed, bf16[8,32,88,128]{3,2,1,0:T(8,128)(2,1)S(1)} %get-tuple-element.7.turned, s32[8,32,128]{2,1,0:T(8,128)S(1)} %copy-done, bf16[32,88,128]{2,1,0:T(8,128)(2,1)S(1)} %collective-permute-done.z_low, ...), custom_call_target="tpu_custom_call" | custom-call | tf_op jit(solution)/shard_map/update/pallas_call | solution.py:408
  (4 shorter events, 0.1 us)
Async XLA Ops:
  0.6 12.7 %copy-start.1 = (s32[32]{0:T(128)S(1)}, s32[32]{0:T(128)}, u32[]{:S(2)}) copy-start(s32[32]{0:T(128)} %picked.1) | copy-start | bytes 388
  5.2 15.2 %collective-permute-start = (bf16[32,88,128]{2,1,0:T(8,128)(2,1)S(1)}, bf16[32,88,128]{2,1,0:T(8,128)(2,1)S(1)}, u32[]{:S(2)}, u32[]{:S(2)}) collective-permute-start(bf16[32,88,128]{2,1,0:T(8,128)(2,1)S(1)} %get-tuple-element.8), channel_id=1, source_target_pairs={{0,4},{4,8},{8,12},{12,16},{16,20},{20,24},{24,28},{28,32},{32,36}... | collective-permute-start | bytes 2162696 | tf_op jit(solution)/shard_map/ppermute | solution.py:355
  6.5 13.9 %collective-permute-start.1 = (bf16[32,88,128]{2,1,0:T(8,128)(2,1)S(1)}, bf16[32,88,128]{2,1,0:T(8,128)(2,1)S(1)}, u32[]{:S(2)}, u32[]{:S(2)}) collective-permute-start(bf16[32,88,128]{2,1,0:T(8,128)(2,1)S(1)} %get-tuple-element.9), channel_id=1, source_target_pairs={{4,0},{8,4},{12,8},{16,12},{20,16},{24,20},{28,24},{32,28},{36,32}... | collective-permute-start | bytes 2162696 | tf_op jit(solution)/shard_map/ppermute | solution.py:355
  7.8 12.5 %collective-permute-start.2 = (bf16[8,88,128]{2,1,0:T(8,128)(2,1)S(1)}, bf16[8,88,128]{2,1,0:T(8,128)(2,1)S(1)}, u32[]{:S(2)}, u32[]{:S(2)}) collective-permute-start(bf16[8,88,128]{2,1,0:T(8,128)(2,1)S(1)} %get-tuple-element.10), channel_id=1, source_target_pairs={{0,1},{1,2},{2,3},{4,5},{5,6},{6,7},{8,9},{9,10},{10,11},{12,13},{... | collective-permute-start | bytes 540680 | tf_op jit(solution)/shard_map/ppermute | solution.py:355
  11.8 8.6 %copy-start = (s32[8,32,128]{2,1,0:T(8,128)S(1)}, s32[8,32,128]{2,1,0:T(8,128)}, u32[]{:S(2)}) copy-start(s32[8,32,128]{2,1,0:T(8,128)} %material.3) | copy-start | bytes 393220
  11.8 8.5 %collective-permute-start.3 = (bf16[8,88,128]{2,1,0:T(8,128)(2,1)S(1)}, bf16[8,88,128]{2,1,0:T(8,128)(2,1)S(1)}, u32[]{:S(2)}, u32[]{:S(2)}) collective-permute-start(bf16[8,88,128]{2,1,0:T(8,128)(2,1)S(1)} %get-tuple-element.11), channel_id=1, source_target_pairs={{1,0},{2,1},{3,2},{5,4},{6,5},{7,6},{9,8},{10,9},{11,10},{13,12},{... | collective-permute-start | bytes 540680 | tf_op jit(solution)/shard_map/ppermute | solution.py:355
  33.1 3.5 %collective-permute-start.4 = (f32[88,128]{1,0:T(8,128)S(1)}, f32[88,128]{1,0:T(8,128)S(1)}, u32[]{:S(2)}, u32[]{:S(2)}) collective-permute-start(f32[88,128]{1,0:T(8,128)S(1)} %normal.1), channel_id=1, source_target_pairs={{0,4},{4,0},{8,12},{12,8},{16,20},{20,16},{24,28},{28,24},{32,36},... | collective-permute-start | bytes 135176 | tf_op jit(solution)/shard_map/ppermute | solution.py:325
  36.6 7.5 %collective-permute-start.7 = (f32[88,128]{1,0:T(8,128)S(1)}, f32[88,128]{1,0:T(8,128)S(1)}, u32[]{:S(2)}, u32[]{:S(2)}) collective-permute-start(f32[88,128]{1,0:T(8,128)S(1)} %add.30), channel_id=1, source_target_pairs={{0,96},{4,100},{8,104},{12,108},{16,112},{20,116},{24,120},{28,124... | collective-permute-start | bytes 135176 | tf_op jit(solution)/shard_map/ppermute | solution.py:325
  41.9 5.7 %collective-permute-start.6 = (f32[88,128]{1,0:T(8,128)S(1)}, f32[88,128]{1,0:T(8,128)S(1)}, u32[]{:S(2)}, u32[]{:S(2)}) collective-permute-start(f32[88,128]{1,0:T(8,128)S(1)} %add.30), channel_id=1, source_target_pairs={{0,32},{4,36},{8,40},{12,44},{16,48},{20,52},{24,56},{28,60},{32,6... | collective-permute-start | bytes 135176 | tf_op jit(solution)/shard_map/ppermute | solution.py:325
  41.9 5.7 %collective-permute-start.5 = (f32[88,128]{1,0:T(8,128)S(1)}, f32[88,128]{1,0:T(8,128)S(1)}, u32[]{:S(2)}, u32[]{:S(2)}) collective-permute-start(f32[88,128]{1,0:T(8,128)S(1)} %add.30), channel_id=1, source_target_pairs={{0,64},{4,68},{8,72},{12,76},{16,80},{20,84},{24,88},{28,92},{32,9... | collective-permute-start | bytes 135176 | tf_op jit(solution)/shard_map/ppermute | solution.py:325
  47.6 4.1 %collective-permute-start.10 = (f32[88,128]{1,0:T(8,128)S(1)}, f32[88,128]{1,0:T(8,128)S(1)}, u32[]{:S(2)}, u32[]{:S(2)}) collective-permute-start(f32[88,128]{1,0:T(8,128)S(1)} %add_add_fusion.2), channel_id=1, source_target_pairs={{0,24},{4,28},{8,0},{12,4},{16,8},{20,12},{24,16},{28,20},{32,56},... | collective-permute-start | bytes 135176 | tf_op jit(solution)/shard_map/ppermute | solution.py:325
  49.6 5.7 %collective-permute-start.9 = (f32[88,128]{1,0:T(8,128)S(1)}, f32[88,128]{1,0:T(8,128)S(1)}, u32[]{:S(2)}, u32[]{:S(2)}) collective-permute-start(f32[88,128]{1,0:T(8,128)S(1)} %add_add_fusion.2), channel_id=1, source_target_pairs={{0,8},{4,12},{8,16},{12,20},{16,24},{20,28},{24,0},{28,4},{32,40},... | collective-permute-start | bytes 135176 | tf_op jit(solution)/shard_map/ppermute | solution.py:325
  49.7 5.7 %collective-permute-start.8 = (f32[88,128]{1,0:T(8,128)S(1)}, f32[88,128]{1,0:T(8,128)S(1)}, u32[]{:S(2)}, u32[]{:S(2)}) collective-permute-start(f32[88,128]{1,0:T(8,128)S(1)} %add_add_fusion.2), channel_id=1, source_target_pairs={{0,16},{4,20},{8,24},{12,28},{16,0},{20,4},{24,8},{28,12},{32,48},... | collective-permute-start | bytes 135176 | tf_op jit(solution)/shard_map/ppermute | solution.py:325
  55.4 6.4 %collective-permute-start.13 = (f32[88,128]{1,0:T(8,128)S(1)}, f32[88,128]{1,0:T(8,128)S(1)}, u32[]{:S(2)}, u32[]{:S(2)}) collective-permute-start(f32[88,128]{1,0:T(8,128)S(1)} %add_add_fusion.1), channel_id=1, source_target_pairs={{0,3},{1,0},{2,1},{3,2},{4,7},{5,4},{6,5},{7,6},{8,11},{9,8},{10,9... | collective-permute-start | bytes 135176 | tf_op jit(solution)/shard_map/ppermute | solution.py:325
  59.6 5.7 %collective-permute-start.12 = (f32[88,128]{1,0:T(8,128)S(1)}, f32[88,128]{1,0:T(8,128)S(1)}, u32[]{:S(2)}, u32[]{:S(2)}) collective-permute-start(f32[88,128]{1,0:T(8,128)S(1)} %add_add_fusion.1), channel_id=1, source_target_pairs={{0,1},{1,2},{2,3},{3,0},{4,5},{5,6},{6,7},{7,4},{8,9},{9,10},{10,1... | collective-permute-start | bytes 135176 | tf_op jit(solution)/shard_map/ppermute | solution.py:325
  59.6 5.7 %collective-permute-start.11 = (f32[88,128]{1,0:T(8,128)S(1)}, f32[88,128]{1,0:T(8,128)S(1)}, u32[]{:S(2)}, u32[]{:S(2)}) collective-permute-start(f32[88,128]{1,0:T(8,128)S(1)} %add_add_fusion.1), channel_id=1, source_target_pairs={{0,2},{1,3},{2,0},{3,1},{4,6},{5,7},{6,4},{7,5},{8,10},{9,11},{10,... | collective-permute-start | bytes 135176 | tf_op jit(solution)/shard_map/ppermute | solution.py:325

commit v2 on v1

--- a/solution.py
+++ b/solution.py
@@ -10,6 +10,7 @@
 CELLS = 4194304.0
 PITCH = 44
 STEP = 40
+SLOTS = 2
 NT = (((1,), (1,)), ((), ()))
 TN = (((0,), (0,)), ((), ()))
 MIB = 2**20
@@ -105,7 +106,8 @@
 
 
 def normal_kernel(
-    sums, turned, material, z_low, z_high, y_low, y_high, packed, field, kinds, gram, sems, kind_sem
+    edges, sums, turned, material, z_low, z_high, y_low, y_high,
+    packed, field, kinds, gram, sems, kind_sem,
 ):
     depth, height, columns, width = turned.shape
     count = sums.shape[0] - columns
@@ -123,6 +125,12 @@
     loads[0].wait()
     loads[1].wait()
 
+    @pl.when(edges[0] == 0)
+    def _():
+        field[0] = jnp.zeros(field.shape[1:], BF16)
+
+    inside = [edges[i].astype(F32) for i in (2, 3)]
+
     def step(z, _):
         @pl.when(z < depth - 1)
         def _():
@@ -132,12 +140,18 @@
         def _():
             loads[depth + 1].wait()
 
+            @pl.when(edges[1] == 0)
+            def _():
+                field[depth + 1] = jnp.zeros(field.shape[1:], BF16)
+
         scale = coefficient(kinds[z])
-        middle = [y_low[z].astype(F32), field[z + 1, 0].astype(F32)]
+        middle = [y_low[z].astype(F32) * inside[0], field[z + 1, 0].astype(F32)]
         highs, lows = [], []
         for y in range(height):
-            after = y_high[z] if y == height - 1 else field[z + 1, y + 1]
-            middle.append(after.astype(F32))
+            if y == height - 1:
+                middle.append(y_high[z].astype(F32) * inside[1])
+            else:
+                middle.append(field[z + 1, y + 1].astype(F32))
             row = middle[y + 1]
             beside = field[z, y].astype(F32) + field[z + 2, y].astype(F32)
             beside = beside + (middle[y] + middle[y + 2])
@@ -147,8 +161,11 @@
             highs.append(rounded)
             lows.append((image - rounded.astype(F32)).astype(BF16))
         rounded = jnp.concatenate(highs, 1)
-        both = jnp.concatenate([rounded, jnp.concatenate(lows, 1)], 0)
-        gram[...] += lax.dot_general(both, rounded, NT, preferred_element_type=F32)
+        gap = jnp.zeros((16 - columns % 16, height * width), BF16)
+        both = jnp.concatenate([rounded, gap, jnp.concatenate(lows, 1)], 0)
+        part = lax.dot_general(both, rounded, NT, preferred_element_type=F32)
+        gram[:columns] += part[:columns]
+        gram[columns:] += part[both.shape[0] - columns :]
         return 0
 
     lax.fori_loop(0, depth, step, 0)
@@ -247,7 +264,7 @@
 
 
 def update_kernel(
-    packed, turned, material, z_low, z_high, y_low, y_high, recycle, images,
+    edges, packed, turned, material, z_low, z_high, y_low, y_high, recycle, images,
     field, kinds, planes, first_out, second_out, load_sems, kind_sem, store_sems,
 ):
     depth, height, columns, width = turned.shape
@@ -270,10 +287,18 @@
     low = combine(jnp.concatenate([y_low[z] for z in range(depth)], 1))
     high = combine(jnp.concatenate([y_high[z] for z in range(depth)], 1))
     for z in range(depth):
-        planes[z + 1, 0] = low[:, z * width : (z + 1) * width]
-        planes[z + 1, height + 1] = high[:, z * width : (z + 1) * width]
+        planes[z + 1, 0] = low[:, z * width : (z + 1) * width] * edges[2].astype(F32)
+        planes[z + 1, height + 1] = high[:, z * width : (z + 1) * width] * edges[3].astype(F32)
     for copy in loads:
         copy.wait()
+
+    @pl.when(edges[0] == 0)
+    def _():
+        field[0] = jnp.zeros(field.shape[1:], BF16)
+
+    @pl.when(edges[1] == 0)
+    def _():
+        field[depth + 1] = jnp.zeros(field.shape[1:], BF16)
 
     def fill(z):
         plane = combine(jnp.concatenate([field[z, y] for y in range(height)], 1))
@@ -292,12 +317,12 @@
     first, last = lane == 0, lane == width - 1
 
     def step(z, _):
-        slot = lax.rem(z, 2)
+        slot = lax.rem(z, SLOTS)
         fill(z + 2)
 
-        @pl.when(z >= 2)
+        @pl.when(z >= SLOTS)
         def _():
-            for copy in stores(z - 2, slot):
+            for copy in stores(z - SLOTS, slot):
                 copy.wait()
 
         scale = coefficient(kinds[z])
@@ -315,8 +340,8 @@
         return 0
 
     lax.fori_loop(0, depth, step, 0)
-    for z in (depth - 2, depth - 1):
-        for copy in stores(z, z % 2):
+    for z in range(depth - SLOTS, depth):
+        for copy in stores(z, z % SLOTS):
             copy.wait()
 
 
@@ -350,7 +375,7 @@
     slabs, pencils = lax.axis_size("slab"), lax.axis_size("pencil")
 
     def neighbours(low_face, high_face, axis, size):
-        up = [(i, i + 1) for i in range(size - 1)]
+        up = [(i, (i + 1) % size) for i in range(size)]
         down = [(j, i) for i, j in up]
         return lax.ppermute(high_face, axis, up), lax.ppermute(low_face, axis, down)
 
@@ -387,7 +412,10 @@
         name="gram",
     )(picked, image, basis)
     faces = (z_low, z_high, y_low, y_high)
-    specs = [whole(), whole(pl.ANY), whole(pltpu.HBM), whole(pl.ANY), whole(pl.ANY), whole(), whole()]
+    slab, pencil = lax.axis_index("slab"), lax.axis_index("pencil")
+    inner = (slab > 0, slab < slabs - 1, pencil > 0, pencil < pencils - 1)
+    edges = jnp.stack(inner).astype(jnp.int32)
+    specs = [whole(pltpu.SMEM), whole(), whole(pl.ANY), whole(pltpu.HBM), whole(pl.ANY), whole(pl.ANY), whole(), whole()]
     packed = pl.pallas_call(
         normal_kernel,
         in_specs=specs,
@@ -402,7 +430,7 @@
         ],
         compiler_params=pltpu.CompilerParams(vmem_limit_bytes=24 * MIB),
         name="normal",
-    )(sums, turned, material, *faces)
+    )(edges, sums, turned, material, *faces)
     packed = device_sum(packed)
     grid_shape = (count, depth, height, width)
     return pl.pallas_call(
@@ -414,15 +442,15 @@
             pltpu.VMEM((depth + 2, height, columns, width), BF16),
             pltpu.VMEM((depth, height, width), jnp.int32),
             pltpu.VMEM((depth + 2, height + 2, count, width), F32),
-            pltpu.VMEM((2, count, STEP, width), F32),
-            pltpu.VMEM((2, count, STEP, width), F32),
+            pltpu.VMEM((SLOTS, count, STEP, width), F32),
+            pltpu.VMEM((SLOTS, count, STEP, width), F32),
             pltpu.SemaphoreType.DMA((depth + 2,)),
             pltpu.SemaphoreType.DMA,
-            pltpu.SemaphoreType.DMA((2, 2)),
+            pltpu.SemaphoreType.DMA((SLOTS, 2)),
         ],
         compiler_params=pltpu.CompilerParams(vmem_limit_bytes=32 * MIB),
         name="update",
-    )(packed, turned, material, *faces)
+    )(edges, packed, turned, material, *faces)
 
 
 def solution(mesh):

time: 81.1 us -> 79.5 us (0.980)
  starting transfers between devices: 28.4 us -> 21.1 us
  local copies, waits for them, and re-layouts: 0.01 us -> 2.5 us
  Pallas kernels: 39.5 us -> 41.4 us
  waiting for transfers between devices: 11.8 us -> 13.4 us
    ppermute x10, starting transfers between devices: 20.4 us -> 12.1 us  [shifted(): return lax.ppermute(value, axis, perm)]
    ppermute x2, starting transfers between devices: 2.72 us -> 7.41 us  [neighbours(): lax.ppermute(low_face, axis, down)]
    ppermute x2, starting transfers between devices: 5.36 us -> 1.58 us  [neighbours(): lax.ppermute(high_face, axis, up)]
    unnamed x4 -> x8, local copies, waits for them, and re-layouts: 0.01 us -> 2.5 us
    ppermute x10, waiting for transfers between devices: 11.8 us -> 13.4 us  [shifted(): return lax.ppermute(value, axis, perm)]
  transfers between devices with their start and end apart: 14 -> 14, of which waited for: 5 -> 8; matrix products, arithmetic and copies ran while one was open for 0% -> 0% of each run, Pallas kernels for 9% -> 10%
where the time goes in v2:
time: 79.5 us; the launch traced here: 79.2 us
  Pallas kernels  41.4 us (52%)
  starting transfers between devices  21.1 us (27%)
  waiting for transfers between devices  13.4 us (17%)
  local copies, waits for them, and re-layouts  2.5 us (3%)
    pallas_call x1, Pallas kernels, local(): pl.pallas_call(update_kernel, in_specs=specs, out_specs=[whole(pltpu.HBM)...  15.8 us
    ppermute x10, waiting for transfers between devices, shifted(): return lax.ppermute(value, axis, perm)  13.4 us
    pallas_call x1, Pallas kernels, local(): pl.pallas_call(normal_kernel, in_specs=specs, out_specs=whole(), out_shap...  12.9 us
    ppermute x10, starting transfers between devices, shifted(): return lax.ppermute(value, axis, perm)  12.1 us
    pallas_call x1, Pallas kernels, local(): pl.pallas_call(gram_kernel, in_specs=[whole(pltpu.SMEM), whole(pltpu.HBM)...  7.59 us
    ppermute x2, starting transfers between devices, neighbours(): lax.ppermute(low_face, axis, down)  7.41 us
    pallas_call x1, Pallas kernels, local(): pl.pallas_call(turn_kernel, in_specs=[whole(pltpu.HBM)], out_specs=[whole...  5.09 us
    unnamed x8, local copies, waits for them, and re-layouts  2.5 us
  transfers between devices with their start and end apart: 14, of which 8 were waited for; matrix products, arithmetic and copies ran while one was open for 0% of the time, Pallas kernels for 10%

profile of v2, /device:TPU:0, one launch (start us, length us, event | category | flops | bytes accessed | tf_op | source)
XLA Modules:
  0.0 79.2 jit_solution(2121367983841835314)
XLA Ops:
  0.6 0.0 copy-start.3
  0.6 5.1 %turn.1 = (bf16[8,32,88,128]{3,2,1,0:T(8,128)(2,1)S(1)}, bf16[32,88,128]{2,1,0:T(8,128)(2,1)S(1)}, bf16[32,88,128]{2,1,0:T(8,128)(2,1)S(1)}, bf16[8,88,128]{2,1,0:T(8,128)(2,1)S(1)}, bf16[8,88,128]{2,1,0:T(8,128)(2,1)}) custom-call(bf16[88,8,32,128]{3,2,1,0:T(8,128)(2,1)} %basis.3), custom_call_target="tpu_custom_call" | custom-call | tf_op jit(solution)/shard_map/turn/pallas_call | solution.py:384
  5.7 0.0 copy-start
  5.7 2.5 %copy-done = bf16[8,32,88,128]{3,2,1,0:T(8,128)(2,1)} copy-done((bf16[8,32,88,128]{3,2,1,0:T(8,128)(2,1)}, bf16[8,32,88,128]{3,2,1,0:T(8,128)(2,1)S(1)}, u32[]{:S(2)}) %copy-start) | copy-done | bytes 5767192
  8.2 0.0 collective-permute-start
  8.2 5.8 %collective-permute-start.1 = (bf16[32,88,128]{2,1,0:T(8,128)(2,1)S(1)}, bf16[32,88,128]{2,1,0:T(8,128)(2,1)S(1)}, u32[]{:S(2)}, u32[]{:S(2)}) collective-permute-start(bf16[32,88,128]{2,1,0:T(8,128)(2,1)S(1)} %get-tuple-element.9), channel_id=1, source_target_pairs={{4,0},{8,4},{12,8},{16,12},{20,16},{24,20},{28,24},{32,28},{36,32}... | collective-permute-start | bytes 2162696 | tf_op jit(solution)/shard_map/ppermute | solution.py:380
  14.0 1.6 %collective-permute-start.2 = (bf16[8,88,128]{2,1,0:T(8,128)(2,1)}, bf16[8,88,128]{2,1,0:T(8,128)(2,1)S(1)}, u32[]{:S(2)}, u32[]{:S(2)}) collective-permute-start(bf16[8,88,128]{2,1,0:T(8,128)(2,1)} %get-tuple-element.10), channel_id=1, source_target_pairs={{0,1},{1,2},{2,3},{3,0},{4,5},{5,6},{6,7},{7,4},{8,9},{9,10},{10,1... | collective-permute-start | bytes 540680 | tf_op jit(solution)/shard_map/ppermute | solution.py:380
  15.6 1.7 %collective-permute-start.3 = (bf16[8,88,128]{2,1,0:T(8,128)(2,1)S(1)}, bf16[8,88,128]{2,1,0:T(8,128)(2,1)S(1)}, u32[]{:S(2)}, u32[]{:S(2)}) collective-permute-start(bf16[8,88,128]{2,1,0:T(8,128)(2,1)S(1)} %get-tuple-element.11), channel_id=1, source_target_pairs={{1,0},{2,1},{3,2},{0,3},{5,4},{6,5},{7,6},{4,7},{9,8},{10,9},{11,1... | collective-permute-start | bytes 540680 | tf_op jit(solution)/shard_map/ppermute | solution.py:380
  17.2 0.1 add_convert_fusion.edges
  17.3 0.0 copy-done.3
  17.3 0.0 copy-start.1
  17.3 0.0 copy-start.2
  17.3 7.6 %gram.1.sums = f32[120,88]{1,0:T(8,128)S(1)} custom-call(s32[32]{0:T(128)S(1)} %copy-done.3, bf16[88,8,32,128]{3,2,1,0:T(8,128)(2,1)} %image.1, bf16[88,8,32,128]{3,2,1,0:T(8,128)(2,1)} %basis.3), custom_call_target="tpu_custom_call" | custom-call | flops 2000000000 | bytes 17000000 | tf_op jit(solution)/shard_map/gram/pallas_call | solution.py:398
  24.9 0.0 collective-permute-done.2.y_low
  24.9 0.0 collective-permute-done.3.y_high
  24.9 0.0 collective-permute-done.z_low
  24.9 0.0 collective-permute-done.1.z_high
  24.9 0.0 copy-done.1
  25.0 0.0 copy-done.2
  25.0 12.9 %normal.1 = f32[88,128]{1,0:T(8,128)S(1)} custom-call(s32[4]{0:T(128)S(1)} %add_convert_fusion.edges, f32[120,88]{1,0:T(8,128)S(1)} %gram.1.sums, bf16[8,32,88,128]{3,2,1,0:T(8,128)(2,1)S(1)} %copy-done.1, s32[8,32,128]{2,1,0:T(8,128)S(1)} %copy-done.2, bf16[32,88,128]{2,1,0:T(8,128)(2,1)S(1)} %collective-permute-done.z_low, ...), custom_call_target="tpu_custom_call" | custom-call | tf_op jit(solution)/shard_map/normal/pallas_call | solution.py:419
  37.9 0.1 collective-permute-start.4
  38.0 1.2 %collective-permute-done.4 = f32[88,128]{1,0:T(8,128)S(1)} collective-permute-done((f32[88,128]{1,0:T(8,128)S(1)}, f32[88,128]{1,0:T(8,128)S(1)}, u32[]{:S(2)}, u32[]{:S(2)}) %collective-permute-start.4) | collective-permute-done | bytes 45088 | tf_op jit(solution)/shard_map/ppermute | solution.py:350
  39.2 0.9 %collective-permute-start.7 = (f32[88,128]{1,0:T(8,128)S(1)}, f32[88,128]{1,0:T(8,128)S(1)}, u32[]{:S(2)}, u32[]{:S(2)}) collective-permute-start(f32[88,128]{1,0:T(8,128)S(1)} %add.30), channel_id=1, source_target_pairs={{0,96},{4,100},{8,104},{12,108},{16,112},{20,116},{24,120},{28,124... | collective-permute-start | bytes 135176 | tf_op jit(solution)/shard_map/ppermute | solution.py:350
  40.1 1.2 %collective-permute-start.6 = (f32[88,128]{1,0:T(8,128)S(1)}, f32[88,128]{1,0:T(8,128)S(1)}, u32[]{:S(2)}, u32[]{:S(2)}) collective-permute-start(f32[88,128]{1,0:T(8,128)S(1)} %add.30), channel_id=1, source_target_pairs={{0,32},{4,36},{8,40},{12,44},{16,48},{20,52},{24,56},{28,60},{32,6... | collective-permute-start | bytes 135176 | tf_op jit(solution)/shard_map/ppermute | solution.py:350
  41.3 1.1 %collective-permute-start.5 = (f32[88,128]{1,0:T(8,128)S(1)}, f32[88,128]{1,0:T(8,128)S(1)}, u32[]{:S(2)}, u32[]{:S(2)}) collective-permute-start(f32[88,128]{1,0:T(8,128)S(1)} %add.30), channel_id=1, source_target_pairs={{0,64},{4,68},{8,72},{12,76},{16,80},{20,84},{24,88},{28,92},{32,9... | collective-permute-start | bytes 135176 | tf_op jit(solution)/shard_map/ppermute | solution.py:350
  42.4 0.9 %collective-permute-done.7 = f32[88,128]{1,0:T(8,128)S(1)} collective-permute-done((f32[88,128]{1,0:T(8,128)S(1)}, f32[88,128]{1,0:T(8,128)S(1)}, u32[]{:S(2)}, u32[]{:S(2)}) %collective-permute-start.7) | collective-permute-done | bytes 45088 | tf_op jit(solution)/shard_map/ppermute | solution.py:350
  43.3 2.5 %collective-permute-done.6 = f32[88,128]{1,0:T(8,128)S(1)} collective-permute-done((f32[88,128]{1,0:T(8,128)S(1)}, f32[88,128]{1,0:T(8,128)S(1)}, u32[]{:S(2)}, u32[]{:S(2)}) %collective-permute-start.6) | collective-permute-done | bytes 45088 | tf_op jit(solution)/shard_map/ppermute | solution.py:350
  45.8 1.0 %collective-permute-done.5 = f32[88,128]{1,0:T(8,128)S(1)} collective-permute-done((f32[88,128]{1,0:T(8,128)S(1)}, f32[88,128]{1,0:T(8,128)S(1)}, u32[]{:S(2)}, u32[]{:S(2)}) %collective-permute-start.5) | collective-permute-done | bytes 45088 | tf_op jit(solution)/shard_map/ppermute | solution.py:350
  46.8 2.0 %collective-permute-start.10 = (f32[88,128]{1,0:T(8,128)S(1)}, f32[88,128]{1,0:T(8,128)S(1)}, u32[]{:S(2)}, u32[]{:S(2)}) collective-permute-start(f32[88,128]{1,0:T(8,128)S(1)} %add_add_fusion.2), channel_id=1, source_target_pairs={{0,24},{4,28},{8,0},{12,4},{16,8},{20,12},{24,16},{28,20},{32,56},... | collective-permute-start | bytes 135176 | tf_op jit(solution)/shard_map/ppermute | solution.py:350
  48.8 0.1 collective-permute-start.9
  48.9 1.4 %collective-permute-start.8 = (f32[88,128]{1,0:T(8,128)S(1)}, f32[88,128]{1,0:T(8,128)S(1)}, u32[]{:S(2)}, u32[]{:S(2)}) collective-permute-start(f32[88,128]{1,0:T(8,128)S(1)} %add_add_fusion.2), channel_id=1, source_target_pairs={{0,16},{4,20},{8,24},{12,28},{16,0},{20,4},{24,8},{28,12},{32,48},... | collective-permute-start | bytes 135176 | tf_op jit(solution)/shard_map/ppermute | solution.py:350
  50.4 0.6 collective-permute-done.10
  51.0 3.1 %collective-permute-done.9 = f32[88,128]{1,0:T(8,128)S(1)} collective-permute-done((f32[88,128]{1,0:T(8,128)S(1)}, f32[88,128]{1,0:T(8,128)S(1)}, u32[]{:S(2)}, u32[]{:S(2)}) %collective-permute-start.9) | collective-permute-done | bytes 45088 | tf_op jit(solution)/shard_map/ppermute | solution.py:350
  54.1 0.5 collective-permute-done.8
  54.6 3.1 %collective-permute-start.13 = (f32[88,128]{1,0:T(8,128)S(1)}, f32[88,128]{1,0:T(8,128)S(1)}, u32[]{:S(2)}, u32[]{:S(2)}) collective-permute-start(f32[88,128]{1,0:T(8,128)S(1)} %add_add_fusion.1), channel_id=1, source_target_pairs={{0,3},{1,0},{2,1},{3,2},{4,7},{5,4},{6,5},{7,6},{8,11},{9,8},{10,9... | collective-permute-start | bytes 135176 | tf_op jit(solution)/shard_map/ppermute | solution.py:350
  57.7 0.0 collective-permute-start.12
  57.7 2.2 %collective-permute-start.11 = (f32[88,128]{1,0:T(8,128)S(1)}, f32[88,128]{1,0:T(8,128)S(1)}, u32[]{:S(2)}, u32[]{:S(2)}) collective-permute-start(f32[88,128]{1,0:T(8,128)S(1)} %add_add_fusion.1), channel_id=1, source_target_pairs={{0,2},{1,3},{2,0},{3,1},{4,6},{5,7},{6,4},{7,5},{8,10},{9,11},{10,... | collective-permute-start | bytes 135176 | tf_op jit(solution)/shard_map/ppermute | solution.py:350
  59.9 0.0 collective-permute-done.13
  59.9 3.5 %collective-permute-done.12 = f32[88,128]{1,0:T(8,128)S(1)} collective-permute-done((f32[88,128]{1,0:T(8,128)S(1)}, f32[88,128]{1,0:T(8,128)S(1)}, u32[]{:S(2)}, u32[]{:S(2)}) %collective-permute-start.12) | collective-permute-done | bytes 45088 | tf_op jit(solution)/shard_map/ppermute | solution.py:350
  63.4 0.0 collective-permute-done.11
  63.4 15.8 %update.1 = (f32[32,8,32,128]{3,2,1,0:T(8,128)}, f32[32,8,32,128]{3,2,1,0:T(8,128)}) custom-call(s32[4]{0:T(128)S(1)} %add_convert_fusion.edges, f32[88,128]{1,0:T(8,128)S(1)} %add_add_fusion.packed, bf16[8,32,88,128]{3,2,1,0:T(8,128)(2,1)S(1)} %copy-done.1, s32[8,32,128]{2,1,0:T(8,128)S(1)} %copy-done.2, ...), custom_call_target="tpu_custom_call" | custom-call | tf_op jit(solution)/shard_map/update/pallas_call | solution.py:436
  (4 shorter events, 0.1 us)
Async XLA Ops:
  0.6 16.7 %copy-start.3 = (s32[32]{0:T(128)S(1)}, s32[32]{0:T(128)}, u32[]{:S(2)}) copy-start(s32[32]{0:T(128)} %picked.1) | copy-start | bytes 388
  5.7 2.5 %copy-start = (bf16[8,32,88,128]{3,2,1,0:T(8,128)(2,1)}, bf16[8,32,88,128]{3,2,1,0:T(8,128)(2,1)S(1)}, u32[]{:S(2)}) copy-start(bf16[8,32,88,128]{3,2,1,0:T(8,128)(2,1)S(1)} %get-tuple-element.7.turned) | copy-start | bytes 17301508
  8.2 16.7 %collective-permute-start = (bf16[32,88,128]{2,1,0:T(8,128)(2,1)S(1)}, bf16[32,88,128]{2,1,0:T(8,128)(2,1)S(1)}, u32[]{:S(2)}, u32[]{:S(2)}) collective-permute-start(bf16[32,88,128]{2,1,0:T(8,128)(2,1)S(1)} %get-tuple-element.8), channel_id=1, source_target_pairs={{0,4},{4,8},{8,12},{12,16},{16,20},{20,24},{24,28},{28,32},{32,36}... | collective-permute-start | bytes 2162696 | tf_op jit(solution)/shard_map/ppermute | solution.py:380
  8.2 16.7 %collective-permute-start.1 = (bf16[32,88,128]{2,1,0:T(8,128)(2,1)S(1)}, bf16[32,88,128]{2,1,0:T(8,128)(2,1)S(1)}, u32[]{:S(2)}, u32[]{:S(2)}) collective-permute-start(bf16[32,88,128]{2,1,0:T(8,128)(2,1)S(1)} %get-tuple-element.9), channel_id=1, source_target_pairs={{4,0},{8,4},{12,8},{16,12},{20,16},{24,20},{28,24},{32,28},{36,32}... | collective-permute-start | bytes 2162696 | tf_op jit(solution)/shard_map/ppermute | solution.py:380
  14.0 10.9 %collective-permute-start.2 = (bf16[8,88,128]{2,1,0:T(8,128)(2,1)}, bf16[8,88,128]{2,1,0:T(8,128)(2,1)S(1)}, u32[]{:S(2)}, u32[]{:S(2)}) collective-permute-start(bf16[8,88,128]{2,1,0:T(8,128)(2,1)} %get-tuple-element.10), channel_id=1, source_target_pairs={{0,1},{1,2},{2,3},{3,0},{4,5},{5,6},{6,7},{7,4},{8,9},{9,10},{10,1... | collective-permute-start | bytes 540680 | tf_op jit(solution)/shard_map/ppermute | solution.py:380
  15.6 9.4 %collective-permute-start.3 = (bf16[8,88,128]{2,1,0:T(8,128)(2,1)S(1)}, bf16[8,88,128]{2,1,0:T(8,128)(2,1)S(1)}, u32[]{:S(2)}, u32[]{:S(2)}) collective-permute-start(bf16[8,88,128]{2,1,0:T(8,128)(2,1)S(1)} %get-tuple-element.11), channel_id=1, source_target_pairs={{1,0},{2,1},{3,2},{0,3},{5,4},{6,5},{7,6},{4,7},{9,8},{10,9},{11,1... | collective-permute-start | bytes 540680 | tf_op jit(solution)/shard_map/ppermute | solution.py:380
  17.3 7.6 %copy-start.1 = (bf16[8,32,88,128]{3,2,1,0:T(8,128)(2,1)S(1)}, bf16[8,32,88,128]{3,2,1,0:T(8,128)(2,1)}, u32[]{:S(2)}) copy-start(bf16[8,32,88,128]{3,2,1,0:T(8,128)(2,1)} %copy-done) | copy-start | bytes 17301508
  17.3 7.7 %copy-start.2 = (s32[8,32,128]{2,1,0:T(8,128)S(1)}, s32[8,32,128]{2,1,0:T(8,128)}, u32[]{:S(2)}) copy-start(s32[8,32,128]{2,1,0:T(8,128)} %material.3) | copy-start | bytes 393220
  37.9 1.3 %collective-permute-start.4 = (f32[88,128]{1,0:T(8,128)S(1)}, f32[88,128]{1,0:T(8,128)S(1)}, u32[]{:S(2)}, u32[]{:S(2)}) collective-permute-start(f32[88,128]{1,0:T(8,128)S(1)} %normal.1), channel_id=1, source_target_pairs={{0,4},{4,0},{8,12},{12,8},{16,20},{20,16},{24,28},{28,24},{32,36},... | collective-permute-start | bytes 135176 | tf_op jit(solution)/shard_map/ppermute | solution.py:350
  39.2 4.1 %collective-permute-start.7 = (f32[88,128]{1,0:T(8,128)S(1)}, f32[88,128]{1,0:T(8,128)S(1)}, u32[]{:S(2)}, u32[]{:S(2)}) collective-permute-start(f32[88,128]{1,0:T(8,128)S(1)} %add.30), channel_id=1, source_target_pairs={{0,96},{4,100},{8,104},{12,108},{16,112},{20,116},{24,120},{28,124... | collective-permute-start | bytes 135176 | tf_op jit(solution)/shard_map/ppermute | solution.py:350
  40.1 5.7 %collective-permute-start.6 = (f32[88,128]{1,0:T(8,128)S(1)}, f32[88,128]{1,0:T(8,128)S(1)}, u32[]{:S(2)}, u32[]{:S(2)}) collective-permute-start(f32[88,128]{1,0:T(8,128)S(1)} %add.30), channel_id=1, source_target_pairs={{0,32},{4,36},{8,40},{12,44},{16,48},{20,52},{24,56},{28,60},{32,6... | collective-permute-start | bytes 135176 | tf_op jit(solution)/shard_map/ppermute | solution.py:350
  41.3 5.6 %collective-permute-start.5 = (f32[88,128]{1,0:T(8,128)S(1)}, f32[88,128]{1,0:T(8,128)S(1)}, u32[]{:S(2)}, u32[]{:S(2)}) collective-permute-start(f32[88,128]{1,0:T(8,128)S(1)} %add.30), channel_id=1, source_target_pairs={{0,64},{4,68},{8,72},{12,76},{16,80},{20,84},{24,88},{28,92},{32,9... | collective-permute-start | bytes 135176 | tf_op jit(solution)/shard_map/ppermute | solution.py:350
  46.8 4.1 %collective-permute-start.10 = (f32[88,128]{1,0:T(8,128)S(1)}, f32[88,128]{1,0:T(8,128)S(1)}, u32[]{:S(2)}, u32[]{:S(2)}) collective-permute-start(f32[88,128]{1,0:T(8,128)S(1)} %add_add_fusion.2), channel_id=1, source_target_pairs={{0,24},{4,28},{8,0},{12,4},{16,8},{20,12},{24,16},{28,20},{32,56},... | collective-permute-start | bytes 135176 | tf_op jit(solution)/shard_map/ppermute | solution.py:350
  48.8 5.3 %collective-permute-start.9 = (f32[88,128]{1,0:T(8,128)S(1)}, f32[88,128]{1,0:T(8,128)S(1)}, u32[]{:S(2)}, u32[]{:S(2)}) collective-permute-start(f32[88,128]{1,0:T(8,128)S(1)} %add_add_fusion.2), channel_id=1, source_target_pairs={{0,8},{4,12},{8,16},{12,20},{16,24},{20,28},{24,0},{28,4},{32,40},... | collective-permute-start | bytes 135176 | tf_op jit(solution)/shard_map/ppermute | solution.py:350
  48.9 5.6 %collective-permute-start.8 = (f32[88,128]{1,0:T(8,128)S(1)}, f32[88,128]{1,0:T(8,128)S(1)}, u32[]{:S(2)}, u32[]{:S(2)}) collective-permute-start(f32[88,128]{1,0:T(8,128)S(1)} %add_add_fusion.2), channel_id=1, source_target_pairs={{0,16},{4,20},{8,24},{12,28},{16,0},{20,4},{24,8},{28,12},{32,48},... | collective-permute-start | bytes 135176 | tf_op jit(solution)/shard_map/ppermute | solution.py:350
  54.6 5.3 %collective-permute-start.13 = (f32[88,128]{1,0:T(8,128)S(1)}, f32[88,128]{1,0:T(8,128)S(1)}, u32[]{:S(2)}, u32[]{:S(2)}) collective-permute-start(f32[88,128]{1,0:T(8,128)S(1)} %add_add_fusion.1), channel_id=1, source_target_pairs={{0,3},{1,0},{2,1},{3,2},{4,7},{5,4},{6,5},{7,6},{8,11},{9,8},{10,9... | collective-permute-start | bytes 135176 | tf_op jit(solution)/shard_map/ppermute | solution.py:350
  57.7 5.7 %collective-permute-start.12 = (f32[88,128]{1,0:T(8,128)S(1)}, f32[88,128]{1,0:T(8,128)S(1)}, u32[]{:S(2)}, u32[]{:S(2)}) collective-permute-start(f32[88,128]{1,0:T(8,128)S(1)} %add_add_fusion.1), channel_id=1, source_target_pairs={{0,1},{1,2},{2,3},{3,0},{4,5},{5,6},{6,7},{7,4},{8,9},{9,10},{10,1... | collective-permute-start | bytes 135176 | tf_op jit(solution)/shard_map/ppermute | solution.py:350
  57.7 5.7 %collective-permute-start.11 = (f32[88,128]{1,0:T(8,128)S(1)}, f32[88,128]{1,0:T(8,128)S(1)}, u32[]{:S(2)}, u32[]{:S(2)}) collective-permute-start(f32[88,128]{1,0:T(8,128)S(1)} %add_add_fusion.1), channel_id=1, source_target_pairs={{0,2},{1,3},{2,0},{3,1},{4,6},{5,7},{6,4},{7,5},{8,10},{9,11},{10,... | collective-permute-start | bytes 135176 | tf_op jit(solution)/shard_map/ppermute | solution.py:350

commit v3 on v2

--- a/solution.py
+++ b/solution.py
@@ -116,7 +116,7 @@
     for z in range(depth):
         loads.append(pltpu.make_async_copy(turned.at[z], field.at[z + 1], sems.at[z + 1]))
     loads.append(pltpu.make_async_copy(z_high, field.at[depth + 1], sems.at[depth + 1]))
-    for copy in [kind_load] + loads:
+    for copy in [kind_load] + loads[:4]:
         copy.start()
     gram[...] = jnp.zeros_like(gram)
     lane = lax.broadcasted_iota(jnp.int32, (columns, width), 1)
@@ -132,6 +132,14 @@
     inside = [edges[i].astype(F32) for i in (2, 3)]
 
     def step(z, _):
+        @pl.when(z + 3 < depth)
+        def _():
+            pltpu.make_async_copy(turned.at[z + 3], field.at[z + 4], sems.at[z + 4]).start()
+
+        @pl.when(z + 3 == depth)
+        def _():
+            loads[depth + 1].start()
+
         @pl.when(z < depth - 1)
         def _():
             pltpu.make_async_copy(turned.at[z + 1], field.at[z + 2], sems.at[z + 2]).wait()
@@ -265,17 +273,10 @@
 
 def update_kernel(
     edges, packed, turned, material, z_low, z_high, y_low, y_high, recycle, images,
-    field, kinds, planes, first_out, second_out, load_sems, kind_sem, store_sems,
+    planes, first_out, second_out, store_sems,
 ):
     depth, height, columns, width = turned.shape
     count = recycle.shape[0]
-    loads = [pltpu.make_async_copy(z_low, field.at[0], load_sems.at[0])]
-    for z in range(depth):
-        loads.append(pltpu.make_async_copy(turned.at[z], field.at[z + 1], load_sems.at[z + 1]))
-    loads.append(pltpu.make_async_copy(z_high, field.at[depth + 1], load_sems.at[depth + 1]))
-    loads.append(pltpu.make_async_copy(material, kinds, kind_sem))
-    for copy in loads:
-        copy.start()
     weights = combination(packed[...], columns, count)
     rounded = weights.astype(BF16)
     both = jnp.concatenate([rounded, (weights - rounded.astype(F32)).astype(BF16)], 0)
@@ -289,19 +290,11 @@
     for z in range(depth):
         planes[z + 1, 0] = low[:, z * width : (z + 1) * width] * edges[2].astype(F32)
         planes[z + 1, height + 1] = high[:, z * width : (z + 1) * width] * edges[3].astype(F32)
-    for copy in loads:
-        copy.wait()
-
-    @pl.when(edges[0] == 0)
-    def _():
-        field[0] = jnp.zeros(field.shape[1:], BF16)
-
-    @pl.when(edges[1] == 0)
-    def _():
-        field[depth + 1] = jnp.zeros(field.shape[1:], BF16)
-
-    def fill(z):
-        plane = combine(jnp.concatenate([field[z, y] for y in range(height)], 1))
+
+    def fill(z, source, keep=None):
+        plane = combine(jnp.concatenate([source[y] for y in range(height)], 1))
+        if keep is not None:
+            plane = plane * keep.astype(F32)
         for y in range(height):
             planes[z, y + 1] = plane[:, y * width : (y + 1) * width]
 
@@ -311,21 +304,25 @@
             pltpu.make_async_copy(second_out.at[slot, :, :height], images.at[:, z], store_sems.at[slot, 1]),
         )
 
-    fill(0)
-    fill(1)
+    fill(0, z_low, edges[0])
+    fill(1, turned.at[0])
+    fill(depth + 1, z_high, edges[1])
     lane = lax.broadcasted_iota(jnp.int32, (count, width), 1)
     first, last = lane == 0, lane == width - 1
 
     def step(z, _):
         slot = lax.rem(z, SLOTS)
-        fill(z + 2)
+
+        @pl.when(z + 1 < depth)
+        def _():
+            fill(z + 2, turned.at[z + 1])
 
         @pl.when(z >= SLOTS)
         def _():
             for copy in stores(z - SLOTS, slot):
                 copy.wait()
 
-        scale = coefficient(kinds[z])
+        scale = coefficient(material[z])
         one = first_out.at[slot].reshape(count * STEP, width)
         two = second_out.at[slot].reshape(count * STEP, width)
         for y in range(height):
@@ -407,7 +404,7 @@
             pltpu.SemaphoreType.DMA((3,)),
             pltpu.SemaphoreType.DMA((count,)),
         ],
-        compiler_params=pltpu.CompilerParams(vmem_limit_bytes=51 * MIB),
+        compiler_params=pltpu.CompilerParams(vmem_limit_bytes=49 * MIB),
         cost_estimate=pl.CostEstimate(flops=2 * 10**9, bytes_accessed=17 * 10**6, transcendentals=0),
         name="gram",
     )(picked, image, basis)
@@ -435,20 +432,16 @@
     grid_shape = (count, depth, height, width)
     return pl.pallas_call(
         update_kernel,
-        in_specs=specs,
+        in_specs=[whole(pltpu.SMEM)] + [whole()] * 7,
         out_specs=[whole(pltpu.HBM), whole(pltpu.HBM)],
         out_shape=[jax.ShapeDtypeStruct(grid_shape, F32)] * 2,
         scratch_shapes=[
-            pltpu.VMEM((depth + 2, height, columns, width), BF16),
-            pltpu.VMEM((depth, height, width), jnp.int32),
             pltpu.VMEM((depth + 2, height + 2, count, width), F32),
             pltpu.VMEM((SLOTS, count, STEP, width), F32),
             pltpu.VMEM((SLOTS, count, STEP, width), F32),
-            pltpu.SemaphoreType.DMA((depth + 2,)),
-            pltpu.SemaphoreType.DMA,
             pltpu.SemaphoreType.DMA((SLOTS, 2)),
         ],
-        compiler_params=pltpu.CompilerParams(vmem_limit_bytes=32 * MIB),
+        compiler_params=pltpu.CompilerParams(vmem_limit_bytes=20 * MIB),
         name="update",
     )(edges, packed, turned, material, *faces)
 

time: 79.5 us -> 76.9 us (0.967)
  Pallas kernels: 41.4 us -> 38.6 us
    pallas_call x1, Pallas kernels: 15.8 us -> 12.9 us  [local(): pl.pallas_call(update_kernel, in_specs=[whole(pltpu.SMEM)] + [whole()] *...]
where the time goes in v3:
time: 76.9 us; the launch traced here: 76.6 us
  Pallas kernels  38.6 us (50%)
  starting transfers between devices  21.1 us (27%)
  waiting for transfers between devices  13.4 us (17%)
  local copies, waits for them, and re-layouts  2.5 us (3%)
  between operations  0.91 us (1%)
    ppermute x10, waiting for transfers between devices, shifted(): return lax.ppermute(value, axis, perm)  13.4 us
    pallas_call x1, Pallas kernels, local(): pl.pallas_call(normal_kernel, in_specs=specs, out_specs=whole(), out_shap...  13 us
    pallas_call x1, Pallas kernels, local(): pl.pallas_call(update_kernel, in_specs=[whole(pltpu.SMEM)] + [whole()] *...  12.9 us
    ppermute x10, starting transfers between devices, shifted(): return lax.ppermute(value, axis, perm)  12.1 us
    pallas_call x1, Pallas kernels, local(): pl.pallas_call(gram_kernel, in_specs=[whole(pltpu.SMEM), whole(pltpu.HBM)...  7.58 us
    ppermute x2, starting transfers between devices, neighbours(): lax.ppermute(low_face, axis, down)  7.41 us
    pallas_call x1, Pallas kernels, local(): pl.pallas_call(turn_kernel, in_specs=[whole(pltpu.HBM)], out_specs=[whole...  5.09 us
    unnamed x8, local copies, waits for them, and re-layouts  2.5 us
  transfers between devices with their start and end apart: 14, of which 8 were waited for; matrix products, arithmetic and copies ran while one was open for 0% of the time, Pallas kernels for 10%

profile of v3, /device:TPU:0, one launch (start us, length us, event | category | flops | bytes accessed | tf_op | source)
XLA Modules:
  0.0 76.6 jit_solution(9481568593046790658)
XLA Ops:
  0.6 0.0 copy-start.3
  0.6 5.1 %turn.1 = (bf16[8,32,88,128]{3,2,1,0:T(8,128)(2,1)S(1)}, bf16[32,88,128]{2,1,0:T(8,128)(2,1)S(1)}, bf16[32,88,128]{2,1,0:T(8,128)(2,1)S(1)}, bf16[8,88,128]{2,1,0:T(8,128)(2,1)S(1)}, bf16[8,88,128]{2,1,0:T(8,128)(2,1)}) custom-call(bf16[88,8,32,128]{3,2,1,0:T(8,128)(2,1)} %basis.3), custom_call_target="tpu_custom_call" | custom-call | tf_op jit(solution)/shard_map/turn/pallas_call | solution.py:381
  5.7 0.0 copy-start
  5.7 2.5 %copy-done = bf16[8,32,88,128]{3,2,1,0:T(8,128)(2,1)} copy-done((bf16[8,32,88,128]{3,2,1,0:T(8,128)(2,1)}, bf16[8,32,88,128]{3,2,1,0:T(8,128)(2,1)S(1)}, u32[]{:S(2)}) %copy-start) | copy-done | bytes 5767192
  8.2 0.0 collective-permute-start
  8.2 5.8 %collective-permute-start.1 = (bf16[32,88,128]{2,1,0:T(8,128)(2,1)S(1)}, bf16[32,88,128]{2,1,0:T(8,128)(2,1)S(1)}, u32[]{:S(2)}, u32[]{:S(2)}) collective-permute-start(bf16[32,88,128]{2,1,0:T(8,128)(2,1)S(1)} %get-tuple-element.9), channel_id=1, source_target_pairs={{4,0},{8,4},{12,8},{16,12},{20,16},{24,20},{28,24},{32,28},{36,32}... | collective-permute-start | bytes 2162696 | tf_op jit(solution)/shard_map/ppermute | solution.py:377
  14.0 1.6 %collective-permute-start.2 = (bf16[8,88,128]{2,1,0:T(8,128)(2,1)}, bf16[8,88,128]{2,1,0:T(8,128)(2,1)S(1)}, u32[]{:S(2)}, u32[]{:S(2)}) collective-permute-start(bf16[8,88,128]{2,1,0:T(8,128)(2,1)} %get-tuple-element.10), channel_id=1, source_target_pairs={{0,1},{1,2},{2,3},{3,0},{4,5},{5,6},{6,7},{7,4},{8,9},{9,10},{10,1... | collective-permute-start | bytes 540680 | tf_op jit(solution)/shard_map/ppermute | solution.py:377
  15.6 1.7 %collective-permute-start.3 = (bf16[8,88,128]{2,1,0:T(8,128)(2,1)S(1)}, bf16[8,88,128]{2,1,0:T(8,128)(2,1)S(1)}, u32[]{:S(2)}, u32[]{:S(2)}) collective-permute-start(bf16[8,88,128]{2,1,0:T(8,128)(2,1)S(1)} %get-tuple-element.11), channel_id=1, source_target_pairs={{1,0},{2,1},{3,2},{0,3},{5,4},{6,5},{7,6},{4,7},{9,8},{10,9},{11,1... | collective-permute-start | bytes 540680 | tf_op jit(solution)/shard_map/ppermute | solution.py:377
  17.2 0.1 add_convert_fusion.edges
  17.3 0.0 copy-done.3
  17.3 0.0 copy-start.1
  17.3 0.0 copy-start.2
  17.3 7.6 %gram.1.sums = f32[120,88]{1,0:T(8,128)S(1)} custom-call(s32[32]{0:T(128)S(1)} %copy-done.3, bf16[88,8,32,128]{3,2,1,0:T(8,128)(2,1)} %image.1, bf16[88,8,32,128]{3,2,1,0:T(8,128)(2,1)} %basis.3), custom_call_target="tpu_custom_call" | custom-call | flops 2000000000 | bytes 17000000 | tf_op jit(solution)/shard_map/gram/pallas_call | solution.py:395
  24.9 0.0 collective-permute-done.2.y_low
  24.9 0.0 collective-permute-done.3.y_high
  24.9 0.0 collective-permute-done.z_low
  24.9 0.0 collective-permute-done.1.z_high
  24.9 0.0 copy-done.1
  25.0 0.0 copy-done.2
  25.0 13.0 %normal.1 = f32[88,128]{1,0:T(8,128)S(1)} custom-call(s32[4]{0:T(128)S(1)} %add_convert_fusion.edges, f32[120,88]{1,0:T(8,128)S(1)} %gram.1.sums, bf16[8,32,88,128]{3,2,1,0:T(8,128)(2,1)S(1)} %copy-done.1, s32[8,32,128]{2,1,0:T(8,128)S(1)} %copy-done.2, bf16[32,88,128]{2,1,0:T(8,128)(2,1)S(1)} %collective-permute-done.z_low, ...), custom_call_target="tpu_custom_call" | custom-call | tf_op jit(solution)/shard_map/normal/pallas_call | solution.py:416
  37.9 0.1 collective-permute-start.4
  38.0 1.2 %collective-permute-done.4 = f32[88,128]{1,0:T(8,128)S(1)} collective-permute-done((f32[88,128]{1,0:T(8,128)S(1)}, f32[88,128]{1,0:T(8,128)S(1)}, u32[]{:S(2)}, u32[]{:S(2)}) %collective-permute-start.4) | collective-permute-done | bytes 45088 | tf_op jit(solution)/shard_map/ppermute | solution.py:347
  39.3 0.9 %collective-permute-start.7 = (f32[88,128]{1,0:T(8,128)S(1)}, f32[88,128]{1,0:T(8,128)S(1)}, u32[]{:S(2)}, u32[]{:S(2)}) collective-permute-start(f32[88,128]{1,0:T(8,128)S(1)} %add.30), channel_id=1, source_target_pairs={{0,96},{4,100},{8,104},{12,108},{16,112},{20,116},{24,120},{28,124... | collective-permute-start | bytes 135176 | tf_op jit(solution)/shard_map/ppermute | solution.py:347
  40.2 1.2 %collective-permute-start.6 = (f32[88,128]{1,0:T(8,128)S(1)}, f32[88,128]{1,0:T(8,128)S(1)}, u32[]{:S(2)}, u32[]{:S(2)}) collective-permute-start(f32[88,128]{1,0:T(8,128)S(1)} %add.30), channel_id=1, source_target_pairs={{0,32},{4,36},{8,40},{12,44},{16,48},{20,52},{24,56},{28,60},{32,6... | collective-permute-start | bytes 135176 | tf_op jit(solution)/shard_map/ppermute | solution.py:347
  41.3 1.1 %collective-permute-start.5 = (f32[88,128]{1,0:T(8,128)S(1)}, f32[88,128]{1,0:T(8,128)S(1)}, u32[]{:S(2)}, u32[]{:S(2)}) collective-permute-start(f32[88,128]{1,0:T(8,128)S(1)} %add.30), channel_id=1, source_target_pairs={{0,64},{4,68},{8,72},{12,76},{16,80},{20,84},{24,88},{28,92},{32,9... | collective-permute-start | bytes 135176 | tf_op jit(solution)/shard_map/ppermute | solution.py:347
  42.5 0.9 %collective-permute-done.7 = f32[88,128]{1,0:T(8,128)S(1)} collective-permute-done((f32[88,128]{1,0:T(8,128)S(1)}, f32[88,128]{1,0:T(8,128)S(1)}, u32[]{:S(2)}, u32[]{:S(2)}) %collective-permute-start.7) | collective-permute-done | bytes 45088 | tf_op jit(solution)/shard_map/ppermute | solution.py:347
  43.4 2.5 %collective-permute-done.6 = f32[88,128]{1,0:T(8,128)S(1)} collective-permute-done((f32[88,128]{1,0:T(8,128)S(1)}, f32[88,128]{1,0:T(8,128)S(1)}, u32[]{:S(2)}, u32[]{:S(2)}) %collective-permute-start.6) | collective-permute-done | bytes 45088 | tf_op jit(solution)/shard_map/ppermute | solution.py:347
  45.9 1.0 %collective-permute-done.5 = f32[88,128]{1,0:T(8,128)S(1)} collective-permute-done((f32[88,128]{1,0:T(8,128)S(1)}, f32[88,128]{1,0:T(8,128)S(1)}, u32[]{:S(2)}, u32[]{:S(2)}) %collective-permute-start.5) | collective-permute-done | bytes 45088 | tf_op jit(solution)/shard_map/ppermute | solution.py:347
  46.9 2.0 %collective-permute-start.10 = (f32[88,128]{1,0:T(8,128)S(1)}, f32[88,128]{1,0:T(8,128)S(1)}, u32[]{:S(2)}, u32[]{:S(2)}) collective-permute-start(f32[88,128]{1,0:T(8,128)S(1)} %add_add_fusion.2), channel_id=1, source_target_pairs={{0,24},{4,28},{8,0},{12,4},{16,8},{20,12},{24,16},{28,20},{32,56},... | collective-permute-start | bytes 135176 | tf_op jit(solution)/shard_map/ppermute | solution.py:347
  48.9 0.1 collective-permute-start.9
  49.0 1.4 %collective-permute-start.8 = (f32[88,128]{1,0:T(8,128)S(1)}, f32[88,128]{1,0:T(8,128)S(1)}, u32[]{:S(2)}, u32[]{:S(2)}) collective-permute-start(f32[88,128]{1,0:T(8,128)S(1)} %add_add_fusion.2), channel_id=1, source_target_pairs={{0,16},{4,20},{8,24},{12,28},{16,0},{20,4},{24,8},{28,12},{32,48},... | collective-permute-start | bytes 135176 | tf_op jit(solution)/shard_map/ppermute | solution.py:347
  50.4 0.6 collective-permute-done.10
  51.0 3.1 %collective-permute-done.9 = f32[88,128]{1,0:T(8,128)S(1)} collective-permute-done((f32[88,128]{1,0:T(8,128)S(1)}, f32[88,128]{1,0:T(8,128)S(1)}, u32[]{:S(2)}, u32[]{:S(2)}) %collective-permute-start.9) | collective-permute-done | bytes 45088 | tf_op jit(solution)/shard_map/ppermute | solution.py:347
  54.2 0.5 collective-permute-done.8
  54.7 3.1 %collective-permute-start.13 = (f32[88,128]{1,0:T(8,128)S(1)}, f32[88,128]{1,0:T(8,128)S(1)}, u32[]{:S(2)}, u32[]{:S(2)}) collective-permute-start(f32[88,128]{1,0:T(8,128)S(1)} %add_add_fusion.1), channel_id=1, source_target_pairs={{0,3},{1,0},{2,1},{3,2},{4,7},{5,4},{6,5},{7,6},{8,11},{9,8},{10,9... | collective-permute-start | bytes 135176 | tf_op jit(solution)/shard_map/ppermute | solution.py:347
  57.7 0.0 collective-permute-start.12
  57.7 2.2 %collective-permute-start.11 = (f32[88,128]{1,0:T(8,128)S(1)}, f32[88,128]{1,0:T(8,128)S(1)}, u32[]{:S(2)}, u32[]{:S(2)}) collective-permute-start(f32[88,128]{1,0:T(8,128)S(1)} %add_add_fusion.1), channel_id=1, source_target_pairs={{0,2},{1,3},{2,0},{3,1},{4,6},{5,7},{6,4},{7,5},{8,10},{9,11},{10,... | collective-permute-start | bytes 135176 | tf_op jit(solution)/shard_map/ppermute | solution.py:347
  60.0 0.0 collective-permute-done.13
  60.0 3.5 %collective-permute-done.12 = f32[88,128]{1,0:T(8,128)S(1)} collective-permute-done((f32[88,128]{1,0:T(8,128)S(1)}, f32[88,128]{1,0:T(8,128)S(1)}, u32[]{:S(2)}, u32[]{:S(2)}) %collective-permute-start.12) | collective-permute-done | bytes 45088 | tf_op jit(solution)/shard_map/ppermute | solution.py:347
  63.5 0.0 collective-permute-done.11
  63.5 12.9 %update.1 = (f32[32,8,32,128]{3,2,1,0:T(8,128)}, f32[32,8,32,128]{3,2,1,0:T(8,128)}) custom-call(s32[4]{0:T(128)S(1)} %add_convert_fusion.edges, f32[88,128]{1,0:T(8,128)S(1)} %add_add_fusion.packed, bf16[8,32,88,128]{3,2,1,0:T(8,128)(2,1)S(1)} %copy-done.1, s32[8,32,128]{2,1,0:T(8,128)S(1)} %copy-done.2, ...), custom_call_target="tpu_custom_call" | custom-call | tf_op jit(solution)/shard_map/update/pallas_call | solution.py:433
  (4 shorter events, 0.1 us)
Async XLA Ops:
  0.6 16.7 %copy-start.3 = (s32[32]{0:T(128)S(1)}, s32[32]{0:T(128)}, u32[]{:S(2)}) copy-start(s32[32]{0:T(128)} %picked.1) | copy-start | bytes 388
  5.7 2.5 %copy-start = (bf16[8,32,88,128]{3,2,1,0:T(8,128)(2,1)}, bf16[8,32,88,128]{3,2,1,0:T(8,128)(2,1)S(1)}, u32[]{:S(2)}) copy-start(bf16[8,32,88,128]{3,2,1,0:T(8,128)(2,1)S(1)} %get-tuple-element.7.turned) | copy-start | bytes 17301508
  8.2 16.7 %collective-permute-start = (bf16[32,88,128]{2,1,0:T(8,128)(2,1)S(1)}, bf16[32,88,128]{2,1,0:T(8,128)(2,1)S(1)}, u32[]{:S(2)}, u32[]{:S(2)}) collective-permute-start(bf16[32,88,128]{2,1,0:T(8,128)(2,1)S(1)} %get-tuple-element.8), channel_id=1, source_target_pairs={{0,4},{4,8},{8,12},{12,16},{16,20},{20,24},{24,28},{28,32},{32,36}... | collective-permute-start | bytes 2162696 | tf_op jit(solution)/shard_map/ppermute | solution.py:377
  8.2 16.7 %collective-permute-start.1 = (bf16[32,88,128]{2,1,0:T(8,128)(2,1)S(1)}, bf16[32,88,128]{2,1,0:T(8,128)(2,1)S(1)}, u32[]{:S(2)}, u32[]{:S(2)}) collective-permute-start(bf16[32,88,128]{2,1,0:T(8,128)(2,1)S(1)} %get-tuple-element.9), channel_id=1, source_target_pairs={{4,0},{8,4},{12,8},{16,12},{20,16},{24,20},{28,24},{32,28},{36,32}... | collective-permute-start | bytes 2162696 | tf_op jit(solution)/shard_map/ppermute | solution.py:377
  14.0 10.9 %collective-permute-start.2 = (bf16[8,88,128]{2,1,0:T(8,128)(2,1)}, bf16[8,88,128]{2,1,0:T(8,128)(2,1)S(1)}, u32[]{:S(2)}, u32[]{:S(2)}) collective-permute-start(bf16[8,88,128]{2,1,0:T(8,128)(2,1)} %get-tuple-element.10), channel_id=1, source_target_pairs={{0,1},{1,2},{2,3},{3,0},{4,5},{5,6},{6,7},{7,4},{8,9},{9,10},{10,1... | collective-permute-start | bytes 540680 | tf_op jit(solution)/shard_map/ppermute | solution.py:377
  15.6 9.3 %collective-permute-start.3 = (bf16[8,88,128]{2,1,0:T(8,128)(2,1)S(1)}, bf16[8,88,128]{2,1,0:T(8,128)(2,1)S(1)}, u32[]{:S(2)}, u32[]{:S(2)}) collective-permute-start(bf16[8,88,128]{2,1,0:T(8,128)(2,1)S(1)} %get-tuple-element.11), channel_id=1, source_target_pairs={{1,0},{2,1},{3,2},{0,3},{5,4},{6,5},{7,6},{4,7},{9,8},{10,9},{11,1... | collective-permute-start | bytes 540680 | tf_op jit(solution)/shard_map/ppermute | solution.py:377
  17.3 7.6 %copy-start.1 = (bf16[8,32,88,128]{3,2,1,0:T(8,128)(2,1)S(1)}, bf16[8,32,88,128]{3,2,1,0:T(8,128)(2,1)}, u32[]{:S(2)}) copy-start(bf16[8,32,88,128]{3,2,1,0:T(8,128)(2,1)} %copy-done) | copy-start | bytes 17301508
  17.3 7.6 %copy-start.2 = (s32[8,32,128]{2,1,0:T(8,128)S(1)}, s32[8,32,128]{2,1,0:T(8,128)}, u32[]{:S(2)}) copy-start(s32[8,32,128]{2,1,0:T(8,128)} %material.3) | copy-start | bytes 393220
  37.9 1.3 %collective-permute-start.4 = (f32[88,128]{1,0:T(8,128)S(1)}, f32[88,128]{1,0:T(8,128)S(1)}, u32[]{:S(2)}, u32[]{:S(2)}) collective-permute-start(f32[88,128]{1,0:T(8,128)S(1)} %normal.1), channel_id=1, source_target_pairs={{0,4},{4,0},{8,12},{12,8},{16,20},{20,16},{24,28},{28,24},{32,36},... | collective-permute-start | bytes 135176 | tf_op jit(solution)/shard_map/ppermute | solution.py:347
  39.3 4.1 %collective-permute-start.7 = (f32[88,128]{1,0:T(8,128)S(1)}, f32[88,128]{1,0:T(8,128)S(1)}, u32[]{:S(2)}, u32[]{:S(2)}) collective-permute-start(f32[88,128]{1,0:T(8,128)S(1)} %add.30), channel_id=1, source_target_pairs={{0,96},{4,100},{8,104},{12,108},{16,112},{20,116},{24,120},{28,124... | collective-permute-start | bytes 135176 | tf_op jit(solution)/shard_map/ppermute | solution.py:347
  40.2 5.7 %collective-permute-start.6 = (f32[88,128]{1,0:T(8,128)S(1)}, f32[88,128]{1,0:T(8,128)S(1)}, u32[]{:S(2)}, u32[]{:S(2)}) collective-permute-start(f32[88,128]{1,0:T(8,128)S(1)} %add.30), channel_id=1, source_target_pairs={{0,32},{4,36},{8,40},{12,44},{16,48},{20,52},{24,56},{28,60},{32,6... | collective-permute-start | bytes 135176 | tf_op jit(solution)/shard_map/ppermute | solution.py:347
  41.3 5.6 %collective-permute-start.5 = (f32[88,128]{1,0:T(8,128)S(1)}, f32[88,128]{1,0:T(8,128)S(1)}, u32[]{:S(2)}, u32[]{:S(2)}) collective-permute-start(f32[88,128]{1,0:T(8,128)S(1)} %add.30), channel_id=1, source_target_pairs={{0,64},{4,68},{8,72},{12,76},{16,80},{20,84},{24,88},{28,92},{32,9... | collective-permute-start | bytes 135176 | tf_op jit(solution)/shard_map/ppermute | solution.py:347
  46.9 4.1 %collective-permute-start.10 = (f32[88,128]{1,0:T(8,128)S(1)}, f32[88,128]{1,0:T(8,128)S(1)}, u32[]{:S(2)}, u32[]{:S(2)}) collective-permute-start(f32[88,128]{1,0:T(8,128)S(1)} %add_add_fusion.2), channel_id=1, source_target_pairs={{0,24},{4,28},{8,0},{12,4},{16,8},{20,12},{24,16},{28,20},{32,56},... | collective-permute-start | bytes 135176 | tf_op jit(solution)/shard_map/ppermute | solution.py:347
  48.9 5.3 %collective-permute-start.9 = (f32[88,128]{1,0:T(8,128)S(1)}, f32[88,128]{1,0:T(8,128)S(1)}, u32[]{:S(2)}, u32[]{:S(2)}) collective-permute-start(f32[88,128]{1,0:T(8,128)S(1)} %add_add_fusion.2), channel_id=1, source_target_pairs={{0,8},{4,12},{8,16},{12,20},{16,24},{20,28},{24,0},{28,4},{32,40},... | collective-permute-start | bytes 135176 | tf_op jit(solution)/shard_map/ppermute | solution.py:347
  49.0 5.6 %collective-permute-start.8 = (f32[88,128]{1,0:T(8,128)S(1)}, f32[88,128]{1,0:T(8,128)S(1)}, u32[]{:S(2)}, u32[]{:S(2)}) collective-permute-start(f32[88,128]{1,0:T(8,128)S(1)} %add_add_fusion.2), channel_id=1, source_target_pairs={{0,16},{4,20},{8,24},{12,28},{16,0},{20,4},{24,8},{28,12},{32,48},... | collective-permute-start | bytes 135176 | tf_op jit(solution)/shard_map/ppermute | solution.py:347
  54.7 5.3 %collective-permute-start.13 = (f32[88,128]{1,0:T(8,128)S(1)}, f32[88,128]{1,0:T(8,128)S(1)}, u32[]{:S(2)}, u32[]{:S(2)}) collective-permute-start(f32[88,128]{1,0:T(8,128)S(1)} %add_add_fusion.1), channel_id=1, source_target_pairs={{0,3},{1,0},{2,1},{3,2},{4,7},{5,4},{6,5},{7,6},{8,11},{9,8},{10,9... | collective-permute-start | bytes 135176 | tf_op jit(solution)/shard_map/ppermute | solution.py:347
  57.7 5.7 %collective-permute-start.12 = (f32[88,128]{1,0:T(8,128)S(1)}, f32[88,128]{1,0:T(8,128)S(1)}, u32[]{:S(2)}, u32[]{:S(2)}) collective-permute-start(f32[88,128]{1,0:T(8,128)S(1)} %add_add_fusion.1), channel_id=1, source_target_pairs={{0,1},{1,2},{2,3},{3,0},{4,5},{5,6},{6,7},{7,4},{8,9},{9,10},{10,1... | collective-permute-start | bytes 135176 | tf_op jit(solution)/shard_map/ppermute | solution.py:347
  57.7 5.7 %collective-permute-start.11 = (f32[88,128]{1,0:T(8,128)S(1)}, f32[88,128]{1,0:T(8,128)S(1)}, u32[]{:S(2)}, u32[]{:S(2)}) collective-permute-start(f32[88,128]{1,0:T(8,128)S(1)} %add_add_fusion.1), channel_id=1, source_target_pairs={{0,2},{1,3},{2,0},{3,1},{4,6},{5,7},{6,4},{7,5},{8,10},{9,11},{10,... | collective-permute-start | bytes 135176 | tf_op jit(solution)/shard_map/ppermute | solution.py:347

commit v4 on v3

--- a/solution.py
+++ b/solution.py
@@ -16,13 +16,16 @@
 MIB = 2**20
 
 
-def turn_kernel(basis, turned, z_first, z_last, y_first, y_last, slab, sems):
+def turn_kernel(basis, turned, z_first, z_last, y_first, y_last, slab, moved, sems, out_sems):
     columns, depth, height, width = basis.shape
     slots = slab.shape[0]
 
     def load(z, slot):
         return pltpu.make_async_copy(basis.at[:, z], slab.at[slot], sems.at[slot])
 
+    def store(z, slot):
+        return pltpu.make_async_copy(moved.at[slot], turned.at[z], out_sems.at[slot])
+
     for z in range(slots - 1):
         load(z, z).start()
 
@@ -32,20 +35,31 @@
         @pl.when(z + slots - 1 < depth)
         def _():
             load(z + slots - 1, lax.rem(z + slots - 1, slots)).start()
+
+        @pl.when(z >= slots)
+        def _():
+            store(z - slots, slot).wait()
 
         load(z, slot).wait()
         for y in range(0, height, 16):
             part = jnp.swapaxes(slab[slot, :, y : y + 16, :], 0, 1)
-            turned[z, y : y + 16] = part
+            moved[slot, y : y + 16] = part
             if y == 0:
                 y_first[z] = part[0]
             if y + 16 == height:
                 y_last[z] = part[15]
+        store(z, slot).start()
+
+        @pl.when(z == 0)
+        def _():
+            z_first[...] = moved[0]
+
         return 0
 
     lax.fori_loop(0, depth, step, 0)
-    z_first[...] = turned[0]
-    z_last[...] = turned[depth - 1]
+    z_last[...] = moved[(depth - 1) % slots]
+    for z in range(depth - slots, depth):
+        store(z, z % slots).wait()
 
 
 def gram_kernel(picked, image, basis, sums, image_slab, picked_slab, rows, sems, picked_sems):
@@ -106,77 +120,51 @@
 
 
 def normal_kernel(
-    edges, sums, turned, material, z_low, z_high, y_low, y_high,
-    packed, field, kinds, gram, sems, kind_sem,
+    edges, sums, turned, material, z_low, z_high, y_low, y_high, packed, gram
 ):
     depth, height, columns, width = turned.shape
     count = sums.shape[0] - columns
-    kind_load = pltpu.make_async_copy(material, kinds, kind_sem)
-    loads = [pltpu.make_async_copy(z_low, field.at[0], sems.at[0])]
-    for z in range(depth):
-        loads.append(pltpu.make_async_copy(turned.at[z], field.at[z + 1], sems.at[z + 1]))
-    loads.append(pltpu.make_async_copy(z_high, field.at[depth + 1], sems.at[depth + 1]))
-    for copy in [kind_load] + loads[:4]:
-        copy.start()
     gram[...] = jnp.zeros_like(gram)
     lane = lax.broadcasted_iota(jnp.int32, (columns, width), 1)
     first, last = lane == 0, lane == width - 1
-    kind_load.wait()
-    loads[0].wait()
-    loads[1].wait()
-
-    @pl.when(edges[0] == 0)
-    def _():
-        field[0] = jnp.zeros(field.shape[1:], BF16)
-
-    inside = [edges[i].astype(F32) for i in (2, 3)]
-
-    def step(z, _):
-        @pl.when(z + 3 < depth)
-        def _():
-            pltpu.make_async_copy(turned.at[z + 3], field.at[z + 4], sems.at[z + 4]).start()
-
-        @pl.when(z + 3 == depth)
-        def _():
-            loads[depth + 1].start()
-
-        @pl.when(z < depth - 1)
-        def _():
-            pltpu.make_async_copy(turned.at[z + 1], field.at[z + 2], sems.at[z + 2]).wait()
-
-        @pl.when(z == depth - 1)
-        def _():
-            loads[depth + 1].wait()
-
-            @pl.when(edges[1] == 0)
-            def _():
-                field[depth + 1] = jnp.zeros(field.shape[1:], BF16)
-
-        scale = coefficient(kinds[z])
-        middle = [y_low[z].astype(F32) * inside[0], field[z + 1, 0].astype(F32)]
+    inside = [edges[i].astype(F32) for i in range(4)]
+    gap = jnp.zeros((16 - columns % 16, height * width), BF16)
+
+    def plane(z, below, here, above, keep_below=None, keep_above=None):
+        scale = coefficient(material[z])
+        middle = [y_low[z].astype(F32) * inside[2], here[0].astype(F32)]
         highs, lows = [], []
         for y in range(height):
             if y == height - 1:
-                middle.append(y_high[z].astype(F32) * inside[1])
+                middle.append(y_high[z].astype(F32) * inside[3])
             else:
-                middle.append(field[z + 1, y + 1].astype(F32))
+                middle.append(here[y + 1].astype(F32))
             row = middle[y + 1]
-            beside = field[z, y].astype(F32) + field[z + 2, y].astype(F32)
-            beside = beside + (middle[y] + middle[y + 2])
+            under, over = below[y].astype(F32), above[y].astype(F32)
+            if keep_below is not None:
+                under = under * keep_below
+            if keep_above is not None:
+                over = over * keep_above
+            beside = under + over + (middle[y] + middle[y + 2])
             beside = beside + beside_in_row(row, first, last)
             image = scale[y : y + 1, :] * row - beside
             rounded = image.astype(BF16)
             highs.append(rounded)
             lows.append((image - rounded.astype(F32)).astype(BF16))
         rounded = jnp.concatenate(highs, 1)
-        gap = jnp.zeros((16 - columns % 16, height * width), BF16)
         both = jnp.concatenate([rounded, gap, jnp.concatenate(lows, 1)], 0)
         part = lax.dot_general(both, rounded, NT, preferred_element_type=F32)
         gram[:columns] += part[:columns]
         gram[columns:] += part[both.shape[0] - columns :]
+
+    def step(z, _):
+        plane(z, turned.at[z - 1], turned.at[z], turned.at[z + 1])
         return 0
 
-    lax.fori_loop(0, depth, step, 0)
+    lax.fori_loop(1, depth - 1, step, 0)
+    plane(0, z_low, turned.at[0], turned.at[1], keep_below=inside[0])
+    end = depth - 1
+    plane(end, turned.at[end - 1], turned.at[end], z_high, keep_above=inside[1])
     side = jnp.zeros((columns, 128 - columns), F32)
     foot = jnp.zeros((128 - columns, 128), F32)
     cross = jnp.concatenate([gram[columns:], side], 1)
@@ -306,7 +294,6 @@
 
     fill(0, z_low, edges[0])
     fill(1, turned.at[0])
-    fill(depth + 1, z_high, edges[1])
     lane = lax.broadcasted_iota(jnp.int32, (count, width), 1)
     first, last = lane == 0, lane == width - 1
 
@@ -316,6 +303,10 @@
         @pl.when(z + 1 < depth)
         def _():
             fill(z + 2, turned.at[z + 1])
+
+        @pl.when(z + 1 == depth)
+        def _():
+            fill(z + 2, z_high, edges[1])
 
         @pl.when(z >= SLOTS)
         def _():
@@ -381,13 +372,15 @@
     turned, z_first, z_last, y_first, y_last = pl.pallas_call(
         turn_kernel,
         in_specs=[whole(pltpu.HBM)],
-        out_specs=[whole()] * 5,
+        out_specs=[whole(pltpu.HBM)] + [whole()] * 4,
         out_shape=[jax.ShapeDtypeStruct((depth, height, columns, width), BF16), face, face, edge, edge],
         scratch_shapes=[
             pltpu.VMEM((3, columns, height, width), BF16),
+            pltpu.VMEM((3, height, columns, width), BF16),
+            pltpu.SemaphoreType.DMA((3,)),
             pltpu.SemaphoreType.DMA((3,)),
         ],
-        compiler_params=pltpu.CompilerParams(vmem_limit_bytes=46 * MIB),
+        compiler_params=pltpu.CompilerParams(vmem_limit_bytes=57 * MIB),
         name="turn",
     )(basis)
     z_low, z_high = neighbours(z_first, z_last, "slab", slabs)
@@ -412,20 +405,13 @@
     slab, pencil = lax.axis_index("slab"), lax.axis_index("pencil")
     inner = (slab > 0, slab < slabs - 1, pencil > 0, pencil < pencils - 1)
     edges = jnp.stack(inner).astype(jnp.int32)
-    specs = [whole(pltpu.SMEM), whole(), whole(pl.ANY), whole(pltpu.HBM), whole(pl.ANY), whole(pl.ANY), whole(), whole()]
     packed = pl.pallas_call(
         normal_kernel,
-        in_specs=specs,
+        in_specs=[whole(pltpu.SMEM)] + [whole()] * 7,
         out_specs=whole(),
         out_shape=jax.ShapeDtypeStruct((columns, 128), F32),
-        scratch_shapes=[
-            pltpu.VMEM((depth + 2, height, columns, width), BF16),
-            pltpu.VMEM((depth, height, width), jnp.int32),
-            pltpu.VMEM((2 * columns, columns), F32),
-            pltpu.SemaphoreType.DMA((depth + 2,)),
-            pltpu.SemaphoreType.DMA,
-        ],
-        compiler_params=pltpu.CompilerParams(vmem_limit_bytes=24 * MIB),
+        scratch_shapes=[pltpu.VMEM((2 * columns, columns), F32)],
+        compiler_params=pltpu.CompilerParams(vmem_limit_bytes=16 * MIB),
         name="normal",
     )(edges, sums, turned, material, *faces)
     packed = device_sum(packed)

time: 76.9 us -> 73.8 us (0.960)
  local copies, waits for them, and re-layouts: 2.5 us -> 0.01 us
  Pallas kernels: 38.6 us -> 37.6 us
    pallas_call x1, Pallas kernels: 13 us -> 9.49 us  [local(): pl.pallas_call(normal_kernel, in_specs=[whole(pltpu.SMEM)] + [whole()] *...]
    pallas_call x1, Pallas kernels: 5.09 us -> 7.84 us  [local(): pl.pallas_call(turn_kernel, in_specs=[whole(pltpu.HBM)], out_specs=[whole...]
    unnamed x8 -> x6, local copies, waits for them, and re-layouts: 2.5 us -> 0.01 us
  transfers between devices with their start and end apart: 14 -> 14, of which waited for: 8 -> 7; matrix products, arithmetic and copies ran while one was open for 0% -> 0% of each run, Pallas kernels for 10% -> 10%
where the time goes in v4:
time: 73.8 us; the launch traced here: 73.4 us
  Pallas kernels  37.6 us (51%)
  starting transfers between devices  21.5 us (29%)
  waiting for transfers between devices  13.4 us (18%)
  between operations  0.9 us (1%)
    ppermute x10, waiting for transfers between devices, shifted(): return lax.ppermute(value, axis, perm)  13.4 us
    pallas_call x1, Pallas kernels, local(): pl.pallas_call(update_kernel, in_specs=[whole(pltpu.SMEM)] + [whole()] *...  12.6 us
    ppermute x10, starting transfers between devices, shifted(): return lax.ppermute(value, axis, perm)  12.3 us
    pallas_call x1, Pallas kernels, local(): pl.pallas_call(normal_kernel, in_specs=[whole(pltpu.SMEM)] + [whole()] *...  9.49 us
    pallas_call x1, Pallas kernels, local(): pl.pallas_call(turn_kernel, in_specs=[whole(pltpu.HBM)], out_specs=[whole...  7.84 us
    pallas_call x1, Pallas kernels, local(): pl.pallas_call(gram_kernel, in_specs=[whole(pltpu.SMEM), whole(pltpu.HBM)...  7.58 us
    ppermute x2, starting transfers between devices, neighbours(): lax.ppermute(low_face, axis, down)  7.48 us
    ppermute x2, starting transfers between devices, neighbours(): lax.ppermute(high_face, axis, up)  1.65 us
  transfers between devices with their start and end apart: 14, of which 7 were waited for; matrix products, arithmetic and copies ran while one was open for 0% of the time, Pallas kernels for 10%

profile of v4, /device:TPU:0, one launch (start us, length us, event | category | flops | bytes accessed | tf_op | source)
XLA Modules:
  0.0 73.4 jit_solution(17844466893509725246)
XLA Ops:
  0.6 0.0 copy-start.2
  0.6 7.8 %turn.1 = (bf16[8,32,88,128]{3,2,1,0:T(8,128)(2,1)}, bf16[32,88,128]{2,1,0:T(8,128)(2,1)}, bf16[32,88,128]{2,1,0:T(8,128)(2,1)}, bf16[8,88,128]{2,1,0:T(8,128)(2,1)}, bf16[8,88,128]{2,1,0:T(8,128)(2,1)}) custom-call(bf16[88,8,32,128]{3,2,1,0:T(8,128)(2,1)} %basis.3), custom_call_target="tpu_custom_call" | custom-call | tf_op jit(solution)/shard_map/turn/pallas_call | solution.py:372
  8.5 0.1 collective-permute-start
  8.6 5.8 %collective-permute-start.1 = (bf16[32,88,128]{2,1,0:T(8,128)(2,1)}, bf16[32,88,128]{2,1,0:T(8,128)(2,1)S(1)}, u32[]{:S(2)}, u32[]{:S(2)}) collective-permute-start(bf16[32,88,128]{2,1,0:T(8,128)(2,1)} %get-tuple-element.9), channel_id=1, source_target_pairs={{4,0},{8,4},{12,8},{16,12},{20,16},{24,20},{28,24},{32,28},{36,32}... | collective-permute-start | bytes 2162696 | tf_op jit(solution)/shard_map/ppermute | solution.py:368
  14.4 1.6 %collective-permute-start.2 = (bf16[8,88,128]{2,1,0:T(8,128)(2,1)}, bf16[8,88,128]{2,1,0:T(8,128)(2,1)S(1)}, u32[]{:S(2)}, u32[]{:S(2)}) collective-permute-start(bf16[8,88,128]{2,1,0:T(8,128)(2,1)} %get-tuple-element.10), channel_id=1, source_target_pairs={{0,1},{1,2},{2,3},{3,0},{4,5},{5,6},{6,7},{7,4},{8,9},{9,10},{10,1... | collective-permute-start | bytes 540680 | tf_op jit(solution)/shard_map/ppermute | solution.py:368
  16.0 1.7 %collective-permute-start.3 = (bf16[8,88,128]{2,1,0:T(8,128)(2,1)}, bf16[8,88,128]{2,1,0:T(8,128)(2,1)S(1)}, u32[]{:S(2)}, u32[]{:S(2)}) collective-permute-start(bf16[8,88,128]{2,1,0:T(8,128)(2,1)} %get-tuple-element.11), channel_id=1, source_target_pairs={{1,0},{2,1},{3,2},{0,3},{5,4},{6,5},{7,6},{4,7},{9,8},{10,9},{11,1... | collective-permute-start | bytes 540680 | tf_op jit(solution)/shard_map/ppermute | solution.py:368
  17.6 0.1 add_convert_fusion.edges
  17.7 0.0 copy-done.2
  17.7 0.0 copy-start
  17.7 0.0 copy-start.1
  17.7 7.6 %gram.1.sums = f32[120,88]{1,0:T(8,128)S(1)} custom-call(s32[32]{0:T(128)S(1)} %copy-done.2, bf16[88,8,32,128]{3,2,1,0:T(8,128)(2,1)} %image.1, bf16[88,8,32,128]{3,2,1,0:T(8,128)(2,1)} %basis.3), custom_call_target="tpu_custom_call" | custom-call | flops 2000000000 | bytes 17000000 | tf_op jit(solution)/shard_map/gram/pallas_call | solution.py:388
  25.3 0.0 collective-permute-done.2.y_low
  25.3 0.0 collective-permute-done.3.y_high
  25.3 0.0 collective-permute-done.z_low
  25.3 0.0 collective-permute-done.1.z_high
  25.3 0.0 copy-done
  25.4 0.0 copy-done.1
  25.4 9.5 %normal.1 = f32[88,128]{1,0:T(8,128)S(1)} custom-call(s32[4]{0:T(128)S(1)} %add_convert_fusion.edges, f32[120,88]{1,0:T(8,128)S(1)} %gram.1.sums, bf16[8,32,88,128]{3,2,1,0:T(8,128)(2,1)S(1)} %copy-done, s32[8,32,128]{2,1,0:T(8,128)S(1)} %copy-done.1, bf16[32,88,128]{2,1,0:T(8,128)(2,1)S(1)} %collective-permute-done.z_low, ...), custom_call_target="tpu_custom_call" | custom-call | tf_op jit(solution)/shard_map/normal/pallas_call | solution.py:408
  34.9 0.1 collective-permute-start.4
  35.0 1.2 %collective-permute-done.4 = f32[88,128]{1,0:T(8,128)S(1)} collective-permute-done((f32[88,128]{1,0:T(8,128)S(1)}, f32[88,128]{1,0:T(8,128)S(1)}, u32[]{:S(2)}, u32[]{:S(2)}) %collective-permute-start.4) | collective-permute-done | bytes 45088 | tf_op jit(solution)/shard_map/ppermute | solution.py:338
  36.2 0.9 %collective-permute-start.7 = (f32[88,128]{1,0:T(8,128)S(1)}, f32[88,128]{1,0:T(8,128)S(1)}, u32[]{:S(2)}, u32[]{:S(2)}) collective-permute-start(f32[88,128]{1,0:T(8,128)S(1)} %add.30), channel_id=1, source_target_pairs={{0,96},{4,100},{8,104},{12,108},{16,112},{20,116},{24,120},{28,124... | collective-permute-start | bytes 135176 | tf_op jit(solution)/shard_map/ppermute | solution.py:338
  37.1 1.2 %collective-permute-start.6 = (f32[88,128]{1,0:T(8,128)S(1)}, f32[88,128]{1,0:T(8,128)S(1)}, u32[]{:S(2)}, u32[]{:S(2)}) collective-permute-start(f32[88,128]{1,0:T(8,128)S(1)} %add.30), channel_id=1, source_target_pairs={{0,32},{4,36},{8,40},{12,44},{16,48},{20,52},{24,56},{28,60},{32,6... | collective-permute-start | bytes 135176 | tf_op jit(solution)/shard_map/ppermute | solution.py:338
  38.3 1.1 %collective-permute-start.5 = (f32[88,128]{1,0:T(8,128)S(1)}, f32[88,128]{1,0:T(8,128)S(1)}, u32[]{:S(2)}, u32[]{:S(2)}) collective-permute-start(f32[88,128]{1,0:T(8,128)S(1)} %add.30), channel_id=1, source_target_pairs={{0,64},{4,68},{8,72},{12,76},{16,80},{20,84},{24,88},{28,92},{32,9... | collective-permute-start | bytes 135176 | tf_op jit(solution)/shard_map/ppermute | solution.py:338
  39.4 0.9 %collective-permute-done.7 = f32[88,128]{1,0:T(8,128)S(1)} collective-permute-done((f32[88,128]{1,0:T(8,128)S(1)}, f32[88,128]{1,0:T(8,128)S(1)}, u32[]{:S(2)}, u32[]{:S(2)}) %collective-permute-start.7) | collective-permute-done | bytes 45088 | tf_op jit(solution)/shard_map/ppermute | solution.py:338
  40.3 2.5 %collective-permute-done.6 = f32[88,128]{1,0:T(8,128)S(1)} collective-permute-done((f32[88,128]{1,0:T(8,128)S(1)}, f32[88,128]{1,0:T(8,128)S(1)}, u32[]{:S(2)}, u32[]{:S(2)}) %collective-permute-start.6) | collective-permute-done | bytes 45088 | tf_op jit(solution)/shard_map/ppermute | solution.py:338
  42.8 1.0 %collective-permute-done.5 = f32[88,128]{1,0:T(8,128)S(1)} collective-permute-done((f32[88,128]{1,0:T(8,128)S(1)}, f32[88,128]{1,0:T(8,128)S(1)}, u32[]{:S(2)}, u32[]{:S(2)}) %collective-permute-start.5) | collective-permute-done | bytes 45088 | tf_op jit(solution)/shard_map/ppermute | solution.py:338
  43.8 2.2 %collective-permute-start.10 = (f32[88,128]{1,0:T(8,128)S(1)}, f32[88,128]{1,0:T(8,128)S(1)}, u32[]{:S(2)}, u32[]{:S(2)}) collective-permute-start(f32[88,128]{1,0:T(8,128)S(1)} %add_add_fusion.2), channel_id=1, source_target_pairs={{0,24},{4,28},{8,0},{12,4},{16,8},{20,12},{24,16},{28,20},{32,56},... | collective-permute-start | bytes 135176 | tf_op jit(solution)/shard_map/ppermute | solution.py:338
  46.0 0.0 collective-permute-start.9
  46.0 1.5 %collective-permute-start.8 = (f32[88,128]{1,0:T(8,128)S(1)}, f32[88,128]{1,0:T(8,128)S(1)}, u32[]{:S(2)}, u32[]{:S(2)}) collective-permute-start(f32[88,128]{1,0:T(8,128)S(1)} %add_add_fusion.2), channel_id=1, source_target_pairs={{0,16},{4,20},{8,24},{12,28},{16,0},{20,4},{24,8},{28,12},{32,48},... | collective-permute-start | bytes 135176 | tf_op jit(solution)/shard_map/ppermute | solution.py:338
  47.6 0.4 collective-permute-done.10
  48.0 3.8 %collective-permute-done.9 = f32[88,128]{1,0:T(8,128)S(1)} collective-permute-done((f32[88,128]{1,0:T(8,128)S(1)}, f32[88,128]{1,0:T(8,128)S(1)}, u32[]{:S(2)}, u32[]{:S(2)}) %collective-permute-start.9) | collective-permute-done | bytes 45088 | tf_op jit(solution)/shard_map/ppermute | solution.py:338
  51.8 0.0 collective-permute-done.8
  51.8 3.1 %collective-permute-start.13 = (f32[88,128]{1,0:T(8,128)S(1)}, f32[88,128]{1,0:T(8,128)S(1)}, u32[]{:S(2)}, u32[]{:S(2)}) collective-permute-start(f32[88,128]{1,0:T(8,128)S(1)} %add_add_fusion.1), channel_id=1, source_target_pairs={{0,3},{1,0},{2,1},{3,2},{4,7},{5,4},{6,5},{7,6},{8,11},{9,8},{10,9... | collective-permute-start | bytes 135176 | tf_op jit(solution)/shard_map/ppermute | solution.py:338
  54.9 0.0 collective-permute-start.12
  54.9 2.2 %collective-permute-start.11 = (f32[88,128]{1,0:T(8,128)S(1)}, f32[88,128]{1,0:T(8,128)S(1)}, u32[]{:S(2)}, u32[]{:S(2)}) collective-permute-start(f32[88,128]{1,0:T(8,128)S(1)} %add_add_fusion.1), channel_id=1, source_target_pairs={{0,2},{1,3},{2,0},{3,1},{4,6},{5,7},{6,4},{7,5},{8,10},{9,11},{10,... | collective-permute-start | bytes 135176 | tf_op jit(solution)/shard_map/ppermute | solution.py:338
  57.1 0.0 collective-permute-done.13
  57.1 3.5 %collective-permute-done.12 = f32[88,128]{1,0:T(8,128)S(1)} collective-permute-done((f32[88,128]{1,0:T(8,128)S(1)}, f32[88,128]{1,0:T(8,128)S(1)}, u32[]{:S(2)}, u32[]{:S(2)}) %collective-permute-start.12) | collective-permute-done | bytes 45088 | tf_op jit(solution)/shard_map/ppermute | solution.py:338
  60.6 0.0 collective-permute-done.11
  60.6 12.6 %update.1 = (f32[32,8,32,128]{3,2,1,0:T(8,128)}, f32[32,8,32,128]{3,2,1,0:T(8,128)}) custom-call(s32[4]{0:T(128)S(1)} %add_convert_fusion.edges, f32[88,128]{1,0:T(8,128)S(1)} %add_add_fusion.packed, bf16[8,32,88,128]{3,2,1,0:T(8,128)(2,1)S(1)} %copy-done, s32[8,32,128]{2,1,0:T(8,128)S(1)} %copy-done.1, bf16[32,88,128]{2,1,0:T(8,128)(2,1)S(1)} %collective-permute-done.z_low, ...), custom_call_target="tpu_custom_call" | custom-call | tf_op jit(solution)/shard_map/update/pallas_call | solution.py:419
  (4 shorter events, 0.1 us)
Async XLA Ops:
  0.6 17.1 %copy-start.2 = (s32[32]{0:T(128)S(1)}, s32[32]{0:T(128)}, u32[]{:S(2)}) copy-start(s32[32]{0:T(128)} %picked.1) | copy-start | bytes 388
  8.5 16.8 %collective-permute-start = (bf16[32,88,128]{2,1,0:T(8,128)(2,1)}, bf16[32,88,128]{2,1,0:T(8,128)(2,1)S(1)}, u32[]{:S(2)}, u32[]{:S(2)}) collective-permute-start(bf16[32,88,128]{2,1,0:T(8,128)(2,1)} %get-tuple-element.8), channel_id=1, source_target_pairs={{0,4},{4,8},{8,12},{12,16},{16,20},{20,24},{24,28},{28,32},{32,36}... | collective-permute-start | bytes 2162696 | tf_op jit(solution)/shard_map/ppermute | solution.py:368
  8.6 16.8 %collective-permute-start.1 = (bf16[32,88,128]{2,1,0:T(8,128)(2,1)}, bf16[32,88,128]{2,1,0:T(8,128)(2,1)S(1)}, u32[]{:S(2)}, u32[]{:S(2)}) collective-permute-start(bf16[32,88,128]{2,1,0:T(8,128)(2,1)} %get-tuple-element.9), channel_id=1, source_target_pairs={{4,0},{8,4},{12,8},{16,12},{20,16},{24,20},{28,24},{32,28},{36,32}... | collective-permute-start | bytes 2162696 | tf_op jit(solution)/shard_map/ppermute | solution.py:368
  14.4 10.9 %collective-permute-start.2 = (bf16[8,88,128]{2,1,0:T(8,128)(2,1)}, bf16[8,88,128]{2,1,0:T(8,128)(2,1)S(1)}, u32[]{:S(2)}, u32[]{:S(2)}) collective-permute-start(bf16[8,88,128]{2,1,0:T(8,128)(2,1)} %get-tuple-element.10), channel_id=1, source_target_pairs={{0,1},{1,2},{2,3},{3,0},{4,5},{5,6},{6,7},{7,4},{8,9},{9,10},{10,1... | collective-permute-start | bytes 540680 | tf_op jit(solution)/shard_map/ppermute | solution.py:368
  16.0 9.3 %collective-permute-start.3 = (bf16[8,88,128]{2,1,0:T(8,128)(2,1)}, bf16[8,88,128]{2,1,0:T(8,128)(2,1)S(1)}, u32[]{:S(2)}, u32[]{:S(2)}) collective-permute-start(bf16[8,88,128]{2,1,0:T(8,128)(2,1)} %get-tuple-element.11), channel_id=1, source_target_pairs={{1,0},{2,1},{3,2},{0,3},{5,4},{6,5},{7,6},{4,7},{9,8},{10,9},{11,1... | collective-permute-start | bytes 540680 | tf_op jit(solution)/shard_map/ppermute | solution.py:368
  17.7 7.6 %copy-start = (bf16[8,32,88,128]{3,2,1,0:T(8,128)(2,1)S(1)}, bf16[8,32,88,128]{3,2,1,0:T(8,128)(2,1)}, u32[]{:S(2)}) copy-start(bf16[8,32,88,128]{3,2,1,0:T(8,128)(2,1)} %get-tuple-element.7.turned) | copy-start | bytes 17301508
  17.7 7.6 %copy-start.1 = (s32[8,32,128]{2,1,0:T(8,128)S(1)}, s32[8,32,128]{2,1,0:T(8,128)}, u32[]{:S(2)}) copy-start(s32[8,32,128]{2,1,0:T(8,128)} %material.3) | copy-start | bytes 393220
  34.9 1.3 %collective-permute-start.4 = (f32[88,128]{1,0:T(8,128)S(1)}, f32[88,128]{1,0:T(8,128)S(1)}, u32[]{:S(2)}, u32[]{:S(2)}) collective-permute-start(f32[88,128]{1,0:T(8,128)S(1)} %normal.1), channel_id=1, source_target_pairs={{0,4},{4,0},{8,12},{12,8},{16,20},{20,16},{24,28},{28,24},{32,36},... | collective-permute-start | bytes 135176 | tf_op jit(solution)/shard_map/ppermute | solution.py:338
  36.2 4.1 %collective-permute-start.7 = (f32[88,128]{1,0:T(8,128)S(1)}, f32[88,128]{1,0:T(8,128)S(1)}, u32[]{:S(2)}, u32[]{:S(2)}) collective-permute-start(f32[88,128]{1,0:T(8,128)S(1)} %add.30), channel_id=1, source_target_pairs={{0,96},{4,100},{8,104},{12,108},{16,112},{20,116},{24,120},{28,124... | collective-permute-start | bytes 135176 | tf_op jit(solution)/shard_map/ppermute | solution.py:338
  37.1 5.7 %collective-permute-start.6 = (f32[88,128]{1,0:T(8,128)S(1)}, f32[88,128]{1,0:T(8,128)S(1)}, u32[]{:S(2)}, u32[]{:S(2)}) collective-permute-start(f32[88,128]{1,0:T(8,128)S(1)} %add.30), channel_id=1, source_target_pairs={{0,32},{4,36},{8,40},{12,44},{16,48},{20,52},{24,56},{28,60},{32,6... | collective-permute-start | bytes 135176 | tf_op jit(solution)/shard_map/ppermute | solution.py:338
  38.3 5.6 %collective-permute-start.5 = (f32[88,128]{1,0:T(8,128)S(1)}, f32[88,128]{1,0:T(8,128)S(1)}, u32[]{:S(2)}, u32[]{:S(2)}) collective-permute-start(f32[88,128]{1,0:T(8,128)S(1)} %add.30), channel_id=1, source_target_pairs={{0,64},{4,68},{8,72},{12,76},{16,80},{20,84},{24,88},{28,92},{32,9... | collective-permute-start | bytes 135176 | tf_op jit(solution)/shard_map/ppermute | solution.py:338
  43.8 4.1 %collective-permute-start.10 = (f32[88,128]{1,0:T(8,128)S(1)}, f32[88,128]{1,0:T(8,128)S(1)}, u32[]{:S(2)}, u32[]{:S(2)}) collective-permute-start(f32[88,128]{1,0:T(8,128)S(1)} %add_add_fusion.2), channel_id=1, source_target_pairs={{0,24},{4,28},{8,0},{12,4},{16,8},{20,12},{24,16},{28,20},{32,56},... | collective-permute-start | bytes 135176 | tf_op jit(solution)/shard_map/ppermute | solution.py:338
  46.0 5.7 %collective-permute-start.9 = (f32[88,128]{1,0:T(8,128)S(1)}, f32[88,128]{1,0:T(8,128)S(1)}, u32[]{:S(2)}, u32[]{:S(2)}) collective-permute-start(f32[88,128]{1,0:T(8,128)S(1)} %add_add_fusion.2), channel_id=1, source_target_pairs={{0,8},{4,12},{8,16},{12,20},{16,24},{20,28},{24,0},{28,4},{32,40},... | collective-permute-start | bytes 135176 | tf_op jit(solution)/shard_map/ppermute | solution.py:338
  46.0 5.7 %collective-permute-start.8 = (f32[88,128]{1,0:T(8,128)S(1)}, f32[88,128]{1,0:T(8,128)S(1)}, u32[]{:S(2)}, u32[]{:S(2)}) collective-permute-start(f32[88,128]{1,0:T(8,128)S(1)} %add_add_fusion.2), channel_id=1, source_target_pairs={{0,16},{4,20},{8,24},{12,28},{16,0},{20,4},{24,8},{28,12},{32,48},... | collective-permute-start | bytes 135176 | tf_op jit(solution)/shard_map/ppermute | solution.py:338
  51.8 5.3 %collective-permute-start.13 = (f32[88,128]{1,0:T(8,128)S(1)}, f32[88,128]{1,0:T(8,128)S(1)}, u32[]{:S(2)}, u32[]{:S(2)}) collective-permute-start(f32[88,128]{1,0:T(8,128)S(1)} %add_add_fusion.1), channel_id=1, source_target_pairs={{0,3},{1,0},{2,1},{3,2},{4,7},{5,4},{6,5},{7,6},{8,11},{9,8},{10,9... | collective-permute-start | bytes 135176 | tf_op jit(solution)/shard_map/ppermute | solution.py:338
  54.9 5.7 %collective-permute-start.12 = (f32[88,128]{1,0:T(8,128)S(1)}, f32[88,128]{1,0:T(8,128)S(1)}, u32[]{:S(2)}, u32[]{:S(2)}) collective-permute-start(f32[88,128]{1,0:T(8,128)S(1)} %add_add_fusion.1), channel_id=1, source_target_pairs={{0,1},{1,2},{2,3},{3,0},{4,5},{5,6},{6,7},{7,4},{8,9},{9,10},{10,1... | collective-permute-start | bytes 135176 | tf_op jit(solution)/shard_map/ppermute | solution.py:338
  54.9 5.7 %collective-permute-start.11 = (f32[88,128]{1,0:T(8,128)S(1)}, f32[88,128]{1,0:T(8,128)S(1)}, u32[]{:S(2)}, u32[]{:S(2)}) collective-permute-start(f32[88,128]{1,0:T(8,128)S(1)} %add_add_fusion.1), channel_id=1, source_target_pairs={{0,2},{1,3},{2,0},{3,1},{4,6},{5,7},{6,4},{7,5},{8,10},{9,11},{10,... | collective-permute-start | bytes 135176 | tf_op jit(solution)/shard_map/ppermute | solution.py:338

commit v5 on v4

--- a/solution.py
+++ b/solution.py
@@ -16,15 +16,12 @@
 MIB = 2**20
 
 
-def turn_kernel(basis, turned, z_first, z_last, y_first, y_last, slab, moved, sems, out_sems):
-    columns, depth, height, width = basis.shape
+def face_kernel(basis, z_first, z_last, y_first, y_last, slab, sems):
+    depth, height = basis.shape[1:3]
     slots = slab.shape[0]
 
     def load(z, slot):
         return pltpu.make_async_copy(basis.at[:, z], slab.at[slot], sems.at[slot])
-
-    def store(z, slot):
-        return pltpu.make_async_copy(moved.at[slot], turned.at[z], out_sems.at[slot])
 
     for z in range(slots - 1):
         load(z, z).start()
@@ -36,66 +33,57 @@
         def _():
             load(z + slots - 1, lax.rem(z + slots - 1, slots)).start()
 
-        @pl.when(z >= slots)
-        def _():
-            store(z - slots, slot).wait()
-
         load(z, slot).wait()
-        for y in range(0, height, 16):
-            part = jnp.swapaxes(slab[slot, :, y : y + 16, :], 0, 1)
-            moved[slot, y : y + 16] = part
-            if y == 0:
-                y_first[z] = part[0]
-            if y + 16 == height:
-                y_last[z] = part[15]
-        store(z, slot).start()
-
-        @pl.when(z == 0)
-        def _():
-            z_first[...] = moved[0]
-
+        y_first[z] = jnp.swapaxes(slab[slot, :, :16, :], 0, 1)[0]
+        y_last[z] = jnp.swapaxes(slab[slot, :, height - 16 :, :], 0, 1)[15]
+
+        def whole_plane(face):
+            for y in range(0, height, 16):
+                face[y : y + 16] = jnp.swapaxes(slab[slot, :, y : y + 16, :], 0, 1)
+
+        pl.when(z == 0)(lambda: whole_plane(z_first))
+        pl.when(z == depth - 1)(lambda: whole_plane(z_last))
         return 0
 
     lax.fori_loop(0, depth, step, 0)
-    z_last[...] = moved[(depth - 1) % slots]
-    for z in range(depth - slots, depth):
-        store(z, z % slots).wait()
-
-
-def gram_kernel(picked, image, basis, sums, image_slab, picked_slab, rows, sems, picked_sems):
+
+
+def gram_kernel(
+    picked, image, basis, sums, turned, image_slab, basis_slab, rows, image_sems, basis_sems
+):
     columns, depth, height, width = image.shape
     count = picked.shape[0]
     total = columns + count
     slots = image_slab.shape[0]
 
-    def load(z, slot):
-        return pltpu.make_async_copy(image.at[:, z], image_slab.at[slot], sems.at[slot])
-
-    def load_picked(c):
-        return pltpu.make_async_copy(basis.at[picked[c]], picked_slab.at[c], picked_sems.at[c])
-
-    load(0, 0).start()
-    for c in range(count):
-        load_picked(c).start()
-    for z in range(1, slots - 1):
-        load(z, z).start()
+    def loads(z, slot):
+        return (
+            pltpu.make_async_copy(image.at[:, z], image_slab.at[slot], image_sems.at[slot]),
+            pltpu.make_async_copy(basis.at[:, z], basis_slab.at[slot], basis_sems.at[slot]),
+        )
+
+    for z in range(slots - 1):
+        for copy in loads(z, z):
+            copy.start()
     sums[...] = jnp.zeros_like(sums)
-    for c in range(count):
-        load_picked(c).wait()
 
     def step(z, _):
         slot = lax.rem(z, slots)
 
         @pl.when(z + slots - 1 < depth)
         def _():
-            load(z + slots - 1, lax.rem(z + slots - 1, slots)).start()
-
+            for copy in loads(z + slots - 1, lax.rem(z + slots - 1, slots)):
+                copy.start()
+
+        for copy in loads(z, slot):
+            copy.wait()
+        for c in range(columns):
+            rows[c * PITCH : c * PITCH + height] = image_slab[slot, c].astype(F32)
         for c in range(count):
             at = (columns + c) * PITCH
-            rows[at : at + height] = picked_slab[c, z].astype(F32)
-        load(z, slot).wait()
-        for c in range(columns):
-            rows[c * PITCH : c * PITCH + height] = image_slab[slot, c].astype(F32)
+            rows[at : at + height] = basis_slab[slot, picked[c]].astype(F32)
+        for y in range(0, height, 16):
+            turned[z, y : y + 16] = jnp.swapaxes(basis_slab[slot, :, y : y + 16, :], 0, 1)
         both = jnp.concatenate(
             [rows[pl.ds(y, total, stride=PITCH), :].astype(BF16) for y in range(height)], 1
         )
@@ -369,35 +357,36 @@
 
     face = jax.ShapeDtypeStruct((height, columns, width), BF16)
     edge = jax.ShapeDtypeStruct((depth, columns, width), BF16)
-    turned, z_first, z_last, y_first, y_last = pl.pallas_call(
-        turn_kernel,
+    z_first, z_last, y_first, y_last = pl.pallas_call(
+        face_kernel,
         in_specs=[whole(pltpu.HBM)],
-        out_specs=[whole(pltpu.HBM)] + [whole()] * 4,
-        out_shape=[jax.ShapeDtypeStruct((depth, height, columns, width), BF16), face, face, edge, edge],
+        out_specs=[whole()] * 4,
+        out_shape=[face, face, edge, edge],
         scratch_shapes=[
-            pltpu.VMEM((3, columns, height, width), BF16),
-            pltpu.VMEM((3, height, columns, width), BF16),
-            pltpu.SemaphoreType.DMA((3,)),
-            pltpu.SemaphoreType.DMA((3,)),
+            pltpu.VMEM((4, columns, height, width), BF16),
+            pltpu.SemaphoreType.DMA((4,)),
         ],
-        compiler_params=pltpu.CompilerParams(vmem_limit_bytes=57 * MIB),
-        name="turn",
+        compiler_params=pltpu.CompilerParams(vmem_limit_bytes=52 * MIB),
+        name="faces",
     )(basis)
     z_low, z_high = neighbours(z_first, z_last, "slab", slabs)
     y_low, y_high = neighbours(y_first, y_last, "pencil", pencils)
-    sums = pl.pallas_call(
+    sums, turned = pl.pallas_call(
         gram_kernel,
         in_specs=[whole(pltpu.SMEM), whole(pltpu.HBM), whole(pltpu.HBM)],
-        out_specs=whole(),
-        out_shape=jax.ShapeDtypeStruct((columns + count, columns), F32),
+        out_specs=[whole()] * 2,
+        out_shape=[
+            jax.ShapeDtypeStruct((columns + count, columns), F32),
+            jax.ShapeDtypeStruct((depth, height, columns, width), BF16),
+        ],
         scratch_shapes=[
-            pltpu.VMEM((3, columns, height, width), BF16),
-            pltpu.VMEM((count, depth, height, width), BF16),
+            pltpu.VMEM((4, columns, height, width), BF16),
+            pltpu.VMEM((4, columns, height, width), BF16),
             pltpu.VMEM(((columns + count) * PITCH, width), F32),
-            pltpu.SemaphoreType.DMA((3,)),
-            pltpu.SemaphoreType.DMA((count,)),
+            pltpu.SemaphoreType.DMA((4,)),
+            pltpu.SemaphoreType.DMA((4,)),
         ],
-        compiler_params=pltpu.CompilerParams(vmem_limit_bytes=49 * MIB),
+        compiler_params=pltpu.CompilerParams(vmem_limit_bytes=46 * MIB),
         cost_estimate=pl.CostEstimate(flops=2 * 10**9, bytes_accessed=17 * 10**6, transcendentals=0),
         name="gram",
     )(picked, image, basis)

time: 73.8 us -> 69.9 us (0.947)
  Pallas kernels: 37.6 us -> 34.2 us
    pallas_call x1, Pallas kernels: 7.84 us -> 4.27 us  [local(): pl.pallas_call(face_kernel, in_specs=[whole(pltpu.HBM)], out_specs=[whole...]
  transfers between devices with their start and end apart: 14 -> 14, of which waited for: 7 -> 8; matrix products, arithmetic and copies ran while one was open for 0% -> 0% of each run, Pallas kernels for 10% -> 11%
where the time goes in v5:
time: 69.9 us; the launch traced here: 69.7 us
  Pallas kernels  34.2 us (49%)
  starting transfers between devices  21 us (30%)
  waiting for transfers between devices  13.4 us (19%)
  between operations  0.89 us (1%)
    ppermute x10, waiting for transfers between devices, shifted(): return lax.ppermute(value, axis, perm)  13.4 us
    pallas_call x1, Pallas kernels, local(): pl.pallas_call(update_kernel, in_specs=[whole(pltpu.SMEM)] + [whole()] *...  12.7 us
    ppermute x10, starting transfers between devices, shifted(): return lax.ppermute(value, axis, perm)  11.9 us
    pallas_call x1, Pallas kernels, local(): pl.pallas_call(normal_kernel, in_specs=[whole(pltpu.SMEM)] + [whole()] *...  9.49 us
    pallas_call x1, Pallas kernels, local(): pl.pallas_call(gram_kernel, in_specs=[whole(pltpu.SMEM), whole(pltpu.HBM)...  7.74 us
    ppermute x2, starting transfers between devices, neighbours(): lax.ppermute(low_face, axis, down)  7.48 us
    pallas_call x1, Pallas kernels, local(): pl.pallas_call(face_kernel, in_specs=[whole(pltpu.HBM)], out_specs=[whole...  4.27 us
    ppermute x2, starting transfers between devices, neighbours(): lax.ppermute(high_face, axis, up)  1.65 us
  transfers between devices with their start and end apart: 14, of which 8 were waited for; matrix products, arithmetic and copies ran while one was open for 0% of the time, Pallas kernels for 11%

profile of v5, /device:TPU:0, one launch (start us, length us, event | category | flops | bytes accessed | tf_op | source)
XLA Modules:
  0.0 69.7 jit_solution(12181943025518465377)
XLA Ops:
  0.6 0.0 copy-start.1
  0.6 4.3 %faces.1 = (bf16[32,88,128]{2,1,0:T(8,128)(2,1)S(1)}, bf16[32,88,128]{2,1,0:T(8,128)(2,1)S(1)}, bf16[8,88,128]{2,1,0:T(8,128)(2,1)S(1)}, bf16[8,88,128]{2,1,0:T(8,128)(2,1)}) custom-call(bf16[88,8,32,128]{3,2,1,0:T(8,128)(2,1)} %basis.3), custom_call_target="tpu_custom_call" | custom-call | tf_op jit(solution)/shard_map/faces/pallas_call | solution.py:360
  4.9 0.1 collective-permute-start
  5.0 5.8 %collective-permute-start.1 = (bf16[32,88,128]{2,1,0:T(8,128)(2,1)S(1)}, bf16[32,88,128]{2,1,0:T(8,128)(2,1)S(1)}, u32[]{:S(2)}, u32[]{:S(2)}) collective-permute-start(bf16[32,88,128]{2,1,0:T(8,128)(2,1)S(1)} %get-tuple-element.11), channel_id=1, source_target_pairs={{4,0},{8,4},{12,8},{16,12},{20,16},{24,20},{28,24},{32,28},{36,32}... | collective-permute-start | bytes 2162696 | tf_op jit(solution)/shard_map/ppermute | solution.py:356
  10.8 1.6 %collective-permute-start.2 = (bf16[8,88,128]{2,1,0:T(8,128)(2,1)}, bf16[8,88,128]{2,1,0:T(8,128)(2,1)S(1)}, u32[]{:S(2)}, u32[]{:S(2)}) collective-permute-start(bf16[8,88,128]{2,1,0:T(8,128)(2,1)} %get-tuple-element.12), channel_id=1, source_target_pairs={{0,1},{1,2},{2,3},{3,0},{4,5},{5,6},{6,7},{7,4},{8,9},{9,10},{10,1... | collective-permute-start | bytes 540680 | tf_op jit(solution)/shard_map/ppermute | solution.py:356
  12.4 1.7 %collective-permute-start.3 = (bf16[8,88,128]{2,1,0:T(8,128)(2,1)S(1)}, bf16[8,88,128]{2,1,0:T(8,128)(2,1)S(1)}, u32[]{:S(2)}, u32[]{:S(2)}) collective-permute-start(bf16[8,88,128]{2,1,0:T(8,128)(2,1)S(1)} %get-tuple-element.13), channel_id=1, source_target_pairs={{1,0},{2,1},{3,2},{0,3},{5,4},{6,5},{7,6},{4,7},{9,8},{10,9},{11,1... | collective-permute-start | bytes 540680 | tf_op jit(solution)/shard_map/ppermute | solution.py:356
  14.1 0.1 add_convert_fusion.edges
  14.1 0.0 copy-done.1
  14.1 0.0 copy-start
  14.1 7.7 %gram.1 = (f32[120,88]{1,0:T(8,128)S(1)}, bf16[8,32,88,128]{3,2,1,0:T(8,128)(2,1)S(1)}) custom-call(s32[32]{0:T(128)S(1)} %copy-done.1, bf16[88,8,32,128]{3,2,1,0:T(8,128)(2,1)} %image.1, bf16[88,8,32,128]{3,2,1,0:T(8,128)(2,1)} %basis.3), custom_call_target="tpu_custom_call" | custom-call | flops 2000000000 | bytes 17000000 | tf_op jit(solution)/shard_map/gram/pallas_call | solution.py:374
  21.9 0.0 collective-permute-done.2.y_low
  21.9 0.0 collective-permute-done.3.y_high
  21.9 0.0 collective-permute-done.z_low
  21.9 0.0 collective-permute-done.1.z_high
  21.9 0.0 copy-done
  21.9 9.5 %normal.1 = f32[88,128]{1,0:T(8,128)S(1)} custom-call(s32[4]{0:T(128)S(1)} %add_convert_fusion.edges, f32[120,88]{1,0:T(8,128)S(1)} %get-tuple-element.8.sums, bf16[8,32,88,128]{3,2,1,0:T(8,128)(2,1)S(1)} %get-tuple-element.9.turned, s32[8,32,128]{2,1,0:T(8,128)S(1)} %copy-done, bf16[32,88,128]{2,1,0:T(8,128)(2,1)S(1)} %collective-permute-done.z_low, ...), custom_call_target="tpu_custom_call" | custom-call | tf_op jit(solution)/shard_map/normal/pallas_call | solution.py:397
  31.4 0.1 collective-permute-start.4
  31.5 1.2 %collective-permute-done.4 = f32[88,128]{1,0:T(8,128)S(1)} collective-permute-done((f32[88,128]{1,0:T(8,128)S(1)}, f32[88,128]{1,0:T(8,128)S(1)}, u32[]{:S(2)}, u32[]{:S(2)}) %collective-permute-start.4) | collective-permute-done | bytes 45088 | tf_op jit(solution)/shard_map/ppermute | solution.py:326
  32.7 0.9 %collective-permute-start.7 = (f32[88,128]{1,0:T(8,128)S(1)}, f32[88,128]{1,0:T(8,128)S(1)}, u32[]{:S(2)}, u32[]{:S(2)}) collective-permute-start(f32[88,128]{1,0:T(8,128)S(1)} %add.30), channel_id=1, source_target_pairs={{0,96},{4,100},{8,104},{12,108},{16,112},{20,116},{24,120},{28,124... | collective-permute-start | bytes 135176 | tf_op jit(solution)/shard_map/ppermute | solution.py:326
  33.7 1.2 %collective-permute-start.6 = (f32[88,128]{1,0:T(8,128)S(1)}, f32[88,128]{1,0:T(8,128)S(1)}, u32[]{:S(2)}, u32[]{:S(2)}) collective-permute-start(f32[88,128]{1,0:T(8,128)S(1)} %add.30), channel_id=1, source_target_pairs={{0,32},{4,36},{8,40},{12,44},{16,48},{20,52},{24,56},{28,60},{32,6... | collective-permute-start | bytes 135176 | tf_op jit(solution)/shard_map/ppermute | solution.py:326
  34.8 1.1 %collective-permute-start.5 = (f32[88,128]{1,0:T(8,128)S(1)}, f32[88,128]{1,0:T(8,128)S(1)}, u32[]{:S(2)}, u32[]{:S(2)}) collective-permute-start(f32[88,128]{1,0:T(8,128)S(1)} %add.30), channel_id=1, source_target_pairs={{0,64},{4,68},{8,72},{12,76},{16,80},{20,84},{24,88},{28,92},{32,9... | collective-permute-start | bytes 135176 | tf_op jit(solution)/shard_map/ppermute | solution.py:326
  36.0 0.9 %collective-permute-done.7 = f32[88,128]{1,0:T(8,128)S(1)} collective-permute-done((f32[88,128]{1,0:T(8,128)S(1)}, f32[88,128]{1,0:T(8,128)S(1)}, u32[]{:S(2)}, u32[]{:S(2)}) %collective-permute-start.7) | collective-permute-done | bytes 45088 | tf_op jit(solution)/shard_map/ppermute | solution.py:326
  36.9 2.5 %collective-permute-done.6 = f32[88,128]{1,0:T(8,128)S(1)} collective-permute-done((f32[88,128]{1,0:T(8,128)S(1)}, f32[88,128]{1,0:T(8,128)S(1)}, u32[]{:S(2)}, u32[]{:S(2)}) %collective-permute-start.6) | collective-permute-done | bytes 45088 | tf_op jit(solution)/shard_map/ppermute | solution.py:326
  39.4 1.0 %collective-permute-done.5 = f32[88,128]{1,0:T(8,128)S(1)} collective-permute-done((f32[88,128]{1,0:T(8,128)S(1)}, f32[88,128]{1,0:T(8,128)S(1)}, u32[]{:S(2)}, u32[]{:S(2)}) %collective-permute-start.5) | collective-permute-done | bytes 45088 | tf_op jit(solution)/shard_map/ppermute | solution.py:326
  40.4 1.8 %collective-permute-start.10 = (f32[88,128]{1,0:T(8,128)S(1)}, f32[88,128]{1,0:T(8,128)S(1)}, u32[]{:S(2)}, u32[]{:S(2)}) collective-permute-start(f32[88,128]{1,0:T(8,128)S(1)} %add_add_fusion.2), channel_id=1, source_target_pairs={{0,24},{4,28},{8,0},{12,4},{16,8},{20,12},{24,16},{28,20},{32,56},... | collective-permute-start | bytes 135176 | tf_op jit(solution)/shard_map/ppermute | solution.py:326
  42.2 0.3 collective-permute-start.9
  42.5 1.3 %collective-permute-start.8 = (f32[88,128]{1,0:T(8,128)S(1)}, f32[88,128]{1,0:T(8,128)S(1)}, u32[]{:S(2)}, u32[]{:S(2)}) collective-permute-start(f32[88,128]{1,0:T(8,128)S(1)} %add_add_fusion.2), channel_id=1, source_target_pairs={{0,16},{4,20},{8,24},{12,28},{16,0},{20,4},{24,8},{28,12},{32,48},... | collective-permute-start | bytes 135176 | tf_op jit(solution)/shard_map/ppermute | solution.py:326
  43.8 0.7 %collective-permute-done.10 = f32[88,128]{1,0:T(8,128)S(1)} collective-permute-done((f32[88,128]{1,0:T(8,128)S(1)}, f32[88,128]{1,0:T(8,128)S(1)}, u32[]{:S(2)}, u32[]{:S(2)}) %collective-permute-start.10) | collective-permute-done | bytes 45088 | tf_op jit(solution)/shard_map/ppermute | solution.py:326
  44.5 3.0 %collective-permute-done.9 = f32[88,128]{1,0:T(8,128)S(1)} collective-permute-done((f32[88,128]{1,0:T(8,128)S(1)}, f32[88,128]{1,0:T(8,128)S(1)}, u32[]{:S(2)}, u32[]{:S(2)}) %collective-permute-start.9) | collective-permute-done | bytes 45088 | tf_op jit(solution)/shard_map/ppermute | solution.py:326
  47.5 0.5 collective-permute-done.8
  48.1 3.0 %collective-permute-start.13 = (f32[88,128]{1,0:T(8,128)S(1)}, f32[88,128]{1,0:T(8,128)S(1)}, u32[]{:S(2)}, u32[]{:S(2)}) collective-permute-start(f32[88,128]{1,0:T(8,128)S(1)} %add_add_fusion.1), channel_id=1, source_target_pairs={{0,3},{1,0},{2,1},{3,2},{4,7},{5,4},{6,5},{7,6},{8,11},{9,8},{10,9... | collective-permute-start | bytes 135176 | tf_op jit(solution)/shard_map/ppermute | solution.py:326
  51.1 0.0 collective-permute-start.12
  51.1 2.2 %collective-permute-start.11 = (f32[88,128]{1,0:T(8,128)S(1)}, f32[88,128]{1,0:T(8,128)S(1)}, u32[]{:S(2)}, u32[]{:S(2)}) collective-permute-start(f32[88,128]{1,0:T(8,128)S(1)} %add_add_fusion.1), channel_id=1, source_target_pairs={{0,2},{1,3},{2,0},{3,1},{4,6},{5,7},{6,4},{7,5},{8,10},{9,11},{10,... | collective-permute-start | bytes 135176 | tf_op jit(solution)/shard_map/ppermute | solution.py:326
  53.3 0.0 collective-permute-done.13
  53.3 3.5 %collective-permute-done.12 = f32[88,128]{1,0:T(8,128)S(1)} collective-permute-done((f32[88,128]{1,0:T(8,128)S(1)}, f32[88,128]{1,0:T(8,128)S(1)}, u32[]{:S(2)}, u32[]{:S(2)}) %collective-permute-start.12) | collective-permute-done | bytes 45088 | tf_op jit(solution)/shard_map/ppermute | solution.py:326
  56.8 0.0 collective-permute-done.11
  56.8 12.7 %update.1 = (f32[32,8,32,128]{3,2,1,0:T(8,128)}, f32[32,8,32,128]{3,2,1,0:T(8,128)}) custom-call(s32[4]{0:T(128)S(1)} %add_convert_fusion.edges, f32[88,128]{1,0:T(8,128)S(1)} %add_add_fusion.packed, bf16[8,32,88,128]{3,2,1,0:T(8,128)(2,1)S(1)} %get-tuple-element.9.turned, s32[8,32,128]{2,1,0:T(8,128)S(1)} %copy-done, ...), custom_call_target="tpu_custom_call" | custom-call | tf_op jit(solution)/shard_map/update/pallas_call | solution.py:408
  (4 shorter events, 0.1 us)
Async XLA Ops:
  0.6 13.5 %copy-start.1 = (s32[32]{0:T(128)S(1)}, s32[32]{0:T(128)}, u32[]{:S(2)}) copy-start(s32[32]{0:T(128)} %picked.1) | copy-start | bytes 388
  4.9 17.0 %collective-permute-start = (bf16[32,88,128]{2,1,0:T(8,128)(2,1)S(1)}, bf16[32,88,128]{2,1,0:T(8,128)(2,1)S(1)}, u32[]{:S(2)}, u32[]{:S(2)}) collective-permute-start(bf16[32,88,128]{2,1,0:T(8,128)(2,1)S(1)} %get-tuple-element.10), channel_id=1, source_target_pairs={{0,4},{4,8},{8,12},{12,16},{16,20},{20,24},{24,28},{28,32},{32,36}... | collective-permute-start | bytes 2162696 | tf_op jit(solution)/shard_map/ppermute | solution.py:356
  5.0 16.9 %collective-permute-start.1 = (bf16[32,88,128]{2,1,0:T(8,128)(2,1)S(1)}, bf16[32,88,128]{2,1,0:T(8,128)(2,1)S(1)}, u32[]{:S(2)}, u32[]{:S(2)}) collective-permute-start(bf16[32,88,128]{2,1,0:T(8,128)(2,1)S(1)} %get-tuple-element.11), channel_id=1, source_target_pairs={{4,0},{8,4},{12,8},{16,12},{20,16},{24,20},{28,24},{32,28},{36,32}... | collective-permute-start | bytes 2162696 | tf_op jit(solution)/shard_map/ppermute | solution.py:356
  10.8 11.1 %collective-permute-start.2 = (bf16[8,88,128]{2,1,0:T(8,128)(2,1)}, bf16[8,88,128]{2,1,0:T(8,128)(2,1)S(1)}, u32[]{:S(2)}, u32[]{:S(2)}) collective-permute-start(bf16[8,88,128]{2,1,0:T(8,128)(2,1)} %get-tuple-element.12), channel_id=1, source_target_pairs={{0,1},{1,2},{2,3},{3,0},{4,5},{5,6},{6,7},{7,4},{8,9},{9,10},{10,1... | collective-permute-start | bytes 540680 | tf_op jit(solution)/shard_map/ppermute | solution.py:356
  12.4 9.5 %collective-permute-start.3 = (bf16[8,88,128]{2,1,0:T(8,128)(2,1)S(1)}, bf16[8,88,128]{2,1,0:T(8,128)(2,1)S(1)}, u32[]{:S(2)}, u32[]{:S(2)}) collective-permute-start(bf16[8,88,128]{2,1,0:T(8,128)(2,1)S(1)} %get-tuple-element.13), channel_id=1, source_target_pairs={{1,0},{2,1},{3,2},{0,3},{5,4},{6,5},{7,6},{4,7},{9,8},{10,9},{11,1... | collective-permute-start | bytes 540680 | tf_op jit(solution)/shard_map/ppermute | solution.py:356
  14.1 7.8 %copy-start = (s32[8,32,128]{2,1,0:T(8,128)S(1)}, s32[8,32,128]{2,1,0:T(8,128)}, u32[]{:S(2)}) copy-start(s32[8,32,128]{2,1,0:T(8,128)} %material.3) | copy-start | bytes 393220
  31.4 1.3 %collective-permute-start.4 = (f32[88,128]{1,0:T(8,128)S(1)}, f32[88,128]{1,0:T(8,128)S(1)}, u32[]{:S(2)}, u32[]{:S(2)}) collective-permute-start(f32[88,128]{1,0:T(8,128)S(1)} %normal.1), channel_id=1, source_target_pairs={{0,4},{4,0},{8,12},{12,8},{16,20},{20,16},{24,28},{28,24},{32,36},... | collective-permute-start | bytes 135176 | tf_op jit(solution)/shard_map/ppermute | solution.py:326
  32.7 4.1 %collective-permute-start.7 = (f32[88,128]{1,0:T(8,128)S(1)}, f32[88,128]{1,0:T(8,128)S(1)}, u32[]{:S(2)}, u32[]{:S(2)}) collective-permute-start(f32[88,128]{1,0:T(8,128)S(1)} %add.30), channel_id=1, source_target_pairs={{0,96},{4,100},{8,104},{12,108},{16,112},{20,116},{24,120},{28,124... | collective-permute-start | bytes 135176 | tf_op jit(solution)/shard_map/ppermute | solution.py:326
  33.7 5.7 %collective-permute-start.6 = (f32[88,128]{1,0:T(8,128)S(1)}, f32[88,128]{1,0:T(8,128)S(1)}, u32[]{:S(2)}, u32[]{:S(2)}) collective-permute-start(f32[88,128]{1,0:T(8,128)S(1)} %add.30), channel_id=1, source_target_pairs={{0,32},{4,36},{8,40},{12,44},{16,48},{20,52},{24,56},{28,60},{32,6... | collective-permute-start | bytes 135176 | tf_op jit(solution)/shard_map/ppermute | solution.py:326
  34.8 5.6 %collective-permute-start.5 = (f32[88,128]{1,0:T(8,128)S(1)}, f32[88,128]{1,0:T(8,128)S(1)}, u32[]{:S(2)}, u32[]{:S(2)}) collective-permute-start(f32[88,128]{1,0:T(8,128)S(1)} %add.30), channel_id=1, source_target_pairs={{0,64},{4,68},{8,72},{12,76},{16,80},{20,84},{24,88},{28,92},{32,9... | collective-permute-start | bytes 135176 | tf_op jit(solution)/shard_map/ppermute | solution.py:326
  40.4 4.1 %collective-permute-start.10 = (f32[88,128]{1,0:T(8,128)S(1)}, f32[88,128]{1,0:T(8,128)S(1)}, u32[]{:S(2)}, u32[]{:S(2)}) collective-permute-start(f32[88,128]{1,0:T(8,128)S(1)} %add_add_fusion.2), channel_id=1, source_target_pairs={{0,24},{4,28},{8,0},{12,4},{16,8},{20,12},{24,16},{28,20},{32,56},... | collective-permute-start | bytes 135176 | tf_op jit(solution)/shard_map/ppermute | solution.py:326
  42.2 5.3 %collective-permute-start.9 = (f32[88,128]{1,0:T(8,128)S(1)}, f32[88,128]{1,0:T(8,128)S(1)}, u32[]{:S(2)}, u32[]{:S(2)}) collective-permute-start(f32[88,128]{1,0:T(8,128)S(1)} %add_add_fusion.2), channel_id=1, source_target_pairs={{0,8},{4,12},{8,16},{12,20},{16,24},{20,28},{24,0},{28,4},{32,40},... | collective-permute-start | bytes 135176 | tf_op jit(solution)/shard_map/ppermute | solution.py:326
  42.5 5.6 %collective-permute-start.8 = (f32[88,128]{1,0:T(8,128)S(1)}, f32[88,128]{1,0:T(8,128)S(1)}, u32[]{:S(2)}, u32[]{:S(2)}) collective-permute-start(f32[88,128]{1,0:T(8,128)S(1)} %add_add_fusion.2), channel_id=1, source_target_pairs={{0,16},{4,20},{8,24},{12,28},{16,0},{20,4},{24,8},{28,12},{32,48},... | collective-permute-start | bytes 135176 | tf_op jit(solution)/shard_map/ppermute | solution.py:326
  48.1 5.2 %collective-permute-start.13 = (f32[88,128]{1,0:T(8,128)S(1)}, f32[88,128]{1,0:T(8,128)S(1)}, u32[]{:S(2)}, u32[]{:S(2)}) collective-permute-start(f32[88,128]{1,0:T(8,128)S(1)} %add_add_fusion.1), channel_id=1, source_target_pairs={{0,3},{1,0},{2,1},{3,2},{4,7},{5,4},{6,5},{7,6},{8,11},{9,8},{10,9... | collective-permute-start | bytes 135176 | tf_op jit(solution)/shard_map/ppermute | solution.py:326
  51.1 5.7 %collective-permute-start.12 = (f32[88,128]{1,0:T(8,128)S(1)}, f32[88,128]{1,0:T(8,128)S(1)}, u32[]{:S(2)}, u32[]{:S(2)}) collective-permute-start(f32[88,128]{1,0:T(8,128)S(1)} %add_add_fusion.1), channel_id=1, source_target_pairs={{0,1},{1,2},{2,3},{3,0},{4,5},{5,6},{6,7},{7,4},{8,9},{9,10},{10,1... | collective-permute-start | bytes 135176 | tf_op jit(solution)/shard_map/ppermute | solution.py:326
  51.1 5.7 %collective-permute-start.11 = (f32[88,128]{1,0:T(8,128)S(1)}, f32[88,128]{1,0:T(8,128)S(1)}, u32[]{:S(2)}, u32[]{:S(2)}) collective-permute-start(f32[88,128]{1,0:T(8,128)S(1)} %add_add_fusion.1), channel_id=1, source_target_pairs={{0,2},{1,3},{2,0},{3,1},{4,6},{5,7},{6,4},{7,5},{8,10},{9,11},{10,... | collective-permute-start | bytes 135176 | tf_op jit(solution)/shard_map/ppermute | solution.py:326

commit v6 on v5

--- a/solution.py
+++ b/solution.py
@@ -107,52 +107,63 @@
     return up + down
 
 
-def normal_kernel(
-    edges, sums, turned, material, z_low, z_high, y_low, y_high, packed, gram
+def add_plane(gram, scale, below, here, above, before, after, keeps):
+    height, columns, width = here.shape
+    lane = lax.broadcasted_iota(jnp.int32, (columns, width), 1)
+    first, last = lane == 0, lane == width - 1
+    middle = [before.astype(F32) * keeps[2], here[0].astype(F32)]
+    highs, lows = [], []
+    for y in range(height):
+        if y == height - 1:
+            middle.append(after.astype(F32) * keeps[3])
+        else:
+            middle.append(here[y + 1].astype(F32))
+        row = middle[y + 1]
+        under, over = below[y].astype(F32), above[y].astype(F32)
+        if keeps[0] is not None:
+            under = under * keeps[0]
+        if keeps[1] is not None:
+            over = over * keeps[1]
+        beside = under + over + (middle[y] + middle[y + 2])
+        beside = beside + beside_in_row(row, first, last)
+        image = scale[y : y + 1, :] * row - beside
+        rounded = image.astype(BF16)
+        highs.append(rounded)
+        lows.append((image - rounded.astype(F32)).astype(BF16))
+    gap = jnp.zeros((16 - columns % 16, height * width), BF16)
+    rounded = jnp.concatenate(highs, 1)
+    both = jnp.concatenate([rounded, gap, jnp.concatenate(lows, 1)], 0)
+    part = lax.dot_general(both, rounded, NT, preferred_element_type=F32)
+    gram[:columns] += part[:columns]
+    gram[columns:] += part[both.shape[0] - columns :]
+
+
+def inner_kernel(edges, turned, material, y_low, y_high, gram):
+    depth = turned.shape[0]
+    gram[...] = jnp.zeros_like(gram)
+    keeps = (None, None, edges[2].astype(F32), edges[3].astype(F32))
+
+    def step(z, _):
+        planes = (turned.at[z - 1], turned.at[z], turned.at[z + 1])
+        add_plane(gram, coefficient(material[z]), *planes, y_low[z], y_high[z], keeps)
+        return 0
+
+    lax.fori_loop(1, depth - 1, step, 0)
+
+
+def outer_kernel(
+    edges, sums, part, turned, material, z_low, z_high, y_low, y_high, packed, gram
 ):
     depth, height, columns, width = turned.shape
     count = sums.shape[0] - columns
-    gram[...] = jnp.zeros_like(gram)
-    lane = lax.broadcasted_iota(jnp.int32, (columns, width), 1)
-    first, last = lane == 0, lane == width - 1
+    gram[...] = part[...]
     inside = [edges[i].astype(F32) for i in range(4)]
-    gap = jnp.zeros((16 - columns % 16, height * width), BF16)
-
-    def plane(z, below, here, above, keep_below=None, keep_above=None):
-        scale = coefficient(material[z])
-        middle = [y_low[z].astype(F32) * inside[2], here[0].astype(F32)]
-        highs, lows = [], []
-        for y in range(height):
-            if y == height - 1:
-                middle.append(y_high[z].astype(F32) * inside[3])
-            else:
-                middle.append(here[y + 1].astype(F32))
-            row = middle[y + 1]
-            under, over = below[y].astype(F32), above[y].astype(F32)
-            if keep_below is not None:
-                under = under * keep_below
-            if keep_above is not None:
-                over = over * keep_above
-            beside = under + over + (middle[y] + middle[y + 2])
-            beside = beside + beside_in_row(row, first, last)
-            image = scale[y : y + 1, :] * row - beside
-            rounded = image.astype(BF16)
-            highs.append(rounded)
-            lows.append((image - rounded.astype(F32)).astype(BF16))
-        rounded = jnp.concatenate(highs, 1)
-        both = jnp.concatenate([rounded, gap, jnp.concatenate(lows, 1)], 0)
-        part = lax.dot_general(both, rounded, NT, preferred_element_type=F32)
-        gram[:columns] += part[:columns]
-        gram[columns:] += part[both.shape[0] - columns :]
-
-    def step(z, _):
-        plane(z, turned.at[z - 1], turned.at[z], turned.at[z + 1])
-        return 0
-
-    lax.fori_loop(1, depth - 1, step, 0)
-    plane(0, z_low, turned.at[0], turned.at[1], keep_below=inside[0])
-    end = depth - 1
-    plane(end, turned.at[end - 1], turned.at[end], z_high, keep_above=inside[1])
+    for z, planes, keeps in (
+        (0, (z_low, turned.at[0], turned.at[1]), (inside[0], None)),
+        (depth - 1, (turned.at[depth - 2], turned.at[depth - 1], z_high), (None, inside[1])),
+    ):
+        keeps = keeps + (inside[2], inside[3])
+        add_plane(gram, coefficient(material[z]), *planes, y_low[z], y_high[z], keeps)
     side = jnp.zeros((columns, 128 - columns), F32)
     foot = jnp.zeros((128 - columns, 128), F32)
     cross = jnp.concatenate([gram[columns:], side], 1)
@@ -322,22 +333,13 @@
 
 
 def device_sum(value):
-    def shifted(axis, perm):
-        return lax.ppermute(value, axis, perm)
-
-    slabs = range(32)
-    value = value + shifted("slab", [(i, i ^ 1) for i in slabs])
-    for stride in (8, 2, 0):
-        if stride:
-            def move(i, d):
-                place = (i // stride) % 4
-                return i + ((place + d) % 4 - place) * stride
-            axis, perms = "slab", [[(i, move(i, d)) for i in slabs] for d in (1, 2, 3)]
-        else:
-            axis = "pencil"
-            perms = [[(i, (i + d) % 4) for i in range(4)] for d in (1, 2, 3)]
-        left, opposite, right = [shifted(axis, perm) for perm in perms]
-        value = (value + opposite) + (left + right)
+    def exchanged(axis, size, distance):
+        return lax.ppermute(value, axis, [(i, i ^ distance) for i in range(size)])
+
+    value = value + exchanged("slab", 32, 1)
+    for axis, size, stride in (("slab", 32, 8), ("slab", 32, 2), ("pencil", 4, 1)):
+        near, opposite, far = [exchanged(axis, size, d * stride) for d in (1, 2, 3)]
+        value = (value + opposite) + (near + far)
     return value
 
 
@@ -394,15 +396,25 @@
     slab, pencil = lax.axis_index("slab"), lax.axis_index("pencil")
     inner = (slab > 0, slab < slabs - 1, pencil > 0, pencil < pencils - 1)
     edges = jnp.stack(inner).astype(jnp.int32)
+    grams = jax.ShapeDtypeStruct((2 * columns, columns), F32)
+    part = pl.pallas_call(
+        inner_kernel,
+        in_specs=[whole(pltpu.SMEM)] + [whole()] * 4,
+        out_specs=whole(),
+        out_shape=grams,
+        compiler_params=pltpu.CompilerParams(vmem_limit_bytes=16 * MIB),
+        cost_estimate=pl.CostEstimate(flops=10**10, bytes_accessed=10**7, transcendentals=0),
+        name="inner",
+    )(edges, turned, material, y_low, y_high)
     packed = pl.pallas_call(
-        normal_kernel,
-        in_specs=[whole(pltpu.SMEM)] + [whole()] * 7,
+        outer_kernel,
+        in_specs=[whole(pltpu.SMEM)] + [whole()] * 8,
         out_specs=whole(),
         out_shape=jax.ShapeDtypeStruct((columns, 128), F32),
-        scratch_shapes=[pltpu.VMEM((2 * columns, columns), F32)],
+        scratch_shapes=[pltpu.VMEM(grams.shape, F32)],
         compiler_params=pltpu.CompilerParams(vmem_limit_bytes=16 * MIB),
-        name="normal",
-    )(edges, sums, turned, material, *faces)
+        name="outer",
+    )(edges, sums, part, turned, material, *faces)
     packed = device_sum(packed)
     grid_shape = (count, depth, height, width)
     return pl.pallas_call(

time: 69.9 us -> 68.9 us (0.986)
  waiting for transfers between devices: 13.4 us -> 9.22 us
  starting transfers between devices: 21 us -> 23.1 us
    ppermute x10, waiting for transfers between devices: 13.4 us -> 9.21 us  [exchanged(): return lax.ppermute(value, axis, [(i, i ^ distance) for i in range(size)])]
    ppermute x10, starting transfers between devices: 11.9 us -> 14.4 us  [exchanged(): return lax.ppermute(value, axis, [(i, i ^ distance) for i in range(size)])]
    pallas_call x1 -> x2, Pallas kernels: 9.49 us -> 10.1 us  [the longest x1 7.22 us: local(): pl.pallas_call(inner_kernel, in_specs=[whole(pltpu.SMEM)] + [whole()] * 4...]
  transfers between devices with their start and end apart: 14 -> 14, of which waited for: 8 -> 10; matrix products, arithmetic and copies ran while one was open for 0% -> 0% of each run, Pallas kernels for 11% -> 22%
where the time goes in v6:
time: 68.9 us; the launch traced here: 68.1 us
  Pallas kernels  34.8 us (51%)
  starting transfers between devices  23.1 us (34%)
  waiting for transfers between devices  9.22 us (13%)
  between operations  0.89 us (1%)
    ppermute x10, starting transfers between devices, exchanged(): return lax.ppermute(value, axis, [(i, i ^ distance) for i in range(size)])  14.4 us
    pallas_call x1, Pallas kernels, local(): pl.pallas_call(update_kernel, in_specs=[whole(pltpu.SMEM)] + [whole()] *...  12.7 us
    ppermute x10, waiting for transfers between devices, exchanged(): return lax.ppermute(value, axis, [(i, i ^ distance) for i in range(size)])  9.21 us
    pallas_call x1, Pallas kernels, local(): pl.pallas_call(gram_kernel, in_specs=[whole(pltpu.SMEM), whole(pltpu.HBM)...  7.74 us
    pallas_call x1, Pallas kernels, local(): pl.pallas_call(inner_kernel, in_specs=[whole(pltpu.SMEM)] + [whole()] * 4...  7.22 us
    ppermute x2, starting transfers between devices, neighbours(): lax.ppermute(low_face, axis, down)  6.91 us
    pallas_call x1, Pallas kernels, local(): pl.pallas_call(face_kernel, in_specs=[whole(pltpu.HBM)], out_specs=[whole...  4.27 us
    pallas_call x1, Pallas kernels, local(): pl.pallas_call(outer_kernel, in_specs=[whole(pltpu.SMEM)] + [whole()] * 8...  2.89 us
  transfers between devices with their start and end apart: 14, of which 10 were waited for; matrix products, arithmetic and copies ran while one was open for 0% of the time, Pallas kernels for 22%

profile of v6, /device:TPU:0, one launch (start us, length us, event | category | flops | bytes accessed | tf_op | source)
XLA Modules:
  0.0 68.1 jit_solution(16876114038648608188)
XLA Ops:
  0.6 0.0 copy-start.1
  0.6 4.3 %faces.1 = (bf16[32,88,128]{2,1,0:T(8,128)(2,1)S(1)}, bf16[32,88,128]{2,1,0:T(8,128)(2,1)S(1)}, bf16[8,88,128]{2,1,0:T(8,128)(2,1)S(1)}, bf16[8,88,128]{2,1,0:T(8,128)(2,1)}) custom-call(bf16[88,8,32,128]{3,2,1,0:T(8,128)(2,1)} %basis.3), custom_call_target="tpu_custom_call" | custom-call | tf_op jit(solution)/shard_map/faces/pallas_call | solution.py:362
  4.9 1.7 %collective-permute-start = (bf16[8,88,128]{2,1,0:T(8,128)(2,1)}, bf16[8,88,128]{2,1,0:T(8,128)(2,1)S(1)}, u32[]{:S(2)}, u32[]{:S(2)}) collective-permute-start(bf16[8,88,128]{2,1,0:T(8,128)(2,1)} %get-tuple-element.10), channel_id=1, source_target_pairs={{0,1},{1,2},{2,3},{3,0},{4,5},{5,6},{6,7},{7,4},{8,9},{9,10},{10,1... | collective-permute-start | bytes 540680 | tf_op jit(solution)/shard_map/ppermute | solution.py:358
  6.6 1.6 %collective-permute-start.1 = (bf16[8,88,128]{2,1,0:T(8,128)(2,1)S(1)}, bf16[8,88,128]{2,1,0:T(8,128)(2,1)S(1)}, u32[]{:S(2)}, u32[]{:S(2)}) collective-permute-start(bf16[8,88,128]{2,1,0:T(8,128)(2,1)S(1)} %get-tuple-element.11), channel_id=1, source_target_pairs={{1,0},{2,1},{3,2},{0,3},{5,4},{6,5},{7,6},{4,7},{9,8},{10,9},{11,1... | collective-permute-start | bytes 540680 | tf_op jit(solution)/shard_map/ppermute | solution.py:358
  8.2 0.0 collective-permute-start.2
  8.2 5.3 %collective-permute-start.3 = (bf16[32,88,128]{2,1,0:T(8,128)(2,1)S(1)}, bf16[32,88,128]{2,1,0:T(8,128)(2,1)S(1)}, u32[]{:S(2)}, u32[]{:S(2)}) collective-permute-start(bf16[32,88,128]{2,1,0:T(8,128)(2,1)S(1)} %get-tuple-element.13), channel_id=1, source_target_pairs={{4,0},{8,4},{12,8},{16,12},{20,16},{24,20},{28,24},{32,28},{36,32}... | collective-permute-start | bytes 2162696 | tf_op jit(solution)/shard_map/ppermute | solution.py:358
  13.6 0.1 add_convert_fusion.edges
  13.6 0.0 copy-done.1
  13.6 0.0 copy-start
  13.6 7.7 %gram.1 = (f32[120,88]{1,0:T(8,128)S(1)}, bf16[8,32,88,128]{3,2,1,0:T(8,128)(2,1)S(1)}) custom-call(s32[32]{0:T(128)S(1)} %copy-done.1, bf16[88,8,32,128]{3,2,1,0:T(8,128)(2,1)} %image.1, bf16[88,8,32,128]{3,2,1,0:T(8,128)(2,1)} %basis.3), custom_call_target="tpu_custom_call" | custom-call | flops 2000000000 | bytes 17000000 | tf_op jit(solution)/shard_map/gram/pallas_call | solution.py:376
  21.4 0.0 collective-permute-done.y_low
  21.4 0.0 collective-permute-done.1.y_high
  21.4 0.0 copy-done
  21.4 7.2 %inner.1.part = f32[176,88]{1,0:T(8,128)S(1)} custom-call(s32[4]{0:T(128)S(1)} %add_convert_fusion.edges, bf16[8,32,88,128]{3,2,1,0:T(8,128)(2,1)S(1)} %get-tuple-element.9.turned, s32[8,32,128]{2,1,0:T(8,128)S(1)} %copy-done, bf16[8,88,128]{2,1,0:T(8,128)(2,1)S(1)} %collective-permute-done.y_low, bf16[8,88,128]{2,1,0:T(8,128)(2,1)S(1)} %collective-permute-done.1.y_high), custom_call_target="tpu_custom_call" | custom-call | flops 10000000000 | bytes 10000000 | tf_op jit(solution)/shard_map/inner/pallas_call | solution.py:400
  28.6 0.0 collective-permute-done.2.z_low
  28.6 0.0 collective-permute-done.3.z_high
  28.7 2.9 %outer.1 = f32[88,128]{1,0:T(8,128)S(1)} custom-call(s32[4]{0:T(128)S(1)} %add_convert_fusion.edges, f32[120,88]{1,0:T(8,128)S(1)} %get-tuple-element.8.sums, f32[176,88]{1,0:T(8,128)S(1)} %inner.1.part, bf16[8,32,88,128]{3,2,1,0:T(8,128)(2,1)S(1)} %get-tuple-element.9.turned, s32[8,32,128]{2,1,0:T(8,128)S(1)} %copy-done, ...), custom_call_target="tpu_custom_call" | custom-call | tf_op jit(solution)/shard_map/outer/pallas_call | solution.py:409
  31.6 0.1 collective-permute-start.4
  31.6 1.2 %collective-permute-done.4 = f32[88,128]{1,0:T(8,128)S(1)} collective-permute-done((f32[88,128]{1,0:T(8,128)S(1)}, f32[88,128]{1,0:T(8,128)S(1)}, u32[]{:S(2)}, u32[]{:S(2)}) %collective-permute-start.4) | collective-permute-done | bytes 45088 | tf_op jit(solution)/shard_map/ppermute | solution.py:337
  32.9 1.4 %collective-permute-start.7 = (f32[88,128]{1,0:T(8,128)S(1)}, f32[88,128]{1,0:T(8,128)S(1)}, u32[]{:S(2)}, u32[]{:S(2)}) collective-permute-start(f32[88,128]{1,0:T(8,128)S(1)} %add.30), channel_id=1, source_target_pairs={{0,96},{4,100},{8,104},{12,108},{16,112},{20,116},{24,120},{28,124... | collective-permute-start | bytes 135176 | tf_op jit(solution)/shard_map/ppermute | solution.py:337
  34.3 0.2 collective-permute-start.6
  34.5 3.1 %collective-permute-start.5 = (f32[88,128]{1,0:T(8,128)S(1)}, f32[88,128]{1,0:T(8,128)S(1)}, u32[]{:S(2)}, u32[]{:S(2)}) collective-permute-start(f32[88,128]{1,0:T(8,128)S(1)} %add.30), channel_id=1, source_target_pairs={{0,64},{4,68},{8,72},{12,76},{16,80},{20,84},{24,88},{28,92},{32,9... | collective-permute-start | bytes 135176 | tf_op jit(solution)/shard_map/ppermute | solution.py:337
  37.6 0.6 collective-permute-done.7
  38.2 0.2 collective-permute-done.6
  38.4 1.8 %collective-permute-done.5 = f32[88,128]{1,0:T(8,128)S(1)} collective-permute-done((f32[88,128]{1,0:T(8,128)S(1)}, f32[88,128]{1,0:T(8,128)S(1)}, u32[]{:S(2)}, u32[]{:S(2)}) %collective-permute-start.5) | collective-permute-done | bytes 45088 | tf_op jit(solution)/shard_map/ppermute | solution.py:337
  40.2 1.9 %collective-permute-start.10 = (f32[88,128]{1,0:T(8,128)S(1)}, f32[88,128]{1,0:T(8,128)S(1)}, u32[]{:S(2)}, u32[]{:S(2)}) collective-permute-start(f32[88,128]{1,0:T(8,128)S(1)} %add_add_fusion.2), channel_id=1, source_target_pairs={{0,24},{4,28},{8,16},{12,20},{16,8},{20,12},{24,0},{28,4},{32,56},... | collective-permute-start | bytes 135176 | tf_op jit(solution)/shard_map/ppermute | solution.py:337
  42.1 0.0 collective-permute-start.9
  42.1 2.8 %collective-permute-start.8 = (f32[88,128]{1,0:T(8,128)S(1)}, f32[88,128]{1,0:T(8,128)S(1)}, u32[]{:S(2)}, u32[]{:S(2)}) collective-permute-start(f32[88,128]{1,0:T(8,128)S(1)} %add_add_fusion.2), channel_id=1, source_target_pairs={{0,16},{4,20},{8,24},{12,28},{16,0},{20,4},{24,8},{28,12},{32,48},... | collective-permute-start | bytes 135176 | tf_op jit(solution)/shard_map/ppermute | solution.py:337
  44.9 0.6 collective-permute-done.10
  45.5 0.6 collective-permute-done.9
  46.1 1.5 %collective-permute-done.8 = f32[88,128]{1,0:T(8,128)S(1)} collective-permute-done((f32[88,128]{1,0:T(8,128)S(1)}, f32[88,128]{1,0:T(8,128)S(1)}, u32[]{:S(2)}, u32[]{:S(2)}) %collective-permute-start.8) | collective-permute-done | bytes 45088 | tf_op jit(solution)/shard_map/ppermute | solution.py:337
  47.7 1.9 %collective-permute-start.13 = (f32[88,128]{1,0:T(8,128)S(1)}, f32[88,128]{1,0:T(8,128)S(1)}, u32[]{:S(2)}, u32[]{:S(2)}) collective-permute-start(f32[88,128]{1,0:T(8,128)S(1)} %add_add_fusion.1), channel_id=1, source_target_pairs={{0,3},{1,2},{2,1},{3,0},{4,7},{5,6},{6,5},{7,4},{8,11},{9,10},{10,... | collective-permute-start | bytes 135176 | tf_op jit(solution)/shard_map/ppermute | solution.py:337
  49.5 0.1 collective-permute-start.12
  49.7 2.8 %collective-permute-start.11 = (f32[88,128]{1,0:T(8,128)S(1)}, f32[88,128]{1,0:T(8,128)S(1)}, u32[]{:S(2)}, u32[]{:S(2)}) collective-permute-start(f32[88,128]{1,0:T(8,128)S(1)} %add_add_fusion.1), channel_id=1, source_target_pairs={{0,2},{1,3},{2,0},{3,1},{4,6},{5,7},{6,4},{7,5},{8,10},{9,11},{10,... | collective-permute-start | bytes 135176 | tf_op jit(solution)/shard_map/ppermute | solution.py:337
  52.4 0.6 collective-permute-done.13
  53.0 0.6 collective-permute-done.12
  53.6 1.6 %collective-permute-done.11 = f32[88,128]{1,0:T(8,128)S(1)} collective-permute-done((f32[88,128]{1,0:T(8,128)S(1)}, f32[88,128]{1,0:T(8,128)S(1)}, u32[]{:S(2)}, u32[]{:S(2)}) %collective-permute-start.11) | collective-permute-done | bytes 45088 | tf_op jit(solution)/shard_map/ppermute | solution.py:337
  55.3 12.7 %update.1 = (f32[32,8,32,128]{3,2,1,0:T(8,128)}, f32[32,8,32,128]{3,2,1,0:T(8,128)}) custom-call(s32[4]{0:T(128)S(1)} %add_convert_fusion.edges, f32[88,128]{1,0:T(8,128)S(1)} %add_add_fusion.packed, bf16[8,32,88,128]{3,2,1,0:T(8,128)(2,1)S(1)} %get-tuple-element.9.turned, s32[8,32,128]{2,1,0:T(8,128)S(1)} %copy-done, ...), custom_call_target="tpu_custom_call" | custom-call | tf_op jit(solution)/shard_map/update/pallas_call | solution.py:420
  (4 shorter events, 0.1 us)
Async XLA Ops:
  0.6 13.0 %copy-start.1 = (s32[32]{0:T(128)S(1)}, s32[32]{0:T(128)}, u32[]{:S(2)}) copy-start(s32[32]{0:T(128)} %picked.1) | copy-start | bytes 388
  4.9 16.5 %collective-permute-start = (bf16[8,88,128]{2,1,0:T(8,128)(2,1)}, bf16[8,88,128]{2,1,0:T(8,128)(2,1)S(1)}, u32[]{:S(2)}, u32[]{:S(2)}) collective-permute-start(bf16[8,88,128]{2,1,0:T(8,128)(2,1)} %get-tuple-element.10), channel_id=1, source_target_pairs={{0,1},{1,2},{2,3},{3,0},{4,5},{5,6},{6,7},{7,4},{8,9},{9,10},{10,1... | collective-permute-start | bytes 540680 | tf_op jit(solution)/shard_map/ppermute | solution.py:358
  6.6 14.8 %collective-permute-start.1 = (bf16[8,88,128]{2,1,0:T(8,128)(2,1)S(1)}, bf16[8,88,128]{2,1,0:T(8,128)(2,1)S(1)}, u32[]{:S(2)}, u32[]{:S(2)}) collective-permute-start(bf16[8,88,128]{2,1,0:T(8,128)(2,1)S(1)} %get-tuple-element.11), channel_id=1, source_target_pairs={{1,0},{2,1},{3,2},{0,3},{5,4},{6,5},{7,6},{4,7},{9,8},{10,9},{11,1... | collective-permute-start | bytes 540680 | tf_op jit(solution)/shard_map/ppermute | solution.py:358
  8.2 20.4 %collective-permute-start.2 = (bf16[32,88,128]{2,1,0:T(8,128)(2,1)S(1)}, bf16[32,88,128]{2,1,0:T(8,128)(2,1)S(1)}, u32[]{:S(2)}, u32[]{:S(2)}) collective-permute-start(bf16[32,88,128]{2,1,0:T(8,128)(2,1)S(1)} %get-tuple-element.12), channel_id=1, source_target_pairs={{0,4},{4,8},{8,12},{12,16},{16,20},{20,24},{24,28},{28,32},{32,36}... | collective-permute-start | bytes 2162696 | tf_op jit(solution)/shard_map/ppermute | solution.py:358
  8.2 20.4 %collective-permute-start.3 = (bf16[32,88,128]{2,1,0:T(8,128)(2,1)S(1)}, bf16[32,88,128]{2,1,0:T(8,128)(2,1)S(1)}, u32[]{:S(2)}, u32[]{:S(2)}) collective-permute-start(bf16[32,88,128]{2,1,0:T(8,128)(2,1)S(1)} %get-tuple-element.13), channel_id=1, source_target_pairs={{4,0},{8,4},{12,8},{16,12},{20,16},{24,20},{28,24},{32,28},{36,32}... | collective-permute-start | bytes 2162696 | tf_op jit(solution)/shard_map/ppermute | solution.py:358
  13.6 7.8 %copy-start = (s32[8,32,128]{2,1,0:T(8,128)S(1)}, s32[8,32,128]{2,1,0:T(8,128)}, u32[]{:S(2)}) copy-start(s32[8,32,128]{2,1,0:T(8,128)} %material.5) | copy-start | bytes 393220
  31.6 1.3 %collective-permute-start.4 = (f32[88,128]{1,0:T(8,128)S(1)}, f32[88,128]{1,0:T(8,128)S(1)}, u32[]{:S(2)}, u32[]{:S(2)}) collective-permute-start(f32[88,128]{1,0:T(8,128)S(1)} %outer.1), channel_id=1, source_target_pairs={{0,4},{4,0},{8,12},{12,8},{16,20},{20,16},{24,28},{28,24},{32,36},... | collective-permute-start | bytes 135176 | tf_op jit(solution)/shard_map/ppermute | solution.py:337
  32.9 5.3 %collective-permute-start.7 = (f32[88,128]{1,0:T(8,128)S(1)}, f32[88,128]{1,0:T(8,128)S(1)}, u32[]{:S(2)}, u32[]{:S(2)}) collective-permute-start(f32[88,128]{1,0:T(8,128)S(1)} %add.30), channel_id=1, source_target_pairs={{0,96},{4,100},{8,104},{12,108},{16,112},{20,116},{24,120},{28,124... | collective-permute-start | bytes 135176 | tf_op jit(solution)/shard_map/ppermute | solution.py:337
  34.3 4.1 %collective-permute-start.6 = (f32[88,128]{1,0:T(8,128)S(1)}, f32[88,128]{1,0:T(8,128)S(1)}, u32[]{:S(2)}, u32[]{:S(2)}) collective-permute-start(f32[88,128]{1,0:T(8,128)S(1)} %add.30), channel_id=1, source_target_pairs={{0,32},{4,36},{8,40},{12,44},{16,48},{20,52},{24,56},{28,60},{32,0... | collective-permute-start | bytes 135176 | tf_op jit(solution)/shard_map/ppermute | solution.py:337
  34.5 5.6 %collective-permute-start.5 = (f32[88,128]{1,0:T(8,128)S(1)}, f32[88,128]{1,0:T(8,128)S(1)}, u32[]{:S(2)}, u32[]{:S(2)}) collective-permute-start(f32[88,128]{1,0:T(8,128)S(1)} %add.30), channel_id=1, source_target_pairs={{0,64},{4,68},{8,72},{12,76},{16,80},{20,84},{24,88},{28,92},{32,9... | collective-permute-start | bytes 135176 | tf_op jit(solution)/shard_map/ppermute | solution.py:337
  40.2 5.3 %collective-permute-start.10 = (f32[88,128]{1,0:T(8,128)S(1)}, f32[88,128]{1,0:T(8,128)S(1)}, u32[]{:S(2)}, u32[]{:S(2)}) collective-permute-start(f32[88,128]{1,0:T(8,128)S(1)} %add_add_fusion.2), channel_id=1, source_target_pairs={{0,24},{4,28},{8,16},{12,20},{16,8},{20,12},{24,0},{28,4},{32,56},... | collective-permute-start | bytes 135176 | tf_op jit(solution)/shard_map/ppermute | solution.py:337
  42.1 4.0 %collective-permute-start.9 = (f32[88,128]{1,0:T(8,128)S(1)}, f32[88,128]{1,0:T(8,128)S(1)}, u32[]{:S(2)}, u32[]{:S(2)}) collective-permute-start(f32[88,128]{1,0:T(8,128)S(1)} %add_add_fusion.2), channel_id=1, source_target_pairs={{0,8},{4,12},{8,0},{12,4},{16,24},{20,28},{24,16},{28,20},{32,40},... | collective-permute-start | bytes 135176 | tf_op jit(solution)/shard_map/ppermute | solution.py:337
  42.1 5.6 %collective-permute-start.8 = (f32[88,128]{1,0:T(8,128)S(1)}, f32[88,128]{1,0:T(8,128)S(1)}, u32[]{:S(2)}, u32[]{:S(2)}) collective-permute-start(f32[88,128]{1,0:T(8,128)S(1)} %add_add_fusion.2), channel_id=1, source_target_pairs={{0,16},{4,20},{8,24},{12,28},{16,0},{20,4},{24,8},{28,12},{32,48},... | collective-permute-start | bytes 135176 | tf_op jit(solution)/shard_map/ppermute | solution.py:337
  47.7 5.3 %collective-permute-start.13 = (f32[88,128]{1,0:T(8,128)S(1)}, f32[88,128]{1,0:T(8,128)S(1)}, u32[]{:S(2)}, u32[]{:S(2)}) collective-permute-start(f32[88,128]{1,0:T(8,128)S(1)} %add_add_fusion.1), channel_id=1, source_target_pairs={{0,3},{1,2},{2,1},{3,0},{4,7},{5,6},{6,5},{7,4},{8,11},{9,10},{10,... | collective-permute-start | bytes 135176 | tf_op jit(solution)/shard_map/ppermute | solution.py:337
  49.5 4.0 %collective-permute-start.12 = (f32[88,128]{1,0:T(8,128)S(1)}, f32[88,128]{1,0:T(8,128)S(1)}, u32[]{:S(2)}, u32[]{:S(2)}) collective-permute-start(f32[88,128]{1,0:T(8,128)S(1)} %add_add_fusion.1), channel_id=1, source_target_pairs={{0,1},{1,0},{2,3},{3,2},{4,5},{5,4},{6,7},{7,6},{8,9},{9,8},{10,11... | collective-permute-start | bytes 135176 | tf_op jit(solution)/shard_map/ppermute | solution.py:337
  49.7 5.6 %collective-permute-start.11 = (f32[88,128]{1,0:T(8,128)S(1)}, f32[88,128]{1,0:T(8,128)S(1)}, u32[]{:S(2)}, u32[]{:S(2)}) collective-permute-start(f32[88,128]{1,0:T(8,128)S(1)} %add_add_fusion.1), channel_id=1, source_target_pairs={{0,2},{1,3},{2,0},{3,1},{4,6},{5,7},{6,4},{7,5},{8,10},{9,11},{10,... | collective-permute-start | bytes 135176 | tf_op jit(solution)/shard_map/ppermute | solution.py:337

commit v7 on v6

--- a/solution.py
+++ b/solution.py
@@ -112,7 +112,7 @@
     lane = lax.broadcasted_iota(jnp.int32, (columns, width), 1)
     first, last = lane == 0, lane == width - 1
     middle = [before.astype(F32) * keeps[2], here[0].astype(F32)]
-    highs, lows = [], []
+    images = []
     for y in range(height):
         if y == height - 1:
             middle.append(after.astype(F32) * keeps[3])
@@ -126,16 +126,9 @@
             over = over * keeps[1]
         beside = under + over + (middle[y] + middle[y + 2])
         beside = beside + beside_in_row(row, first, last)
-        image = scale[y : y + 1, :] * row - beside
-        rounded = image.astype(BF16)
-        highs.append(rounded)
-        lows.append((image - rounded.astype(F32)).astype(BF16))
-    gap = jnp.zeros((16 - columns % 16, height * width), BF16)
-    rounded = jnp.concatenate(highs, 1)
-    both = jnp.concatenate([rounded, gap, jnp.concatenate(lows, 1)], 0)
-    part = lax.dot_general(both, rounded, NT, preferred_element_type=F32)
-    gram[:columns] += part[:columns]
-    gram[columns:] += part[both.shape[0] - columns :]
+        images.append((scale[y : y + 1, :] * row - beside).astype(BF16))
+    images = jnp.concatenate(images, 1)
+    gram[...] += lax.dot_general(images, images, NT, preferred_element_type=F32)
 
 
 def inner_kernel(edges, turned, material, y_low, y_high, gram):
@@ -165,10 +158,7 @@
         keeps = keeps + (inside[2], inside[3])
         add_plane(gram, coefficient(material[z]), *planes, y_low[z], y_high[z], keeps)
     side = jnp.zeros((columns, 128 - columns), F32)
-    foot = jnp.zeros((128 - columns, 128), F32)
-    cross = jnp.concatenate([gram[columns:], side], 1)
-    cross_t = jnp.concatenate([cross, foot], 0).T[:columns]
-    normal = jnp.concatenate([gram[:columns], side], 1) + cross + cross_t
+    normal = jnp.concatenate([gram[...], side], 1)
     col = lax.broadcasted_iota(jnp.int32, (columns, 128), 1)
     line = lax.broadcasted_iota(jnp.int32, (columns, 128), 0)
     diagonal = jnp.sum(jnp.where(line == col, normal, 0.0), axis=1, keepdims=True)
@@ -209,10 +199,10 @@
             for j in range(k + 1, 8):
                 heads[i][j] = heads[i][j] - factor * heads[k][j]
     for i in followers:
-        block = blocks[i]
-        for j in range(8):
-            block = block - spread(blocks[i], base + j) * rows[j]
-        blocks[i] = block
+        terms = [spread(blocks[i], base + j) * rows[j] for j in range(8)]
+        while len(terms) > 1:
+            terms = [a + b for a, b in zip(terms[::2], terms[1::2])]
+        blocks[i] = blocks[i] - terms[0]
     return rows, forward, pivots
 
 
@@ -396,7 +386,7 @@
     slab, pencil = lax.axis_index("slab"), lax.axis_index("pencil")
     inner = (slab > 0, slab < slabs - 1, pencil > 0, pencil < pencils - 1)
     edges = jnp.stack(inner).astype(jnp.int32)
-    grams = jax.ShapeDtypeStruct((2 * columns, columns), F32)
+    grams = jax.ShapeDtypeStruct((columns, columns), F32)
     part = pl.pallas_call(
         inner_kernel,
         in_specs=[whole(pltpu.SMEM)] + [whole()] * 4,

time: 68.9 us -> 67.6 us (0.981)
  Pallas kernels: 34.8 us -> 33.5 us
    pallas_call x1, Pallas kernels: 7.22 us -> 6.25 us  [local(): pl.pallas_call(inner_kernel, in_specs=[whole(pltpu.SMEM)] + [whole()] * 4...]
  transfers between devices with their start and end apart: 14 -> 14, of which waited for: 10 -> 10; matrix products, arithmetic and copies ran while one was open for 0% -> 0% of each run, Pallas kernels for 22% -> 21%
where the time goes in v7:
time: 67.6 us; the launch traced here: 66.8 us
  Pallas kernels  33.5 us (50%)
  starting transfers between devices  23.1 us (34%)
  waiting for transfers between devices  9.23 us (14%)
  between operations  0.89 us (1%)
    ppermute x10, starting transfers between devices, exchanged(): return lax.ppermute(value, axis, [(i, i ^ distance) for i in range(size)])  14.4 us
    pallas_call x1, Pallas kernels, local(): pl.pallas_call(update_kernel, in_specs=[whole(pltpu.SMEM)] + [whole()] *...  12.7 us
    ppermute x10, waiting for transfers between devices, exchanged(): return lax.ppermute(value, axis, [(i, i ^ distance) for i in range(size)])  9.22 us
    pallas_call x1, Pallas kernels, local(): pl.pallas_call(gram_kernel, in_specs=[whole(pltpu.SMEM), whole(pltpu.HBM)...  7.74 us
    ppermute x2, starting transfers between devices, neighbours(): lax.ppermute(low_face, axis, down)  6.91 us
    pallas_call x1, Pallas kernels, local(): pl.pallas_call(inner_kernel, in_specs=[whole(pltpu.SMEM)] + [whole()] * 4...  6.25 us
    pallas_call x1, Pallas kernels, local(): pl.pallas_call(face_kernel, in_specs=[whole(pltpu.HBM)], out_specs=[whole...  4.27 us
    pallas_call x1, Pallas kernels, local(): pl.pallas_call(outer_kernel, in_specs=[whole(pltpu.SMEM)] + [whole()] * 8...  2.49 us
  transfers between devices with their start and end apart: 14, of which 10 were waited for; matrix products, arithmetic and copies ran while one was open for 0% of the time, Pallas kernels for 21%

profile of v7, /device:TPU:0, one launch (start us, length us, event | category | flops | bytes accessed | tf_op | source)
XLA Modules:
  0.0 66.8 jit_solution(14152273227383341817)
XLA Ops:
  0.6 0.0 copy-start.1
  0.6 4.3 %faces.1 = (bf16[32,88,128]{2,1,0:T(8,128)(2,1)S(1)}, bf16[32,88,128]{2,1,0:T(8,128)(2,1)S(1)}, bf16[8,88,128]{2,1,0:T(8,128)(2,1)S(1)}, bf16[8,88,128]{2,1,0:T(8,128)(2,1)}) custom-call(bf16[88,8,32,128]{3,2,1,0:T(8,128)(2,1)} %basis.3), custom_call_target="tpu_custom_call" | custom-call | tf_op jit(solution)/shard_map/faces/pallas_call | solution.py:352
  4.9 1.7 %collective-permute-start = (bf16[8,88,128]{2,1,0:T(8,128)(2,1)}, bf16[8,88,128]{2,1,0:T(8,128)(2,1)S(1)}, u32[]{:S(2)}, u32[]{:S(2)}) collective-permute-start(bf16[8,88,128]{2,1,0:T(8,128)(2,1)} %get-tuple-element.10), channel_id=1, source_target_pairs={{0,1},{1,2},{2,3},{3,0},{4,5},{5,6},{6,7},{7,4},{8,9},{9,10},{10,1... | collective-permute-start | bytes 540680 | tf_op jit(solution)/shard_map/ppermute | solution.py:348
  6.6 1.6 %collective-permute-start.1 = (bf16[8,88,128]{2,1,0:T(8,128)(2,1)S(1)}, bf16[8,88,128]{2,1,0:T(8,128)(2,1)S(1)}, u32[]{:S(2)}, u32[]{:S(2)}) collective-permute-start(bf16[8,88,128]{2,1,0:T(8,128)(2,1)S(1)} %get-tuple-element.11), channel_id=1, source_target_pairs={{1,0},{2,1},{3,2},{0,3},{5,4},{6,5},{7,6},{4,7},{9,8},{10,9},{11,1... | collective-permute-start | bytes 540680 | tf_op jit(solution)/shard_map/ppermute | solution.py:348
  8.2 0.0 collective-permute-start.2
  8.2 5.3 %collective-permute-start.3 = (bf16[32,88,128]{2,1,0:T(8,128)(2,1)S(1)}, bf16[32,88,128]{2,1,0:T(8,128)(2,1)S(1)}, u32[]{:S(2)}, u32[]{:S(2)}) collective-permute-start(bf16[32,88,128]{2,1,0:T(8,128)(2,1)S(1)} %get-tuple-element.13), channel_id=1, source_target_pairs={{4,0},{8,4},{12,8},{16,12},{20,16},{24,20},{28,24},{32,28},{36,32}... | collective-permute-start | bytes 2162696 | tf_op jit(solution)/shard_map/ppermute | solution.py:348
  13.6 0.1 add_convert_fusion.edges
  13.6 0.0 copy-done.1
  13.6 0.0 copy-start
  13.6 7.7 %gram.1 = (f32[120,88]{1,0:T(8,128)S(1)}, bf16[8,32,88,128]{3,2,1,0:T(8,128)(2,1)S(1)}) custom-call(s32[32]{0:T(128)S(1)} %copy-done.1, bf16[88,8,32,128]{3,2,1,0:T(8,128)(2,1)} %image.1, bf16[88,8,32,128]{3,2,1,0:T(8,128)(2,1)} %basis.3), custom_call_target="tpu_custom_call" | custom-call | flops 2000000000 | bytes 17000000 | tf_op jit(solution)/shard_map/gram/pallas_call | solution.py:366
  21.4 0.0 collective-permute-done.y_low
  21.4 0.0 collective-permute-done.1.y_high
  21.4 0.0 copy-done
  21.4 6.2 %inner.1.part = f32[88,88]{1,0:T(8,128)S(1)} custom-call(s32[4]{0:T(128)S(1)} %add_convert_fusion.edges, bf16[8,32,88,128]{3,2,1,0:T(8,128)(2,1)S(1)} %get-tuple-element.9.turned, s32[8,32,128]{2,1,0:T(8,128)S(1)} %copy-done, bf16[8,88,128]{2,1,0:T(8,128)(2,1)S(1)} %collective-permute-done.y_low, bf16[8,88,128]{2,1,0:T(8,128)(2,1)S(1)} %collective-permute-done.1.y_high), custom_call_target="tpu_custom_call" | custom-call | flops 10000000000 | bytes 10000000 | tf_op jit(solution)/shard_map/inner/pallas_call | solution.py:390
  27.7 0.0 collective-permute-done.2.z_low
  27.7 0.0 collective-permute-done.3.z_high
  27.7 2.5 %outer.1 = f32[88,128]{1,0:T(8,128)S(1)} custom-call(s32[4]{0:T(128)S(1)} %add_convert_fusion.edges, f32[120,88]{1,0:T(8,128)S(1)} %get-tuple-element.8.sums, f32[88,88]{1,0:T(8,128)S(1)} %inner.1.part, bf16[8,32,88,128]{3,2,1,0:T(8,128)(2,1)S(1)} %get-tuple-element.9.turned, s32[8,32,128]{2,1,0:T(8,128)S(1)} %copy-done, ...), custom_call_target="tpu_custom_call" | custom-call | tf_op jit(solution)/shard_map/outer/pallas_call | solution.py:399
  30.2 0.1 collective-permute-start.4
  30.3 1.2 %collective-permute-done.4 = f32[88,128]{1,0:T(8,128)S(1)} collective-permute-done((f32[88,128]{1,0:T(8,128)S(1)}, f32[88,128]{1,0:T(8,128)S(1)}, u32[]{:S(2)}, u32[]{:S(2)}) %collective-permute-start.4) | collective-permute-done | bytes 45088 | tf_op jit(solution)/shard_map/ppermute | solution.py:327
  31.5 1.4 %collective-permute-start.7 = (f32[88,128]{1,0:T(8,128)S(1)}, f32[88,128]{1,0:T(8,128)S(1)}, u32[]{:S(2)}, u32[]{:S(2)}) collective-permute-start(f32[88,128]{1,0:T(8,128)S(1)} %add.30), channel_id=1, source_target_pairs={{0,96},{4,100},{8,104},{12,108},{16,112},{20,116},{24,120},{28,124... | collective-permute-start | bytes 135176 | tf_op jit(solution)/shard_map/ppermute | solution.py:327
  32.9 0.2 collective-permute-start.6
  33.2 3.1 %collective-permute-start.5 = (f32[88,128]{1,0:T(8,128)S(1)}, f32[88,128]{1,0:T(8,128)S(1)}, u32[]{:S(2)}, u32[]{:S(2)}) collective-permute-start(f32[88,128]{1,0:T(8,128)S(1)} %add.30), channel_id=1, source_target_pairs={{0,64},{4,68},{8,72},{12,76},{16,80},{20,84},{24,88},{28,92},{32,9... | collective-permute-start | bytes 135176 | tf_op jit(solution)/shard_map/ppermute | solution.py:327
  36.3 0.6 collective-permute-done.7
  36.8 0.2 collective-permute-done.6
  37.0 1.8 %collective-permute-done.5 = f32[88,128]{1,0:T(8,128)S(1)} collective-permute-done((f32[88,128]{1,0:T(8,128)S(1)}, f32[88,128]{1,0:T(8,128)S(1)}, u32[]{:S(2)}, u32[]{:S(2)}) %collective-permute-start.5) | collective-permute-done | bytes 45088 | tf_op jit(solution)/shard_map/ppermute | solution.py:327
  38.8 1.9 %collective-permute-start.10 = (f32[88,128]{1,0:T(8,128)S(1)}, f32[88,128]{1,0:T(8,128)S(1)}, u32[]{:S(2)}, u32[]{:S(2)}) collective-permute-start(f32[88,128]{1,0:T(8,128)S(1)} %add_add_fusion.2), channel_id=1, source_target_pairs={{0,24},{4,28},{8,16},{12,20},{16,8},{20,12},{24,0},{28,4},{32,56},... | collective-permute-start | bytes 135176 | tf_op jit(solution)/shard_map/ppermute | solution.py:327
  40.7 0.0 collective-permute-start.9
  40.7 2.8 %collective-permute-start.8 = (f32[88,128]{1,0:T(8,128)S(1)}, f32[88,128]{1,0:T(8,128)S(1)}, u32[]{:S(2)}, u32[]{:S(2)}) collective-permute-start(f32[88,128]{1,0:T(8,128)S(1)} %add_add_fusion.2), channel_id=1, source_target_pairs={{0,16},{4,20},{8,24},{12,28},{16,0},{20,4},{24,8},{28,12},{32,48},... | collective-permute-start | bytes 135176 | tf_op jit(solution)/shard_map/ppermute | solution.py:327
  43.6 0.6 collective-permute-done.10
  44.1 0.6 collective-permute-done.9
  44.8 1.5 %collective-permute-done.8 = f32[88,128]{1,0:T(8,128)S(1)} collective-permute-done((f32[88,128]{1,0:T(8,128)S(1)}, f32[88,128]{1,0:T(8,128)S(1)}, u32[]{:S(2)}, u32[]{:S(2)}) %collective-permute-start.8) | collective-permute-done | bytes 45088 | tf_op jit(solution)/shard_map/ppermute | solution.py:327
  46.3 1.9 %collective-permute-start.13 = (f32[88,128]{1,0:T(8,128)S(1)}, f32[88,128]{1,0:T(8,128)S(1)}, u32[]{:S(2)}, u32[]{:S(2)}) collective-permute-start(f32[88,128]{1,0:T(8,128)S(1)} %add_add_fusion.1), channel_id=1, source_target_pairs={{0,3},{1,2},{2,1},{3,0},{4,7},{5,6},{6,5},{7,4},{8,11},{9,10},{10,... | collective-permute-start | bytes 135176 | tf_op jit(solution)/shard_map/ppermute | solution.py:327
  48.2 0.1 collective-permute-start.12
  48.3 2.8 %collective-permute-start.11 = (f32[88,128]{1,0:T(8,128)S(1)}, f32[88,128]{1,0:T(8,128)S(1)}, u32[]{:S(2)}, u32[]{:S(2)}) collective-permute-start(f32[88,128]{1,0:T(8,128)S(1)} %add_add_fusion.1), channel_id=1, source_target_pairs={{0,2},{1,3},{2,0},{3,1},{4,6},{5,7},{6,4},{7,5},{8,10},{9,11},{10,... | collective-permute-start | bytes 135176 | tf_op jit(solution)/shard_map/ppermute | solution.py:327
  51.1 0.6 collective-permute-done.13
  51.6 0.6 collective-permute-done.12
  52.2 1.6 %collective-permute-done.11 = f32[88,128]{1,0:T(8,128)S(1)} collective-permute-done((f32[88,128]{1,0:T(8,128)S(1)}, f32[88,128]{1,0:T(8,128)S(1)}, u32[]{:S(2)}, u32[]{:S(2)}) %collective-permute-start.11) | collective-permute-done | bytes 45088 | tf_op jit(solution)/shard_map/ppermute | solution.py:327
  53.9 12.7 %update.1 = (f32[32,8,32,128]{3,2,1,0:T(8,128)}, f32[32,8,32,128]{3,2,1,0:T(8,128)}) custom-call(s32[4]{0:T(128)S(1)} %add_convert_fusion.edges, f32[88,128]{1,0:T(8,128)S(1)} %add_add_fusion.packed, bf16[8,32,88,128]{3,2,1,0:T(8,128)(2,1)S(1)} %get-tuple-element.9.turned, s32[8,32,128]{2,1,0:T(8,128)S(1)} %copy-done, ...), custom_call_target="tpu_custom_call" | custom-call | tf_op jit(solution)/shard_map/update/pallas_call | solution.py:410
  (4 shorter events, 0.1 us)
Async XLA Ops:
  0.6 13.0 %copy-start.1 = (s32[32]{0:T(128)S(1)}, s32[32]{0:T(128)}, u32[]{:S(2)}) copy-start(s32[32]{0:T(128)} %picked.1) | copy-start | bytes 388
  4.9 16.5 %collective-permute-start = (bf16[8,88,128]{2,1,0:T(8,128)(2,1)}, bf16[8,88,128]{2,1,0:T(8,128)(2,1)S(1)}, u32[]{:S(2)}, u32[]{:S(2)}) collective-permute-start(bf16[8,88,128]{2,1,0:T(8,128)(2,1)} %get-tuple-element.10), channel_id=1, source_target_pairs={{0,1},{1,2},{2,3},{3,0},{4,5},{5,6},{6,7},{7,4},{8,9},{9,10},{10,1... | collective-permute-start | bytes 540680 | tf_op jit(solution)/shard_map/ppermute | solution.py:348
  6.6 14.8 %collective-permute-start.1 = (bf16[8,88,128]{2,1,0:T(8,128)(2,1)S(1)}, bf16[8,88,128]{2,1,0:T(8,128)(2,1)S(1)}, u32[]{:S(2)}, u32[]{:S(2)}) collective-permute-start(bf16[8,88,128]{2,1,0:T(8,128)(2,1)S(1)} %get-tuple-element.11), channel_id=1, source_target_pairs={{1,0},{2,1},{3,2},{0,3},{5,4},{6,5},{7,6},{4,7},{9,8},{10,9},{11,1... | collective-permute-start | bytes 540680 | tf_op jit(solution)/shard_map/ppermute | solution.py:348
  8.2 19.5 %collective-permute-start.2 = (bf16[32,88,128]{2,1,0:T(8,128)(2,1)S(1)}, bf16[32,88,128]{2,1,0:T(8,128)(2,1)S(1)}, u32[]{:S(2)}, u32[]{:S(2)}) collective-permute-start(bf16[32,88,128]{2,1,0:T(8,128)(2,1)S(1)} %get-tuple-element.12), channel_id=1, source_target_pairs={{0,4},{4,8},{8,12},{12,16},{16,20},{20,24},{24,28},{28,32},{32,36}... | collective-permute-start | bytes 2162696 | tf_op jit(solution)/shard_map/ppermute | solution.py:348
  8.2 19.5 %collective-permute-start.3 = (bf16[32,88,128]{2,1,0:T(8,128)(2,1)S(1)}, bf16[32,88,128]{2,1,0:T(8,128)(2,1)S(1)}, u32[]{:S(2)}, u32[]{:S(2)}) collective-permute-start(bf16[32,88,128]{2,1,0:T(8,128)(2,1)S(1)} %get-tuple-element.13), channel_id=1, source_target_pairs={{4,0},{8,4},{12,8},{16,12},{20,16},{24,20},{28,24},{32,28},{36,32}... | collective-permute-start | bytes 2162696 | tf_op jit(solution)/shard_map/ppermute | solution.py:348
  13.6 7.8 %copy-start = (s32[8,32,128]{2,1,0:T(8,128)S(1)}, s32[8,32,128]{2,1,0:T(8,128)}, u32[]{:S(2)}) copy-start(s32[8,32,128]{2,1,0:T(8,128)} %material.5) | copy-start | bytes 393220
  30.2 1.3 %collective-permute-start.4 = (f32[88,128]{1,0:T(8,128)S(1)}, f32[88,128]{1,0:T(8,128)S(1)}, u32[]{:S(2)}, u32[]{:S(2)}) collective-permute-start(f32[88,128]{1,0:T(8,128)S(1)} %outer.1), channel_id=1, source_target_pairs={{0,4},{4,0},{8,12},{12,8},{16,20},{20,16},{24,28},{28,24},{32,36},... | collective-permute-start | bytes 135176 | tf_op jit(solution)/shard_map/ppermute | solution.py:327
  31.5 5.3 %collective-permute-start.7 = (f32[88,128]{1,0:T(8,128)S(1)}, f32[88,128]{1,0:T(8,128)S(1)}, u32[]{:S(2)}, u32[]{:S(2)}) collective-permute-start(f32[88,128]{1,0:T(8,128)S(1)} %add.30), channel_id=1, source_target_pairs={{0,96},{4,100},{8,104},{12,108},{16,112},{20,116},{24,120},{28,124... | collective-permute-start | bytes 135176 | tf_op jit(solution)/shard_map/ppermute | solution.py:327
  32.9 4.1 %collective-permute-start.6 = (f32[88,128]{1,0:T(8,128)S(1)}, f32[88,128]{1,0:T(8,128)S(1)}, u32[]{:S(2)}, u32[]{:S(2)}) collective-permute-start(f32[88,128]{1,0:T(8,128)S(1)} %add.30), channel_id=1, source_target_pairs={{0,32},{4,36},{8,40},{12,44},{16,48},{20,52},{24,56},{28,60},{32,0... | collective-permute-start | bytes 135176 | tf_op jit(solution)/shard_map/ppermute | solution.py:327
  33.2 5.6 %collective-permute-start.5 = (f32[88,128]{1,0:T(8,128)S(1)}, f32[88,128]{1,0:T(8,128)S(1)}, u32[]{:S(2)}, u32[]{:S(2)}) collective-permute-start(f32[88,128]{1,0:T(8,128)S(1)} %add.30), channel_id=1, source_target_pairs={{0,64},{4,68},{8,72},{12,76},{16,80},{20,84},{24,88},{28,92},{32,9... | collective-permute-start | bytes 135176 | tf_op jit(solution)/shard_map/ppermute | solution.py:327
  38.8 5.3 %collective-permute-start.10 = (f32[88,128]{1,0:T(8,128)S(1)}, f32[88,128]{1,0:T(8,128)S(1)}, u32[]{:S(2)}, u32[]{:S(2)}) collective-permute-start(f32[88,128]{1,0:T(8,128)S(1)} %add_add_fusion.2), channel_id=1, source_target_pairs={{0,24},{4,28},{8,16},{12,20},{16,8},{20,12},{24,0},{28,4},{32,56},... | collective-permute-start | bytes 135176 | tf_op jit(solution)/shard_map/ppermute | solution.py:327
  40.7 4.0 %collective-permute-start.9 = (f32[88,128]{1,0:T(8,128)S(1)}, f32[88,128]{1,0:T(8,128)S(1)}, u32[]{:S(2)}, u32[]{:S(2)}) collective-permute-start(f32[88,128]{1,0:T(8,128)S(1)} %add_add_fusion.2), channel_id=1, source_target_pairs={{0,8},{4,12},{8,0},{12,4},{16,24},{20,28},{24,16},{28,20},{32,40},... | collective-permute-start | bytes 135176 | tf_op jit(solution)/shard_map/ppermute | solution.py:327
  40.7 5.6 %collective-permute-start.8 = (f32[88,128]{1,0:T(8,128)S(1)}, f32[88,128]{1,0:T(8,128)S(1)}, u32[]{:S(2)}, u32[]{:S(2)}) collective-permute-start(f32[88,128]{1,0:T(8,128)S(1)} %add_add_fusion.2), channel_id=1, source_target_pairs={{0,16},{4,20},{8,24},{12,28},{16,0},{20,4},{24,8},{28,12},{32,48},... | collective-permute-start | bytes 135176 | tf_op jit(solution)/shard_map/ppermute | solution.py:327
  46.3 5.3 %collective-permute-start.13 = (f32[88,128]{1,0:T(8,128)S(1)}, f32[88,128]{1,0:T(8,128)S(1)}, u32[]{:S(2)}, u32[]{:S(2)}) collective-permute-start(f32[88,128]{1,0:T(8,128)S(1)} %add_add_fusion.1), channel_id=1, source_target_pairs={{0,3},{1,2},{2,1},{3,0},{4,7},{5,6},{6,5},{7,4},{8,11},{9,10},{10,... | collective-permute-start | bytes 135176 | tf_op jit(solution)/shard_map/ppermute | solution.py:327
  48.2 4.0 %collective-permute-start.12 = (f32[88,128]{1,0:T(8,128)S(1)}, f32[88,128]{1,0:T(8,128)S(1)}, u32[]{:S(2)}, u32[]{:S(2)}) collective-permute-start(f32[88,128]{1,0:T(8,128)S(1)} %add_add_fusion.1), channel_id=1, source_target_pairs={{0,1},{1,0},{2,3},{3,2},{4,5},{5,4},{6,7},{7,6},{8,9},{9,8},{10,11... | collective-permute-start | bytes 135176 | tf_op jit(solution)/shard_map/ppermute | solution.py:327
  48.3 5.6 %collective-permute-start.11 = (f32[88,128]{1,0:T(8,128)S(1)}, f32[88,128]{1,0:T(8,128)S(1)}, u32[]{:S(2)}, u32[]{:S(2)}) collective-permute-start(f32[88,128]{1,0:T(8,128)S(1)} %add_add_fusion.1), channel_id=1, source_target_pairs={{0,2},{1,3},{2,0},{3,1},{4,6},{5,7},{6,4},{7,5},{8,10},{9,11},{10,... | collective-permute-start | bytes 135176 | tf_op jit(solution)/shard_map/ppermute | solution.py:327

commit v8 on v7

--- a/solution.py
+++ b/solution.py
@@ -214,8 +214,15 @@
     return out
 
 
+def parts(value):
+    out = []
+    for _ in range(3):
+        out.append(value.astype(BF16))
+        value = value - out[-1].astype(F32)
+    return out
+
+
 def combination(packed, columns, count):
-    exact = lax.Precision.HIGHEST
     shape = (128, 128)
     col = lax.broadcasted_iota(jnp.int32, shape, 1)
     line = lax.broadcasted_iota(jnp.int32, shape, 0)
@@ -234,11 +241,14 @@
         blocks[panel] = stacked(rows)
     solved = jnp.concatenate(blocks + [jnp.zeros((128 - columns, 128), F32)], 0)
     solved = pltpu.roll(solved, 128 - columns, 1)
-    chosen = jnp.where(col < count, solved, 0.0).astype(BF16).astype(F32)
-    chosen_t = chosen.T
-    product = jnp.dot(normal, chosen, precision=exact, preferred_element_type=F32)
-    normal = jnp.dot(chosen_t, product, precision=exact, preferred_element_type=F32)
-    normal = normal[:count] * (1.0 / CELLS)
+    chosen = jnp.where(col < count, solved, 0.0).astype(BF16)
+    chosen_t = chosen.astype(F32).T
+    product = jnp.dot(jnp.concatenate(parts(normal), 0), chosen, preferred_element_type=F32)
+    product = product[:128] + (product[128:256] + product[256:])
+    short_t = chosen_t[:count].astype(BF16)
+    normal = jnp.dot(short_t, jnp.concatenate(parts(product), 1), preferred_element_type=F32)
+    normal = normal[:, :128] + (normal[:, 128:256] + normal[:, 256:])
+    normal = normal * (1.0 / CELLS)
     joined = jnp.where(col[:count] < count, normal, pltpu.roll(chosen_t[:count], count, 1))
     blocks = [joined[8 * i : 8 * i + 8] for i in range(count // 8)]
     for panel in range(len(blocks)):
@@ -283,19 +293,12 @@
 
     fill(0, z_low, edges[0])
     fill(1, turned.at[0])
+    fill(2, turned.at[1])
     lane = lax.broadcasted_iota(jnp.int32, (count, width), 1)
     first, last = lane == 0, lane == width - 1
 
-    def step(z, _):
+    def write(z, ahead):
         slot = lax.rem(z, SLOTS)
-
-        @pl.when(z + 1 < depth)
-        def _():
-            fill(z + 2, turned.at[z + 1])
-
-        @pl.when(z + 1 == depth)
-        def _():
-            fill(z + 2, z_high, edges[1])
 
         @pl.when(z >= SLOTS)
         def _():
@@ -305,6 +308,8 @@
         scale = coefficient(material[z])
         one = first_out.at[slot].reshape(count * STEP, width)
         two = second_out.at[slot].reshape(count * STEP, width)
+        if ahead:
+            fill(z + 3, turned.at[z + 2])
         for y in range(height):
             row = planes[z + 1, y + 1]
             beside = planes[z, y + 1] + planes[z + 2, y + 1]
@@ -316,7 +321,9 @@
             copy.start()
         return 0
 
-    lax.fori_loop(0, depth, step, 0)
+    lax.fori_loop(0, depth - 2, lambda z, _: write(z, True), 0)
+    fill(depth + 1, z_high, edges[1])
+    lax.fori_loop(depth - 2, depth, lambda z, _: write(z, False), 0)
     for z in range(depth - SLOTS, depth):
         for copy in stores(z, z % SLOTS):
             copy.wait()

time: 67.6 us -> 66.9 us (0.990)
  Pallas kernels: 33.5 us -> 32.7 us
    pallas_call x1, Pallas kernels: 12.7 us -> 12 us  [local(): pl.pallas_call(update_kernel, in_specs=[whole(pltpu.SMEM)] + [whole()] *...]
where the time goes in v8:
time: 66.9 us; the launch traced here: 66 us
  Pallas kernels  32.7 us (49%)
  starting transfers between devices  23.1 us (35%)
  waiting for transfers between devices  9.23 us (14%)
  between operations  0.89 us (1%)
    ppermute x10, starting transfers between devices, exchanged(): return lax.ppermute(value, axis, [(i, i ^ distance) for i in range(size)])  14.4 us
    pallas_call x1, Pallas kernels, local(): pl.pallas_call(update_kernel, in_specs=[whole(pltpu.SMEM)] + [whole()] *...  12 us
    ppermute x10, waiting for transfers between devices, exchanged(): return lax.ppermute(value, axis, [(i, i ^ distance) for i in range(size)])  9.22 us
    pallas_call x1, Pallas kernels, local(): pl.pallas_call(gram_kernel, in_specs=[whole(pltpu.SMEM), whole(pltpu.HBM)...  7.74 us
    ppermute x2, starting transfers between devices, neighbours(): lax.ppermute(low_face, axis, down)  6.91 us
    pallas_call x1, Pallas kernels, local(): pl.pallas_call(inner_kernel, in_specs=[whole(pltpu.SMEM)] + [whole()] * 4...  6.25 us
    pallas_call x1, Pallas kernels, local(): pl.pallas_call(face_kernel, in_specs=[whole(pltpu.HBM)], out_specs=[whole...  4.27 us
    pallas_call x1, Pallas kernels, local(): pl.pallas_call(outer_kernel, in_specs=[whole(pltpu.SMEM)] + [whole()] * 8...  2.49 us
  transfers between devices with their start and end apart: 14, of which 10 were waited for; matrix products, arithmetic and copies ran while one was open for 0% of the time, Pallas kernels for 21%

profile of v8, /device:TPU:0, one launch (start us, length us, event | category | flops | bytes accessed | tf_op | source)
XLA Modules:
  0.0 66.0 jit_solution(11858569542551441606)
XLA Ops:
  0.6 0.0 copy-start.1
  0.6 4.3 %faces.1 = (bf16[32,88,128]{2,1,0:T(8,128)(2,1)S(1)}, bf16[32,88,128]{2,1,0:T(8,128)(2,1)S(1)}, bf16[8,88,128]{2,1,0:T(8,128)(2,1)S(1)}, bf16[8,88,128]{2,1,0:T(8,128)(2,1)}) custom-call(bf16[88,8,32,128]{3,2,1,0:T(8,128)(2,1)} %basis.3), custom_call_target="tpu_custom_call" | custom-call | tf_op jit(solution)/shard_map/faces/pallas_call | solution.py:359
  4.9 1.7 %collective-permute-start = (bf16[8,88,128]{2,1,0:T(8,128)(2,1)}, bf16[8,88,128]{2,1,0:T(8,128)(2,1)S(1)}, u32[]{:S(2)}, u32[]{:S(2)}) collective-permute-start(bf16[8,88,128]{2,1,0:T(8,128)(2,1)} %get-tuple-element.10), channel_id=1, source_target_pairs={{0,1},{1,2},{2,3},{3,0},{4,5},{5,6},{6,7},{7,4},{8,9},{9,10},{10,1... | collective-permute-start | bytes 540680 | tf_op jit(solution)/shard_map/ppermute | solution.py:355
  6.6 1.6 %collective-permute-start.1 = (bf16[8,88,128]{2,1,0:T(8,128)(2,1)S(1)}, bf16[8,88,128]{2,1,0:T(8,128)(2,1)S(1)}, u32[]{:S(2)}, u32[]{:S(2)}) collective-permute-start(bf16[8,88,128]{2,1,0:T(8,128)(2,1)S(1)} %get-tuple-element.11), channel_id=1, source_target_pairs={{1,0},{2,1},{3,2},{0,3},{5,4},{6,5},{7,6},{4,7},{9,8},{10,9},{11,1... | collective-permute-start | bytes 540680 | tf_op jit(solution)/shard_map/ppermute | solution.py:355
  8.2 0.0 collective-permute-start.2
  8.2 5.3 %collective-permute-start.3 = (bf16[32,88,128]{2,1,0:T(8,128)(2,1)S(1)}, bf16[32,88,128]{2,1,0:T(8,128)(2,1)S(1)}, u32[]{:S(2)}, u32[]{:S(2)}) collective-permute-start(bf16[32,88,128]{2,1,0:T(8,128)(2,1)S(1)} %get-tuple-element.13), channel_id=1, source_target_pairs={{4,0},{8,4},{12,8},{16,12},{20,16},{24,20},{28,24},{32,28},{36,32}... | collective-permute-start | bytes 2162696 | tf_op jit(solution)/shard_map/ppermute | solution.py:355
  13.6 0.1 add_convert_fusion.edges
  13.6 0.0 copy-done.1
  13.6 0.0 copy-start
  13.6 7.7 %gram.1 = (f32[120,88]{1,0:T(8,128)S(1)}, bf16[8,32,88,128]{3,2,1,0:T(8,128)(2,1)S(1)}) custom-call(s32[32]{0:T(128)S(1)} %copy-done.1, bf16[88,8,32,128]{3,2,1,0:T(8,128)(2,1)} %image.1, bf16[88,8,32,128]{3,2,1,0:T(8,128)(2,1)} %basis.3), custom_call_target="tpu_custom_call" | custom-call | flops 2000000000 | bytes 17000000 | tf_op jit(solution)/shard_map/gram/pallas_call | solution.py:373
  21.4 0.0 collective-permute-done.y_low
  21.4 0.0 collective-permute-done.1.y_high
  21.4 0.0 copy-done
  21.4 6.2 %inner.1.part = f32[88,88]{1,0:T(8,128)S(1)} custom-call(s32[4]{0:T(128)S(1)} %add_convert_fusion.edges, bf16[8,32,88,128]{3,2,1,0:T(8,128)(2,1)S(1)} %get-tuple-element.9.turned, s32[8,32,128]{2,1,0:T(8,128)S(1)} %copy-done, bf16[8,88,128]{2,1,0:T(8,128)(2,1)S(1)} %collective-permute-done.y_low, bf16[8,88,128]{2,1,0:T(8,128)(2,1)S(1)} %collective-permute-done.1.y_high), custom_call_target="tpu_custom_call" | custom-call | flops 10000000000 | bytes 10000000 | tf_op jit(solution)/shard_map/inner/pallas_call | solution.py:397
  27.7 0.0 collective-permute-done.2.z_low
  27.7 0.0 collective-permute-done.3.z_high
  27.7 2.5 %outer.1 = f32[88,128]{1,0:T(8,128)S(1)} custom-call(s32[4]{0:T(128)S(1)} %add_convert_fusion.edges, f32[120,88]{1,0:T(8,128)S(1)} %get-tuple-element.8.sums, f32[88,88]{1,0:T(8,128)S(1)} %inner.1.part, bf16[8,32,88,128]{3,2,1,0:T(8,128)(2,1)S(1)} %get-tuple-element.9.turned, s32[8,32,128]{2,1,0:T(8,128)S(1)} %copy-done, ...), custom_call_target="tpu_custom_call" | custom-call | tf_op jit(solution)/shard_map/outer/pallas_call | solution.py:406
  30.2 0.1 collective-permute-start.4
  30.3 1.2 %collective-permute-done.4 = f32[88,128]{1,0:T(8,128)S(1)} collective-permute-done((f32[88,128]{1,0:T(8,128)S(1)}, f32[88,128]{1,0:T(8,128)S(1)}, u32[]{:S(2)}, u32[]{:S(2)}) %collective-permute-start.4) | collective-permute-done | bytes 45088 | tf_op jit(solution)/shard_map/ppermute | solution.py:334
  31.5 1.4 %collective-permute-start.7 = (f32[88,128]{1,0:T(8,128)S(1)}, f32[88,128]{1,0:T(8,128)S(1)}, u32[]{:S(2)}, u32[]{:S(2)}) collective-permute-start(f32[88,128]{1,0:T(8,128)S(1)} %add.30), channel_id=1, source_target_pairs={{0,96},{4,100},{8,104},{12,108},{16,112},{20,116},{24,120},{28,124... | collective-permute-start | bytes 135176 | tf_op jit(solution)/shard_map/ppermute | solution.py:334
  32.9 0.2 collective-permute-start.6
  33.2 3.1 %collective-permute-start.5 = (f32[88,128]{1,0:T(8,128)S(1)}, f32[88,128]{1,0:T(8,128)S(1)}, u32[]{:S(2)}, u32[]{:S(2)}) collective-permute-start(f32[88,128]{1,0:T(8,128)S(1)} %add.30), channel_id=1, source_target_pairs={{0,64},{4,68},{8,72},{12,76},{16,80},{20,84},{24,88},{28,92},{32,9... | collective-permute-start | bytes 135176 | tf_op jit(solution)/shard_map/ppermute | solution.py:334
  36.3 0.6 collective-permute-done.7
  36.8 0.2 collective-permute-done.6
  37.0 1.8 %collective-permute-done.5 = f32[88,128]{1,0:T(8,128)S(1)} collective-permute-done((f32[88,128]{1,0:T(8,128)S(1)}, f32[88,128]{1,0:T(8,128)S(1)}, u32[]{:S(2)}, u32[]{:S(2)}) %collective-permute-start.5) | collective-permute-done | bytes 45088 | tf_op jit(solution)/shard_map/ppermute | solution.py:334
  38.8 2.0 %collective-permute-start.10 = (f32[88,128]{1,0:T(8,128)S(1)}, f32[88,128]{1,0:T(8,128)S(1)}, u32[]{:S(2)}, u32[]{:S(2)}) collective-permute-start(f32[88,128]{1,0:T(8,128)S(1)} %add_add_fusion.2), channel_id=1, source_target_pairs={{0,24},{4,28},{8,16},{12,20},{16,8},{20,12},{24,0},{28,4},{32,56},... | collective-permute-start | bytes 135176 | tf_op jit(solution)/shard_map/ppermute | solution.py:334
  40.8 0.0 collective-permute-start.9
  40.8 2.8 %collective-permute-start.8 = (f32[88,128]{1,0:T(8,128)S(1)}, f32[88,128]{1,0:T(8,128)S(1)}, u32[]{:S(2)}, u32[]{:S(2)}) collective-permute-start(f32[88,128]{1,0:T(8,128)S(1)} %add_add_fusion.2), channel_id=1, source_target_pairs={{0,16},{4,20},{8,24},{12,28},{16,0},{20,4},{24,8},{28,12},{32,48},... | collective-permute-start | bytes 135176 | tf_op jit(solution)/shard_map/ppermute | solution.py:334
  43.6 0.6 collective-permute-done.10
  44.1 0.7 %collective-permute-done.9 = f32[88,128]{1,0:T(8,128)S(1)} collective-permute-done((f32[88,128]{1,0:T(8,128)S(1)}, f32[88,128]{1,0:T(8,128)S(1)}, u32[]{:S(2)}, u32[]{:S(2)}) %collective-permute-start.9) | collective-permute-done | bytes 45088 | tf_op jit(solution)/shard_map/ppermute | solution.py:334
  44.8 1.5 %collective-permute-done.8 = f32[88,128]{1,0:T(8,128)S(1)} collective-permute-done((f32[88,128]{1,0:T(8,128)S(1)}, f32[88,128]{1,0:T(8,128)S(1)}, u32[]{:S(2)}, u32[]{:S(2)}) %collective-permute-start.8) | collective-permute-done | bytes 45088 | tf_op jit(solution)/shard_map/ppermute | solution.py:334
  46.3 1.9 %collective-permute-start.13 = (f32[88,128]{1,0:T(8,128)S(1)}, f32[88,128]{1,0:T(8,128)S(1)}, u32[]{:S(2)}, u32[]{:S(2)}) collective-permute-start(f32[88,128]{1,0:T(8,128)S(1)} %add_add_fusion.1), channel_id=1, source_target_pairs={{0,3},{1,2},{2,1},{3,0},{4,7},{5,6},{6,5},{7,4},{8,11},{9,10},{10,... | collective-permute-start | bytes 135176 | tf_op jit(solution)/shard_map/ppermute | solution.py:334
  48.2 0.1 collective-permute-start.12
  48.3 2.8 %collective-permute-start.11 = (f32[88,128]{1,0:T(8,128)S(1)}, f32[88,128]{1,0:T(8,128)S(1)}, u32[]{:S(2)}, u32[]{:S(2)}) collective-permute-start(f32[88,128]{1,0:T(8,128)S(1)} %add_add_fusion.1), channel_id=1, source_target_pairs={{0,2},{1,3},{2,0},{3,1},{4,6},{5,7},{6,4},{7,5},{8,10},{9,11},{10,... | collective-permute-start | bytes 135176 | tf_op jit(solution)/shard_map/ppermute | solution.py:334
  51.1 0.6 collective-permute-done.13
  51.7 0.6 collective-permute-done.12
  52.2 1.6 %collective-permute-done.11 = f32[88,128]{1,0:T(8,128)S(1)} collective-permute-done((f32[88,128]{1,0:T(8,128)S(1)}, f32[88,128]{1,0:T(8,128)S(1)}, u32[]{:S(2)}, u32[]{:S(2)}) %collective-permute-start.11) | collective-permute-done | bytes 45088 | tf_op jit(solution)/shard_map/ppermute | solution.py:334
  53.9 12.0 %update.1 = (f32[32,8,32,128]{3,2,1,0:T(8,128)}, f32[32,8,32,128]{3,2,1,0:T(8,128)}) custom-call(s32[4]{0:T(128)S(1)} %add_convert_fusion.edges, f32[88,128]{1,0:T(8,128)S(1)} %add_add_fusion.packed, bf16[8,32,88,128]{3,2,1,0:T(8,128)(2,1)S(1)} %get-tuple-element.9.turned, s32[8,32,128]{2,1,0:T(8,128)S(1)} %copy-done, ...), custom_call_target="tpu_custom_call" | custom-call | tf_op jit(solution)/shard_map/update/pallas_call | solution.py:417
  (4 shorter events, 0.1 us)
Async XLA Ops:
  0.6 13.0 %copy-start.1 = (s32[32]{0:T(128)S(1)}, s32[32]{0:T(128)}, u32[]{:S(2)}) copy-start(s32[32]{0:T(128)} %picked.1) | copy-start | bytes 388
  4.9 16.5 %collective-permute-start = (bf16[8,88,128]{2,1,0:T(8,128)(2,1)}, bf16[8,88,128]{2,1,0:T(8,128)(2,1)S(1)}, u32[]{:S(2)}, u32[]{:S(2)}) collective-permute-start(bf16[8,88,128]{2,1,0:T(8,128)(2,1)} %get-tuple-element.10), channel_id=1, source_target_pairs={{0,1},{1,2},{2,3},{3,0},{4,5},{5,6},{6,7},{7,4},{8,9},{9,10},{10,1... | collective-permute-start | bytes 540680 | tf_op jit(solution)/shard_map/ppermute | solution.py:355
  6.6 14.8 %collective-permute-start.1 = (bf16[8,88,128]{2,1,0:T(8,128)(2,1)S(1)}, bf16[8,88,128]{2,1,0:T(8,128)(2,1)S(1)}, u32[]{:S(2)}, u32[]{:S(2)}) collective-permute-start(bf16[8,88,128]{2,1,0:T(8,128)(2,1)S(1)} %get-tuple-element.11), channel_id=1, source_target_pairs={{1,0},{2,1},{3,2},{0,3},{5,4},{6,5},{7,6},{4,7},{9,8},{10,9},{11,1... | collective-permute-start | bytes 540680 | tf_op jit(solution)/shard_map/ppermute | solution.py:355
  8.2 19.5 %collective-permute-start.2 = (bf16[32,88,128]{2,1,0:T(8,128)(2,1)S(1)}, bf16[32,88,128]{2,1,0:T(8,128)(2,1)S(1)}, u32[]{:S(2)}, u32[]{:S(2)}) collective-permute-start(bf16[32,88,128]{2,1,0:T(8,128)(2,1)S(1)} %get-tuple-element.12), channel_id=1, source_target_pairs={{0,4},{4,8},{8,12},{12,16},{16,20},{20,24},{24,28},{28,32},{32,36}... | collective-permute-start | bytes 2162696 | tf_op jit(solution)/shard_map/ppermute | solution.py:355
  8.2 19.5 %collective-permute-start.3 = (bf16[32,88,128]{2,1,0:T(8,128)(2,1)S(1)}, bf16[32,88,128]{2,1,0:T(8,128)(2,1)S(1)}, u32[]{:S(2)}, u32[]{:S(2)}) collective-permute-start(bf16[32,88,128]{2,1,0:T(8,128)(2,1)S(1)} %get-tuple-element.13), channel_id=1, source_target_pairs={{4,0},{8,4},{12,8},{16,12},{20,16},{24,20},{28,24},{32,28},{36,32}... | collective-permute-start | bytes 2162696 | tf_op jit(solution)/shard_map/ppermute | solution.py:355
  13.6 7.8 %copy-start = (s32[8,32,128]{2,1,0:T(8,128)S(1)}, s32[8,32,128]{2,1,0:T(8,128)}, u32[]{:S(2)}) copy-start(s32[8,32,128]{2,1,0:T(8,128)} %material.5) | copy-start | bytes 393220
  30.2 1.3 %collective-permute-start.4 = (f32[88,128]{1,0:T(8,128)S(1)}, f32[88,128]{1,0:T(8,128)S(1)}, u32[]{:S(2)}, u32[]{:S(2)}) collective-permute-start(f32[88,128]{1,0:T(8,128)S(1)} %outer.1), channel_id=1, source_target_pairs={{0,4},{4,0},{8,12},{12,8},{16,20},{20,16},{24,28},{28,24},{32,36},... | collective-permute-start | bytes 135176 | tf_op jit(solution)/shard_map/ppermute | solution.py:334
  31.5 5.3 %collective-permute-start.7 = (f32[88,128]{1,0:T(8,128)S(1)}, f32[88,128]{1,0:T(8,128)S(1)}, u32[]{:S(2)}, u32[]{:S(2)}) collective-permute-start(f32[88,128]{1,0:T(8,128)S(1)} %add.30), channel_id=1, source_target_pairs={{0,96},{4,100},{8,104},{12,108},{16,112},{20,116},{24,120},{28,124... | collective-permute-start | bytes 135176 | tf_op jit(solution)/shard_map/ppermute | solution.py:334
  32.9 4.1 %collective-permute-start.6 = (f32[88,128]{1,0:T(8,128)S(1)}, f32[88,128]{1,0:T(8,128)S(1)}, u32[]{:S(2)}, u32[]{:S(2)}) collective-permute-start(f32[88,128]{1,0:T(8,128)S(1)} %add.30), channel_id=1, source_target_pairs={{0,32},{4,36},{8,40},{12,44},{16,48},{20,52},{24,56},{28,60},{32,0... | collective-permute-start | bytes 135176 | tf_op jit(solution)/shard_map/ppermute | solution.py:334
  33.2 5.6 %collective-permute-start.5 = (f32[88,128]{1,0:T(8,128)S(1)}, f32[88,128]{1,0:T(8,128)S(1)}, u32[]{:S(2)}, u32[]{:S(2)}) collective-permute-start(f32[88,128]{1,0:T(8,128)S(1)} %add.30), channel_id=1, source_target_pairs={{0,64},{4,68},{8,72},{12,76},{16,80},{20,84},{24,88},{28,92},{32,9... | collective-permute-start | bytes 135176 | tf_op jit(solution)/shard_map/ppermute | solution.py:334
  38.8 5.3 %collective-permute-start.10 = (f32[88,128]{1,0:T(8,128)S(1)}, f32[88,128]{1,0:T(8,128)S(1)}, u32[]{:S(2)}, u32[]{:S(2)}) collective-permute-start(f32[88,128]{1,0:T(8,128)S(1)} %add_add_fusion.2), channel_id=1, source_target_pairs={{0,24},{4,28},{8,16},{12,20},{16,8},{20,12},{24,0},{28,4},{32,56},... | collective-permute-start | bytes 135176 | tf_op jit(solution)/shard_map/ppermute | solution.py:334
  40.8 4.0 %collective-permute-start.9 = (f32[88,128]{1,0:T(8,128)S(1)}, f32[88,128]{1,0:T(8,128)S(1)}, u32[]{:S(2)}, u32[]{:S(2)}) collective-permute-start(f32[88,128]{1,0:T(8,128)S(1)} %add_add_fusion.2), channel_id=1, source_target_pairs={{0,8},{4,12},{8,0},{12,4},{16,24},{20,28},{24,16},{28,20},{32,40},... | collective-permute-start | bytes 135176 | tf_op jit(solution)/shard_map/ppermute | solution.py:334
  40.8 5.6 %collective-permute-start.8 = (f32[88,128]{1,0:T(8,128)S(1)}, f32[88,128]{1,0:T(8,128)S(1)}, u32[]{:S(2)}, u32[]{:S(2)}) collective-permute-start(f32[88,128]{1,0:T(8,128)S(1)} %add_add_fusion.2), channel_id=1, source_target_pairs={{0,16},{4,20},{8,24},{12,28},{16,0},{20,4},{24,8},{28,12},{32,48},... | collective-permute-start | bytes 135176 | tf_op jit(solution)/shard_map/ppermute | solution.py:334
  46.3 5.3 %collective-permute-start.13 = (f32[88,128]{1,0:T(8,128)S(1)}, f32[88,128]{1,0:T(8,128)S(1)}, u32[]{:S(2)}, u32[]{:S(2)}) collective-permute-start(f32[88,128]{1,0:T(8,128)S(1)} %add_add_fusion.1), channel_id=1, source_target_pairs={{0,3},{1,2},{2,1},{3,0},{4,7},{5,6},{6,5},{7,4},{8,11},{9,10},{10,... | collective-permute-start | bytes 135176 | tf_op jit(solution)/shard_map/ppermute | solution.py:334
  48.2 4.0 %collective-permute-start.12 = (f32[88,128]{1,0:T(8,128)S(1)}, f32[88,128]{1,0:T(8,128)S(1)}, u32[]{:S(2)}, u32[]{:S(2)}) collective-permute-start(f32[88,128]{1,0:T(8,128)S(1)} %add_add_fusion.1), channel_id=1, source_target_pairs={{0,1},{1,0},{2,3},{3,2},{4,5},{5,4},{6,7},{7,6},{8,9},{9,8},{10,11... | collective-permute-start | bytes 135176 | tf_op jit(solution)/shard_map/ppermute | solution.py:334
  48.3 5.6 %collective-permute-start.11 = (f32[88,128]{1,0:T(8,128)S(1)}, f32[88,128]{1,0:T(8,128)S(1)}, u32[]{:S(2)}, u32[]{:S(2)}) collective-permute-start(f32[88,128]{1,0:T(8,128)S(1)} %add_add_fusion.1), channel_id=1, source_target_pairs={{0,2},{1,3},{2,0},{3,1},{4,6},{5,7},{6,4},{7,5},{8,10},{9,11},{10,... | collective-permute-start | bytes 135176 | tf_op jit(solution)/shard_map/ppermute | solution.py:334

commit v9 on v8

--- a/solution.py
+++ b/solution.py
@@ -18,28 +18,23 @@
 
 def face_kernel(basis, z_first, z_last, y_first, y_last, slab, sems):
     depth, height = basis.shape[1:3]
-    slots = slab.shape[0]
-
-    def load(z, slot):
-        return pltpu.make_async_copy(basis.at[:, z], slab.at[slot], sems.at[slot])
-
-    for z in range(slots - 1):
-        load(z, z).start()
-
-    def step(z, _):
-        slot = lax.rem(z, slots)
-
-        @pl.when(z + slots - 1 < depth)
-        def _():
-            load(z + slots - 1, lax.rem(z + slots - 1, slots)).start()
-
-        load(z, slot).wait()
-        y_first[z] = jnp.swapaxes(slab[slot, :, :16, :], 0, 1)[0]
-        y_last[z] = jnp.swapaxes(slab[slot, :, height - 16 :, :], 0, 1)[15]
+
+    def load(i):
+        z = lax.rem(depth - i, depth)
+        return pltpu.make_async_copy(basis.at[:, z], slab.at[i], sems.at[i])
+
+    for i in range(depth):
+        load(i).start()
+
+    def step(i, _):
+        z = lax.rem(depth - i, depth)
+        load(i).wait()
+        y_first[z] = jnp.swapaxes(slab[i, :, :16, :], 0, 1)[0]
+        y_last[z] = jnp.swapaxes(slab[i, :, height - 16 :, :], 0, 1)[15]
 
         def whole_plane(face):
             for y in range(0, height, 16):
-                face[y : y + 16] = jnp.swapaxes(slab[slot, :, y : y + 16, :], 0, 1)
+                face[y : y + 16] = jnp.swapaxes(slab[i, :, y : y + 16, :], 0, 1)
 
         pl.when(z == 0)(lambda: whole_plane(z_first))
         pl.when(z == depth - 1)(lambda: whole_plane(z_last))
@@ -362,8 +357,8 @@
         out_specs=[whole()] * 4,
         out_shape=[face, face, edge, edge],
         scratch_shapes=[
-            pltpu.VMEM((4, columns, height, width), BF16),
-            pltpu.SemaphoreType.DMA((4,)),
+            pltpu.VMEM((depth, columns, height, width), BF16),
+            pltpu.SemaphoreType.DMA((depth,)),
         ],
         compiler_params=pltpu.CompilerParams(vmem_limit_bytes=52 * MIB),
         name="faces",

time: 66.9 us -> 66 us (0.987)
  Pallas kernels: 32.7 us -> 31.9 us
    pallas_call x1, Pallas kernels: 4.27 us -> 3.47 us  [local(): pl.pallas_call(face_kernel, in_specs=[whole(pltpu.HBM)], out_specs=[whole...]
where the time goes in v9:
time: 66 us; the launch traced here: 65.2 us
  Pallas kernels  31.9 us (48%)
  starting transfers between devices  23.1 us (35%)
  waiting for transfers between devices  9.23 us (14%)
  between operations  0.89 us (1%)
    ppermute x10, starting transfers between devices, exchanged(): return lax.ppermute(value, axis, [(i, i ^ distance) for i in range(size)])  14.4 us
    pallas_call x1, Pallas kernels, local(): pl.pallas_call(update_kernel, in_specs=[whole(pltpu.SMEM)] + [whole()] *...  12 us
    ppermute x10, waiting for transfers between devices, exchanged(): return lax.ppermute(value, axis, [(i, i ^ distance) for i in range(size)])  9.22 us
    pallas_call x1, Pallas kernels, local(): pl.pallas_call(gram_kernel, in_specs=[whole(pltpu.SMEM), whole(pltpu.HBM)...  7.74 us
    ppermute x2, starting transfers between devices, neighbours(): lax.ppermute(low_face, axis, down)  6.91 us
    pallas_call x1, Pallas kernels, local(): pl.pallas_call(inner_kernel, in_specs=[whole(pltpu.SMEM)] + [whole()] * 4...  6.25 us
    pallas_call x1, Pallas kernels, local(): pl.pallas_call(face_kernel, in_specs=[whole(pltpu.HBM)], out_specs=[whole...  3.47 us
    pallas_call x1, Pallas kernels, local(): pl.pallas_call(outer_kernel, in_specs=[whole(pltpu.SMEM)] + [whole()] * 8...  2.49 us
  transfers between devices with their start and end apart: 14, of which 10 were waited for; matrix products, arithmetic and copies ran while one was open for 0% of the time, Pallas kernels for 21%

profile of v9, /device:TPU:0, one launch (start us, length us, event | category | flops | bytes accessed | tf_op | source)
XLA Modules:
  0.0 65.2 jit_solution(12426068839906899919)
XLA Ops:
  0.6 0.0 copy-start.1
  0.6 3.5 %faces.1 = (bf16[32,88,128]{2,1,0:T(8,128)(2,1)S(1)}, bf16[32,88,128]{2,1,0:T(8,128)(2,1)S(1)}, bf16[8,88,128]{2,1,0:T(8,128)(2,1)S(1)}, bf16[8,88,128]{2,1,0:T(8,128)(2,1)}) custom-call(bf16[88,8,32,128]{3,2,1,0:T(8,128)(2,1)} %basis.3), custom_call_target="tpu_custom_call" | custom-call | tf_op jit(solution)/shard_map/faces/pallas_call | solution.py:354
  4.1 1.7 %collective-permute-start = (bf16[8,88,128]{2,1,0:T(8,128)(2,1)}, bf16[8,88,128]{2,1,0:T(8,128)(2,1)S(1)}, u32[]{:S(2)}, u32[]{:S(2)}) collective-permute-start(bf16[8,88,128]{2,1,0:T(8,128)(2,1)} %get-tuple-element.10), channel_id=1, source_target_pairs={{0,1},{1,2},{2,3},{3,0},{4,5},{5,6},{6,7},{7,4},{8,9},{9,10},{10,1... | collective-permute-start | bytes 540680 | tf_op jit(solution)/shard_map/ppermute | solution.py:350
  5.8 1.6 %collective-permute-start.1 = (bf16[8,88,128]{2,1,0:T(8,128)(2,1)S(1)}, bf16[8,88,128]{2,1,0:T(8,128)(2,1)S(1)}, u32[]{:S(2)}, u32[]{:S(2)}) collective-permute-start(bf16[8,88,128]{2,1,0:T(8,128)(2,1)S(1)} %get-tuple-element.11), channel_id=1, source_target_pairs={{1,0},{2,1},{3,2},{0,3},{5,4},{6,5},{7,6},{4,7},{9,8},{10,9},{11,1... | collective-permute-start | bytes 540680 | tf_op jit(solution)/shard_map/ppermute | solution.py:350
  7.4 0.0 collective-permute-start.2
  7.4 5.3 %collective-permute-start.3 = (bf16[32,88,128]{2,1,0:T(8,128)(2,1)S(1)}, bf16[32,88,128]{2,1,0:T(8,128)(2,1)S(1)}, u32[]{:S(2)}, u32[]{:S(2)}) collective-permute-start(bf16[32,88,128]{2,1,0:T(8,128)(2,1)S(1)} %get-tuple-element.13), channel_id=1, source_target_pairs={{4,0},{8,4},{12,8},{16,12},{20,16},{24,20},{28,24},{32,28},{36,32}... | collective-permute-start | bytes 2162696 | tf_op jit(solution)/shard_map/ppermute | solution.py:350
  12.8 0.1 add_convert_fusion.edges
  12.8 0.0 copy-done.1
  12.8 0.0 copy-start
  12.8 7.7 %gram.1 = (f32[120,88]{1,0:T(8,128)S(1)}, bf16[8,32,88,128]{3,2,1,0:T(8,128)(2,1)S(1)}) custom-call(s32[32]{0:T(128)S(1)} %copy-done.1, bf16[88,8,32,128]{3,2,1,0:T(8,128)(2,1)} %image.1, bf16[88,8,32,128]{3,2,1,0:T(8,128)(2,1)} %basis.3), custom_call_target="tpu_custom_call" | custom-call | flops 2000000000 | bytes 17000000 | tf_op jit(solution)/shard_map/gram/pallas_call | solution.py:368
  20.6 0.0 collective-permute-done.y_low
  20.6 0.0 collective-permute-done.1.y_high
  20.6 0.0 copy-done
  20.6 6.3 %inner.1.part = f32[88,88]{1,0:T(8,128)S(1)} custom-call(s32[4]{0:T(128)S(1)} %add_convert_fusion.edges, bf16[8,32,88,128]{3,2,1,0:T(8,128)(2,1)S(1)} %get-tuple-element.9.turned, s32[8,32,128]{2,1,0:T(8,128)S(1)} %copy-done, bf16[8,88,128]{2,1,0:T(8,128)(2,1)S(1)} %collective-permute-done.y_low, bf16[8,88,128]{2,1,0:T(8,128)(2,1)S(1)} %collective-permute-done.1.y_high), custom_call_target="tpu_custom_call" | custom-call | flops 10000000000 | bytes 10000000 | tf_op jit(solution)/shard_map/inner/pallas_call | solution.py:392
  26.9 0.0 collective-permute-done.2.z_low
  26.9 0.0 collective-permute-done.3.z_high
  26.9 2.5 %outer.1 = f32[88,128]{1,0:T(8,128)S(1)} custom-call(s32[4]{0:T(128)S(1)} %add_convert_fusion.edges, f32[120,88]{1,0:T(8,128)S(1)} %get-tuple-element.8.sums, f32[88,88]{1,0:T(8,128)S(1)} %inner.1.part, bf16[8,32,88,128]{3,2,1,0:T(8,128)(2,1)S(1)} %get-tuple-element.9.turned, s32[8,32,128]{2,1,0:T(8,128)S(1)} %copy-done, ...), custom_call_target="tpu_custom_call" | custom-call | tf_op jit(solution)/shard_map/outer/pallas_call | solution.py:401
  29.4 0.1 collective-permute-start.4
  29.5 1.2 %collective-permute-done.4 = f32[88,128]{1,0:T(8,128)S(1)} collective-permute-done((f32[88,128]{1,0:T(8,128)S(1)}, f32[88,128]{1,0:T(8,128)S(1)}, u32[]{:S(2)}, u32[]{:S(2)}) %collective-permute-start.4) | collective-permute-done | bytes 45088 | tf_op jit(solution)/shard_map/ppermute | solution.py:329
  30.7 1.4 %collective-permute-start.7 = (f32[88,128]{1,0:T(8,128)S(1)}, f32[88,128]{1,0:T(8,128)S(1)}, u32[]{:S(2)}, u32[]{:S(2)}) collective-permute-start(f32[88,128]{1,0:T(8,128)S(1)} %add.30), channel_id=1, source_target_pairs={{0,96},{4,100},{8,104},{12,108},{16,112},{20,116},{24,120},{28,124... | collective-permute-start | bytes 135176 | tf_op jit(solution)/shard_map/ppermute | solution.py:329
  32.1 0.2 collective-permute-start.6
  32.4 3.1 %collective-permute-start.5 = (f32[88,128]{1,0:T(8,128)S(1)}, f32[88,128]{1,0:T(8,128)S(1)}, u32[]{:S(2)}, u32[]{:S(2)}) collective-permute-start(f32[88,128]{1,0:T(8,128)S(1)} %add.30), channel_id=1, source_target_pairs={{0,64},{4,68},{8,72},{12,76},{16,80},{20,84},{24,88},{28,92},{32,9... | collective-permute-start | bytes 135176 | tf_op jit(solution)/shard_map/ppermute | solution.py:329
  35.5 0.6 collective-permute-done.7
  36.0 0.2 collective-permute-done.6
  36.2 1.8 %collective-permute-done.5 = f32[88,128]{1,0:T(8,128)S(1)} collective-permute-done((f32[88,128]{1,0:T(8,128)S(1)}, f32[88,128]{1,0:T(8,128)S(1)}, u32[]{:S(2)}, u32[]{:S(2)}) %collective-permute-start.5) | collective-permute-done | bytes 45088 | tf_op jit(solution)/shard_map/ppermute | solution.py:329
  38.0 1.9 %collective-permute-start.10 = (f32[88,128]{1,0:T(8,128)S(1)}, f32[88,128]{1,0:T(8,128)S(1)}, u32[]{:S(2)}, u32[]{:S(2)}) collective-permute-start(f32[88,128]{1,0:T(8,128)S(1)} %add_add_fusion.2), channel_id=1, source_target_pairs={{0,24},{4,28},{8,16},{12,20},{16,8},{20,12},{24,0},{28,4},{32,56},... | collective-permute-start | bytes 135176 | tf_op jit(solution)/shard_map/ppermute | solution.py:329
  39.9 0.0 collective-permute-start.9
  39.9 2.8 %collective-permute-start.8 = (f32[88,128]{1,0:T(8,128)S(1)}, f32[88,128]{1,0:T(8,128)S(1)}, u32[]{:S(2)}, u32[]{:S(2)}) collective-permute-start(f32[88,128]{1,0:T(8,128)S(1)} %add_add_fusion.2), channel_id=1, source_target_pairs={{0,16},{4,20},{8,24},{12,28},{16,0},{20,4},{24,8},{28,12},{32,48},... | collective-permute-start | bytes 135176 | tf_op jit(solution)/shard_map/ppermute | solution.py:329
  42.8 0.6 collective-permute-done.10
  43.3 0.6 collective-permute-done.9
  44.0 1.5 %collective-permute-done.8 = f32[88,128]{1,0:T(8,128)S(1)} collective-permute-done((f32[88,128]{1,0:T(8,128)S(1)}, f32[88,128]{1,0:T(8,128)S(1)}, u32[]{:S(2)}, u32[]{:S(2)}) %collective-permute-start.8) | collective-permute-done | bytes 45088 | tf_op jit(solution)/shard_map/ppermute | solution.py:329
  45.5 1.9 %collective-permute-start.13 = (f32[88,128]{1,0:T(8,128)S(1)}, f32[88,128]{1,0:T(8,128)S(1)}, u32[]{:S(2)}, u32[]{:S(2)}) collective-permute-start(f32[88,128]{1,0:T(8,128)S(1)} %add_add_fusion.1), channel_id=1, source_target_pairs={{0,3},{1,2},{2,1},{3,0},{4,7},{5,6},{6,5},{7,4},{8,11},{9,10},{10,... | collective-permute-start | bytes 135176 | tf_op jit(solution)/shard_map/ppermute | solution.py:329
  47.4 0.1 collective-permute-start.12
  47.5 2.8 %collective-permute-start.11 = (f32[88,128]{1,0:T(8,128)S(1)}, f32[88,128]{1,0:T(8,128)S(1)}, u32[]{:S(2)}, u32[]{:S(2)}) collective-permute-start(f32[88,128]{1,0:T(8,128)S(1)} %add_add_fusion.1), channel_id=1, source_target_pairs={{0,2},{1,3},{2,0},{3,1},{4,6},{5,7},{6,4},{7,5},{8,10},{9,11},{10,... | collective-permute-start | bytes 135176 | tf_op jit(solution)/shard_map/ppermute | solution.py:329
  50.3 0.6 collective-permute-done.13
  50.8 0.6 collective-permute-done.12
  51.4 1.6 %collective-permute-done.11 = f32[88,128]{1,0:T(8,128)S(1)} collective-permute-done((f32[88,128]{1,0:T(8,128)S(1)}, f32[88,128]{1,0:T(8,128)S(1)}, u32[]{:S(2)}, u32[]{:S(2)}) %collective-permute-start.11) | collective-permute-done | bytes 45088 | tf_op jit(solution)/shard_map/ppermute | solution.py:329
  53.1 12.0 %update.1 = (f32[32,8,32,128]{3,2,1,0:T(8,128)}, f32[32,8,32,128]{3,2,1,0:T(8,128)}) custom-call(s32[4]{0:T(128)S(1)} %add_convert_fusion.edges, f32[88,128]{1,0:T(8,128)S(1)} %add_add_fusion.packed, bf16[8,32,88,128]{3,2,1,0:T(8,128)(2,1)S(1)} %get-tuple-element.9.turned, s32[8,32,128]{2,1,0:T(8,128)S(1)} %copy-done, ...), custom_call_target="tpu_custom_call" | custom-call | tf_op jit(solution)/shard_map/update/pallas_call | solution.py:412
  (4 shorter events, 0.1 us)
Async XLA Ops:
  0.6 12.2 %copy-start.1 = (s32[32]{0:T(128)S(1)}, s32[32]{0:T(128)}, u32[]{:S(2)}) copy-start(s32[32]{0:T(128)} %picked.1) | copy-start | bytes 388
  4.1 16.5 %collective-permute-start = (bf16[8,88,128]{2,1,0:T(8,128)(2,1)}, bf16[8,88,128]{2,1,0:T(8,128)(2,1)S(1)}, u32[]{:S(2)}, u32[]{:S(2)}) collective-permute-start(bf16[8,88,128]{2,1,0:T(8,128)(2,1)} %get-tuple-element.10), channel_id=1, source_target_pairs={{0,1},{1,2},{2,3},{3,0},{4,5},{5,6},{6,7},{7,4},{8,9},{9,10},{10,1... | collective-permute-start | bytes 540680 | tf_op jit(solution)/shard_map/ppermute | solution.py:350
  5.8 14.8 %collective-permute-start.1 = (bf16[8,88,128]{2,1,0:T(8,128)(2,1)S(1)}, bf16[8,88,128]{2,1,0:T(8,128)(2,1)S(1)}, u32[]{:S(2)}, u32[]{:S(2)}) collective-permute-start(bf16[8,88,128]{2,1,0:T(8,128)(2,1)S(1)} %get-tuple-element.11), channel_id=1, source_target_pairs={{1,0},{2,1},{3,2},{0,3},{5,4},{6,5},{7,6},{4,7},{9,8},{10,9},{11,1... | collective-permute-start | bytes 540680 | tf_op jit(solution)/shard_map/ppermute | solution.py:350
  7.4 19.5 %collective-permute-start.2 = (bf16[32,88,128]{2,1,0:T(8,128)(2,1)S(1)}, bf16[32,88,128]{2,1,0:T(8,128)(2,1)S(1)}, u32[]{:S(2)}, u32[]{:S(2)}) collective-permute-start(bf16[32,88,128]{2,1,0:T(8,128)(2,1)S(1)} %get-tuple-element.12), channel_id=1, source_target_pairs={{0,4},{4,8},{8,12},{12,16},{16,20},{20,24},{24,28},{28,32},{32,36}... | collective-permute-start | bytes 2162696 | tf_op jit(solution)/shard_map/ppermute | solution.py:350
  7.4 19.5 %collective-permute-start.3 = (bf16[32,88,128]{2,1,0:T(8,128)(2,1)S(1)}, bf16[32,88,128]{2,1,0:T(8,128)(2,1)S(1)}, u32[]{:S(2)}, u32[]{:S(2)}) collective-permute-start(bf16[32,88,128]{2,1,0:T(8,128)(2,1)S(1)} %get-tuple-element.13), channel_id=1, source_target_pairs={{4,0},{8,4},{12,8},{16,12},{20,16},{24,20},{28,24},{32,28},{36,32}... | collective-permute-start | bytes 2162696 | tf_op jit(solution)/shard_map/ppermute | solution.py:350
  12.8 7.8 %copy-start = (s32[8,32,128]{2,1,0:T(8,128)S(1)}, s32[8,32,128]{2,1,0:T(8,128)}, u32[]{:S(2)}) copy-start(s32[8,32,128]{2,1,0:T(8,128)} %material.5) | copy-start | bytes 393220
  29.4 1.3 %collective-permute-start.4 = (f32[88,128]{1,0:T(8,128)S(1)}, f32[88,128]{1,0:T(8,128)S(1)}, u32[]{:S(2)}, u32[]{:S(2)}) collective-permute-start(f32[88,128]{1,0:T(8,128)S(1)} %outer.1), channel_id=1, source_target_pairs={{0,4},{4,0},{8,12},{12,8},{16,20},{20,16},{24,28},{28,24},{32,36},... | collective-permute-start | bytes 135176 | tf_op jit(solution)/shard_map/ppermute | solution.py:329
  30.7 5.3 %collective-permute-start.7 = (f32[88,128]{1,0:T(8,128)S(1)}, f32[88,128]{1,0:T(8,128)S(1)}, u32[]{:S(2)}, u32[]{:S(2)}) collective-permute-start(f32[88,128]{1,0:T(8,128)S(1)} %add.30), channel_id=1, source_target_pairs={{0,96},{4,100},{8,104},{12,108},{16,112},{20,116},{24,120},{28,124... | collective-permute-start | bytes 135176 | tf_op jit(solution)/shard_map/ppermute | solution.py:329
  32.1 4.1 %collective-permute-start.6 = (f32[88,128]{1,0:T(8,128)S(1)}, f32[88,128]{1,0:T(8,128)S(1)}, u32[]{:S(2)}, u32[]{:S(2)}) collective-permute-start(f32[88,128]{1,0:T(8,128)S(1)} %add.30), channel_id=1, source_target_pairs={{0,32},{4,36},{8,40},{12,44},{16,48},{20,52},{24,56},{28,60},{32,0... | collective-permute-start | bytes 135176 | tf_op jit(solution)/shard_map/ppermute | solution.py:329
  32.4 5.6 %collective-permute-start.5 = (f32[88,128]{1,0:T(8,128)S(1)}, f32[88,128]{1,0:T(8,128)S(1)}, u32[]{:S(2)}, u32[]{:S(2)}) collective-permute-start(f32[88,128]{1,0:T(8,128)S(1)} %add.30), channel_id=1, source_target_pairs={{0,64},{4,68},{8,72},{12,76},{16,80},{20,84},{24,88},{28,92},{32,9... | collective-permute-start | bytes 135176 | tf_op jit(solution)/shard_map/ppermute | solution.py:329
  38.0 5.3 %collective-permute-start.10 = (f32[88,128]{1,0:T(8,128)S(1)}, f32[88,128]{1,0:T(8,128)S(1)}, u32[]{:S(2)}, u32[]{:S(2)}) collective-permute-start(f32[88,128]{1,0:T(8,128)S(1)} %add_add_fusion.2), channel_id=1, source_target_pairs={{0,24},{4,28},{8,16},{12,20},{16,8},{20,12},{24,0},{28,4},{32,56},... | collective-permute-start | bytes 135176 | tf_op jit(solution)/shard_map/ppermute | solution.py:329
  39.9 4.0 %collective-permute-start.9 = (f32[88,128]{1,0:T(8,128)S(1)}, f32[88,128]{1,0:T(8,128)S(1)}, u32[]{:S(2)}, u32[]{:S(2)}) collective-permute-start(f32[88,128]{1,0:T(8,128)S(1)} %add_add_fusion.2), channel_id=1, source_target_pairs={{0,8},{4,12},{8,0},{12,4},{16,24},{20,28},{24,16},{28,20},{32,40},... | collective-permute-start | bytes 135176 | tf_op jit(solution)/shard_map/ppermute | solution.py:329
  39.9 5.6 %collective-permute-start.8 = (f32[88,128]{1,0:T(8,128)S(1)}, f32[88,128]{1,0:T(8,128)S(1)}, u32[]{:S(2)}, u32[]{:S(2)}) collective-permute-start(f32[88,128]{1,0:T(8,128)S(1)} %add_add_fusion.2), channel_id=1, source_target_pairs={{0,16},{4,20},{8,24},{12,28},{16,0},{20,4},{24,8},{28,12},{32,48},... | collective-permute-start | bytes 135176 | tf_op jit(solution)/shard_map/ppermute | solution.py:329
  45.5 5.3 %collective-permute-start.13 = (f32[88,128]{1,0:T(8,128)S(1)}, f32[88,128]{1,0:T(8,128)S(1)}, u32[]{:S(2)}, u32[]{:S(2)}) collective-permute-start(f32[88,128]{1,0:T(8,128)S(1)} %add_add_fusion.1), channel_id=1, source_target_pairs={{0,3},{1,2},{2,1},{3,0},{4,7},{5,6},{6,5},{7,4},{8,11},{9,10},{10,... | collective-permute-start | bytes 135176 | tf_op jit(solution)/shard_map/ppermute | solution.py:329
  47.4 4.0 %collective-permute-start.12 = (f32[88,128]{1,0:T(8,128)S(1)}, f32[88,128]{1,0:T(8,128)S(1)}, u32[]{:S(2)}, u32[]{:S(2)}) collective-permute-start(f32[88,128]{1,0:T(8,128)S(1)} %add_add_fusion.1), channel_id=1, source_target_pairs={{0,1},{1,0},{2,3},{3,2},{4,5},{5,4},{6,7},{7,6},{8,9},{9,8},{10,11... | collective-permute-start | bytes 135176 | tf_op jit(solution)/shard_map/ppermute | solution.py:329
  47.5 5.6 %collective-permute-start.11 = (f32[88,128]{1,0:T(8,128)S(1)}, f32[88,128]{1,0:T(8,128)S(1)}, u32[]{:S(2)}, u32[]{:S(2)}) collective-permute-start(f32[88,128]{1,0:T(8,128)S(1)} %add_add_fusion.1), channel_id=1, source_target_pairs={{0,2},{1,3},{2,0},{3,1},{4,6},{5,7},{6,4},{7,5},{8,10},{9,11},{10,... | collective-permute-start | bytes 135176 | tf_op jit(solution)/shard_map/ppermute | solution.py:329
